TPU v7x, 32 devices: a whole 2x2x4 slice. The times are simulated.
32 devices in a mesh: ctx: 16 (over z, y, x), head: 2 (over core).
Axes of the slice: x: 2, y: 2, z: 4, core: 2. Of those that a mesh axis runs over, the one named last changes fastest.
Arguments:
- queries: bfloat16 [8192, 2048], P('ctx', 'head'), may hold values from -16 to 16
- keys: bfloat16 [8192, 2048], P('ctx', 'head'), may hold values from -16 to 16
- values: bfloat16 [8192, 2048], P('ctx', 'head'), may hold values from -12 to 12
- gain: bfloat16 [2048], P('head'), may hold values from 0.5 to 1.5
- cotangent: bfloat16 [8192, 2048], P('ctx', 'head'), may hold values from -6 to 6
Outputs:
- output: bfloat16 [8192, 2048], P('ctx', 'head')
- grad_queries: bfloat16 [8192, 2048], P('ctx', 'head')
- grad_keys: bfloat16 [8192, 2048], P('ctx', 'head')
- grad_values: bfloat16 [8192, 2048], P('ctx', 'head')
All inputs are finite; a program needn't handle non-finite values.
Results may differ from a plain program's by a relative error of at most 0.0065.
Values may be sent and summed in bfloat16 or wider, within the bound.
No kernel may reach another device: no remote copies, remote signals or barrier semaphores. Data moves between devices by JAX's collectives and lax.ppermute only.
A program may use at most 128 MiB of HBM per device.

v0:
```python
import math

import jax
import jax.numpy as jnp
from jax import lax
from jax.sharding import PartitionSpec as P

HEAD_DIM = 128
WINDOW = 256


epsilon = 1e-06


def passed_along(value, axis, steps):
    count = lax.axis_size(axis)
    initial, last = (max(0, -steps), min(count, count - steps))
    return lax.ppermute(value, axis, [(source, source + steps) for source in range(initial, last)])


def prefix_2(part, axis, combine, identity, reverse):
    count = lax.axis_size(axis)
    place = lax.axis_index(axis)
    ahead = count - 1 - place if reverse else place
    gathered = lax.all_gather(part, axis)
    state = jnp.zeros_like(part) + jnp.asarray(identity, part.dtype)

    def one(step, state):
        source = count - 1 - step if reverse else step
        return combine(state, lax.dynamic_index_in_dim(gathered, source, 0, False))

    return lax.fori_loop(0, ahead, one, state)


def add_states(earlier, later):
    return earlier + later


def mixed(form, left, right):
    return jnp.einsum(form, left, right, preferred_element_type=jnp.float32)


def on_device(queries, keys, values, gain, cotangent):
    tok_rows, row_width = queries.shape
    heads_here = row_width // HEAD_DIM
    inv_root = 1.0 / math.sqrt(HEAD_DIM)
    features = row_width * lax.axis_size("head")
    block_index = lax.axis_index("ctx")
    offsets = jnp.arange(tok_rows, dtype=jnp.int32)
    positions = block_index * tok_rows + offsets
    coefs = 1.0 / jnp.sqrt(HEAD_DIM * (positions + 1).astype(jnp.float32))
    causal = (offsets[:, None] >= offsets[None, :])[None]
    ext_cols = jnp.arange(tok_rows + WINDOW, dtype=jnp.int32)
    window_mask = (
        (ext_cols[None, :] > offsets[:, None])
        & (ext_cols[None, :] <= offsets[:, None] + WINDOW)
        & (block_index * tok_rows - WINDOW + ext_cols[None, :] >= 0)
    )[None]
    query_heads = queries.reshape(tok_rows, heads_here, HEAD_DIM)
    key_heads = keys.reshape(tok_rows, heads_here, HEAD_DIM)
    value_heads = values.reshape(tok_rows, heads_here, HEAD_DIM)
    key_prev, value_prev = passed_along(
        (keys[tok_rows - WINDOW :], values[tok_rows - WINDOW :]), "ctx", 1
    )
    key_ext = jnp.concatenate([key_prev, keys], 0).reshape(tok_rows + WINDOW, heads_here, HEAD_DIM)
    value_ext = jnp.concatenate([value_prev, values], 0).reshape(
        tok_rows + WINDOW, heads_here, HEAD_DIM
    )
    local_state = mixed("tde,tdf->def", key_heads, value_heads)
    prefix = prefix_2(local_state, "ctx", add_states, jnp.zeros_like(local_state), False)
    prefix_b = prefix.astype(jnp.bfloat16)
    lin_weights = jnp.where(
        causal, mixed("tde,sde->dts", query_heads, key_heads) * coefs[None, :, None], 0.0
    ).astype(jnp.bfloat16)
    linear = coefs[:, None, None] * mixed("tde,def->tdf", query_heads, prefix_b)
    linear = linear + mixed("dts,sde->tde", lin_weights, value_heads)
    logits = mixed("tde,sde->dts", query_heads, key_ext) * inv_root
    row_peak = jnp.max(jnp.where(window_mask, logits, -1e30), -1)
    row_total = jnp.sum(jnp.where(window_mask, jnp.exp(logits - row_peak[..., None]), 0.0), -1)
    log_total = row_peak + jnp.log(row_total)
    probs = jnp.where(window_mask, jnp.exp(logits - log_total[..., None]), 0.0)
    probs_b = probs.astype(jnp.bfloat16)
    local_window = mixed("dts,sde->tde", probs_b, value_ext)
    hidden = (linear + local_window).reshape(tok_rows, row_width)
    gain_f = gain.astype(jnp.float32)
    scaled = gain_f[None, :] * cotangent.astype(jnp.float32)
    squares, crossed = lax.psum((jnp.sum(hidden * hidden, 1), jnp.sum(hidden * scaled, 1)), "head")
    recip = 1.0 / jnp.sqrt(squares / features + epsilon)
    output = (hidden * recip[:, None] * gain_f[None, :]).astype(jnp.bfloat16)
    grad_full = recip[:, None] * scaled - hidden * (recip**3 * crossed / features)[:, None]
    grad_b = grad_full.astype(jnp.bfloat16)
    grad_u = (grad_full * coefs[:, None]).astype(jnp.bfloat16)
    grad_heads = grad_b.reshape(tok_rows, heads_here, HEAD_DIM)
    gradu_heads = grad_u.reshape(tok_rows, heads_here, HEAD_DIM)
    local_suffix = mixed("tde,tdf->def", query_heads, gradu_heads)
    suffix = prefix_2(local_suffix, "ctx", add_states, jnp.zeros_like(local_suffix), True)
    suffix_b = suffix.astype(jnp.bfloat16)
    back_lin = jnp.where(causal, mixed("tde,sde->dts", gradu_heads, value_heads), 0.0).astype(
        jnp.bfloat16
    )
    d_query = mixed("tdf,def->tde", gradu_heads, prefix_b) + mixed(
        "dts,sde->tde", back_lin, key_heads
    )
    d_key = mixed("dts,tde->sde", back_lin, query_heads) + mixed(
        "sdf,def->sde", value_heads, suffix_b
    )
    d_value = mixed("dts,tde->sde", lin_weights, grad_heads) + mixed(
        "sde,def->sdf", key_heads, suffix_b
    )
    delta = jnp.sum(grad_heads.astype(jnp.float32) * local_window, -1).T
    d_probs = mixed("tde,sde->dts", grad_heads, value_ext)
    d_logits = (probs * (d_probs - delta[..., None]) * inv_root).astype(jnp.bfloat16)
    d_query = d_query + mixed("dts,sde->tde", d_logits, key_ext)
    d_key_ext = mixed("dts,tde->sde", d_logits, query_heads)
    d_value_ext = mixed("dts,tde->sde", probs_b, grad_heads)
    back_key, back_value = (
        passed_along(d_key_ext[:WINDOW].astype(jnp.bfloat16), "ctx", -1).astype(jnp.float32),
        passed_along(d_value_ext[:WINDOW].astype(jnp.bfloat16), "ctx", -1).astype(jnp.float32),
    )
    own_key = d_key_ext[WINDOW:]
    own_value = d_value_ext[WINDOW:]
    pad_rows = jnp.zeros((tok_rows - WINDOW, heads_here, HEAD_DIM), jnp.float32)
    d_key = d_key + own_key + jnp.concatenate([pad_rows, back_key], 0)
    d_value = d_value + own_value + jnp.concatenate([pad_rows, back_value], 0)
    grad_queries = d_query.reshape(tok_rows, row_width).astype(jnp.bfloat16)
    grad_keys = d_key.reshape(tok_rows, row_width).astype(jnp.bfloat16)
    grad_values = d_value.reshape(tok_rows, row_width).astype(jnp.bfloat16)
    return (output, grad_queries, grad_keys, grad_values)


def solution(mesh):
    return jax.shard_map(
        on_device,
        mesh=mesh,
        in_specs=(
            P("ctx", "head"),
            P("ctx", "head"),
            P("ctx", "head"),
            P("head"),
            P("ctx", "head"),
        ),
        out_specs=(P("ctx", "head"), P("ctx", "head"), P("ctx", "head"), P("ctx", "head")),
        check_vma=False,
    )
```

profile of v0, /device:TPU:0, one launch (start us, length us, event | category | flops | bytes accessed | tf_op | source)
XLA Modules:
  0.0 341.6 jit_solution(6602196441139921693)
XLA Ops:
  7.2 2.6 copy.135
  14.7 5.6 %collective-permute-start = (bf16[256,1024]{1,0:T(8,128)(2,1)}, bf16[256,1024]{1,0:T(8,128)(2,1)}, u32[]{:S(2)}, u32[]{:S(2)}) collective-permute-start(bf16[256,1024]{1,0:T(8,128)(2,1)} %slice.20), channel_id=1, source_target_pairs={{0,2},{2,4},{4,6},{6,8},{8,10},{10,12},{12,14},{14,16},{16,18},{18... | collective-permute-start | bytes 1572872 | tf_op jit(solution)/shard_map/ppermute | solution.py:18
  23.5 3.4 collective-permute-start.1
  27.4 3.5 %select_convert_fusion.1 = bf16[8,512,512]{2,1,0:T(8,128)(2,1)} fusion(f32[512]{0:T(512)S(1)} %multiply_rsqrt_fusion, pred[512,512]{1,0:T(8,128)(4,1)S(1)} %iota_compare_fusion.2, bf16[512,1024]{1,0:T(8,128)(2,1)S(1)} %copy-done.12, bf16[512,1024]{1,0:T(8,128)(2,1)S(1)} %copy-done.5), kind=kOutput, calls=%fused_computation.14 | convolution fusion | flops 543162368 | bytes 6555648 | tf_op jit(solution)/shard_map/tde,sde->dts/dot_general | solution.py:40
  30.8 5.0 %collective-permute-done = bf16[256,1024]{1,0:T(8,128)(2,1)} collective-permute-done((bf16[256,1024]{1,0:T(8,128)(2,1)}, bf16[256,1024]{1,0:T(8,128)(2,1)}, u32[]{:S(2)}, u32[]{:S(2)}) %collective-permute-start) | collective-permute-done | bytes 524320 | tf_op jit(solution)/shard_map/ppermute | solution.py:18
  38.6 7.3 %collective-permute-done.1 = bf16[256,1024]{0,1:T(8,128)(2,1)} collective-permute-done((bf16[256,1024]{0,1:T(8,128)(2,1)}, bf16[256,1024]{0,1:T(8,128)(2,1)}, u32[]{:S(2)}, u32[]{:S(2)}) %collective-permute-start.1) | collective-permute-done | bytes 524320 | tf_op jit(solution)/shard_map/ppermute | solution.py:18
  47.4 3.1 fusion
  50.5 2.6 fusion.3
  55.3 5.4 %fusion.53 = f32[8,128,512]{2,1,0:T(8,128)} fusion(bf16[768,8,128]{0,2,1:T(8,128)(2,1)} %bitcast.181, f32[8,768,512]{2,1,0:T(8,128)S(1)} %get-tuple-element.129, f32[8,512]{1,0:T(8,128)S(1)} %log_add_fusion, pred[512,768]{0,1:T(8,128)(4,1)S(1)} %fusion.14), kind=kOutput, calls=%fused_computation.86 | convolution fusion | flops 817889280 | bytes 16662528 | tf_op jit(solution)/shard_map/dts,sde->tde/dot_general | solution.py:40
  60.7 77.7 %all-gather.5.cloned.1.call-done = f32[128,128,128]{2,1,0:T(8,128)} async-done(((f32[8,128,128]{2,1,0:T(8,128)}), f32[128,128,128]{2,1,0:T(8,128)}) %all-gather.5.cloned.1.call-update) | async-done | bytes 8388624 | tf_op jit(solution)/shard_map/all_gather | solution.py:25
  140.4 5.2 %multiply_reduce_fusion.1 = (f32[512]{0:T(512)S(1)}, f32[512,8,128]{0,2,1:T(8,128)}) fusion(f32[8,128,512]{2,1,0:T(8,128)S(1)} %copy-done.17, bf16[8,512,512]{2,1,0:T(8,128)(2,1)} %select_convert_fusion.1, f32[8,128,512]{2,1,0:T(8,128)S(1)} %fusion.20, f32[512]{0:T(512)S(1)} %multiply_rsqrt_fusion, bf16[512,1024]{1,0:T(8,128)(2,1)S(1)} %copy-done.2), kind=kOutput, calls=%fused_computation.34 | convolution fusion | flops 539491840 | bytes 11538432 | tf_op jit(solution)/shard_map/dts,sde->tde/dot_general | solution.py:40
  145.5 3.0 copy.96
  148.5 2.2 multiply_reduce_fusion
  150.7 3.2 all-reduce.2
  154.6 4.2 %fusion.15 = (bf16[512,1024]{1,0:T(8,128)(2,1)}, bf16[512,1024]{1,0:T(8,128)(2,1)}, bf16[512,1024]{1,0:T(8,128)(2,1)}) fusion(f32[512,1024]{1,0:T(8,128)} %copy.96, bf16[512,1024]{1,0:T(8,128)(2,1)} %param.13, f32[512]{0:T(512)S(1)} %get-tuple-element.126, f32[1024]{0:T(1024)S(1)} %convert_element_type.77, f32[512]{0:T(512)S(1)} %get-tuple-element.127, ...), kind=kLoop, calls=%fused_computation.44 | loop fusion | flops 5767168 | bytes 6301696 | tf_op jit(solution)/shard_map/convert_element_type | solution.py:91
  158.9 2.3 copy.131
  161.1 2.8 convolution_bitcast_fusion.2
  166.0 2.5 copy.136
  168.5 2.5 copy.108
  171.0 2.3 copy.103
  173.2 2.3 fusion.12
  180.7 7.4 %multiply_convert_fusion = bf16[8,512,768]{1,2,0:T(8,128)(2,1)S(1)} fusion(f32[8,768,512]{2,1,0:T(8,128)} %copy-done, f32[8,512]{1,0:T(8,128)S(1)} %bitcast.185, f32[8,512]{1,0:T(8,128)S(1)} %copy-done.23, pred[512,768]{0,1:T(8,128)(4,1)S(1)} %fusion.14, bf16[512,8,128]{0,2,1:T(8,128)(2,1)S(1)} %bitcast.168, bf16[768,8,128]{0,2,1:T(8,128)(2,1)S(1)} %bitcast.182), kind=kOutput, calls=%fused_computation.11 | convolution fusion | flops 827326464 | bytes 21921792 | tf_op jit(solution)/shard_map/tde,sde->dts/dot_general | solution.py:40
  188.2 2.5 fusion.11
  191.2 2.3 copy.118
  193.5 5.3 %convolution_bitcast_fusion.1 = f32[768,8,128]{0,2,1:T(8,128)S(1)} fusion(bf16[8,512,768]{1,2,0:T(8,128)(2,1)} %copy-done.1, bf16[512,8,128]{0,2,1:T(8,128)(2,1)} %copy.108), kind=kOutput, calls=%fused_computation.36 | convolution fusion | flops 805306368 | bytes 10485760 | tf_op jit(solution)/shard_map/dts,tde->sde/dot_general | solution.py:40
  201.3 6.2 %convolution_bitcast_fusion = f32[768,8,128]{0,2,1:T(8,128)S(1)} fusion(bf16[512,8,128]{0,2,1:T(8,128)(2,1)S(1)} %bitcast.169, f32[8,768,512]{2,1,0:T(8,128)} %copy-done, f32[8,512]{1,0:T(8,128)S(1)} %copy-done.23, pred[512,768]{0,1:T(8,128)(4,1)S(1)} %fusion.14), kind=kOutput, calls=%fused_computation.35 | convolution fusion | flops 817889280 | bytes 17186816 | tf_op jit(solution)/shard_map/dts,tde->sde/dot_general | solution.py:40
  211.7 2.1 fusion.56
  215.8 90.7 %all-gather.7.cloned.1.call-done = f32[128,128,128]{2,1,0:T(8,128)} async-done(((f32[8,128,128]{2,1,0:T(8,128)}), f32[128,128,128]{2,1,0:T(8,128)}) %all-gather.7.cloned.1.call-update) | async-done | bytes 8388624 | tf_op jit(solution)/shard_map/all_gather | solution.py:25
  306.6 18.0 %while.23 = (s32[]{:T(128)}, f32[8,128,128]{2,1,0:T(8,128)S(1)}, s32[]{:T(128)}, f32[16,8,128,128]{3,2,1,0:T(8,128)}, s32[]{:T(128)}, /*index=5*/s32[]{:T(128)}, s32[]{:T(128)}, s32[]{:T(128)}) while((s32[]{:T(128)}, f32[8,128,128]{2,1,0:T(8,128)S(1)}, s32[]{:T(128)}, f32[16,8,128,128]{3,2,1,0:T(8,128)}, s32[]{:T(128)}, ...), condition=%wide.region_10.11_spmd, body=%wide.region_9.10_spmd.sunk | while | flops 131078 | bytes 1573007 | solution.py:32
  324.6 3.8 %fusion.8 = bf16[512,8,128]{0,2,1:T(8,128)(2,1)} fusion(f32[768,8,128]{0,2,1:T(8,128)} %copy-done.18, f32[8,128,512]{2,1,0:T(8,128)} %fusion.56, bf16[256,8,128]{0,2,1:T(8,128)(2,1)} %collective-permute-done.3, f32[8,128,128]{2,1,0:T(8,128)S(1)} %get-tuple-element.84, bf16[512,1024]{1,0:T(8,128)(2,1)S(1)} %copy-done.13), kind=kOutput, calls=%fused_computation.17 | convolution fusion | flops 136970240 | bytes 7340032 | tf_op jit(solution)/shard_map/sde,def->sdf/dot_general | solution.py:40
  328.4 2.3 copy.120
  330.7 2.7 fusion.10
  (101 shorter events, 52.9 us)
Async XLA Ops:
  7.2 5.3 %copy-start.2 = (bf16[512,1024]{1,0:T(8,128)(2,1)S(1)}, bf16[512,1024]{1,0:T(8,128)(2,1)}, u32[]{:S(2)}) copy-start(bf16[512,1024]{1,0:T(8,128)(2,1)} %param.11) | copy-start | bytes 3145732
  7.2 131.2 %all-gather.5.cloned.1.call-start = ((), (), s32[]{:S(2)}) async-start(), calls=%async_computation | async-start | bytes 8912896 | tf_op jit(solution)/shard_map/all_gather | solution.py:25
  9.8 10.5 %copy-start.12 = (bf16[512,1024]{1,0:T(8,128)(2,1)S(1)}, bf16[512,1024]{1,0:T(8,128)(2,1)}, u32[]{:S(2)}) copy-start(bf16[512,1024]{1,0:T(8,128)(2,1)} %param.10) | copy-start | bytes 3145732
  11.5 1.0 copy-start.14
  12.5 14.4 %copy-start.24 = (bf16[1024]{0:T(1024)(128)(2,1)S(1)}, bf16[1024]{0:T(1024)(128)(2,1)}, u32[]{:S(2)}) copy-start(bf16[1024]{0:T(1024)(128)(2,1)} %param.12) | copy-start | bytes 6148
  13.7 13.6 %copy-start.5 = (bf16[512,1024]{1,0:T(8,128)(2,1)S(1)}, bf16[512,1024]{1,0:T(8,128)(2,1)}, u32[]{:S(2)}) copy-start(bf16[512,1024]{1,0:T(8,128)(2,1)} %param.9) | copy-start | bytes 3145732
  13.8 292.8 %all-gather.7.cloned.1.call-start = ((), (), s32[]{:S(2)}) async-start(), calls=%async_computation.1 | async-start | bytes 8912896 | tf_op jit(solution)/shard_map/all_gather | solution.py:25
  14.7 21.2 %collective-permute-start = (bf16[256,1024]{1,0:T(8,128)(2,1)}, bf16[256,1024]{1,0:T(8,128)(2,1)}, u32[]{:S(2)}, u32[]{:S(2)}) collective-permute-start(bf16[256,1024]{1,0:T(8,128)(2,1)} %slice.20), channel_id=1, source_target_pairs={{0,2},{2,4},{4,6},{6,8},{8,10},{10,12},{12,14},{14,16},{16,18},{18... | collective-permute-start | bytes 1572872 | tf_op jit(solution)/shard_map/ppermute | solution.py:18
  23.5 22.5 %collective-permute-start.1 = (bf16[256,1024]{0,1:T(8,128)(2,1)}, bf16[256,1024]{0,1:T(8,128)(2,1)}, u32[]{:S(2)}, u32[]{:S(2)}) collective-permute-start(bf16[256,1024]{0,1:T(8,128)(2,1)} %slice.26), channel_id=1, source_target_pairs={{0,2},{2,4},{4,6},{6,8},{8,10},{10,12},{12,14},{14,16},{16,18},{18... | collective-permute-start | bytes 1572872 | tf_op jit(solution)/shard_map/ppermute | solution.py:18
  27.0 3.8 %copy-start.20 = (pred[512,512]{1,0:T(8,128)(4,1)}, pred[512,512]{1,0:T(8,128)(4,1)S(1)}, u32[]{:S(2)}) copy-start(pred[512,512]{1,0:T(8,128)(4,1)S(1)} %iota_compare_fusion.2) | copy-start | bytes 786436
  38.6 8.8 %copy-start.6 = (bf16[512,1024]{1,0:T(8,128)(2,1)S(1)}, bf16[512,1024]{1,0:T(8,128)(2,1)}, u32[]{:S(2)}) copy-start(bf16[512,1024]{1,0:T(8,128)(2,1)} %param.9) | copy-start | bytes 3145732
  50.5 4.6 %copy-start = (f32[8,768,512]{2,1,0:T(8,128)}, f32[8,768,512]{2,1,0:T(8,128)S(1)}, u32[]{:S(2)}) copy-start(f32[8,768,512]{2,1,0:T(8,128)S(1)} %get-tuple-element.129) | copy-start | bytes 37748740
  53.1 2.1 copy-start.22
  138.5 1.9 copy-start.17
  173.2 2.3 copy-start.16
  173.2 2.8 copy-start.21
  176.0 1.5 copy-start.15
  177.5 2.1 copy-start.3
  177.5 2.1 copy-start.10
  177.5 3.2 copy-start.19
  177.5 3.2 copy-start.23
  188.2 3.0 copy-start.1
  193.5 7.8 %copy-start.11 = (bf16[512,1024]{0,1:T(8,128)(2,1)S(1)}, bf16[512,1024]{0,1:T(8,128)(2,1)}, u32[]{:S(2)}) copy-start(bf16[512,1024]{0,1:T(8,128)(2,1)} %copy.103) | copy-start | bytes 3145732
  198.8 1.7 copy-start.8
  201.3 10.4 %copy-start.7 = (bf16[8,512,512]{2,1,0:T(8,128)(2,1)S(1)}, bf16[8,512,512]{2,1,0:T(8,128)(2,1)}, u32[]{:S(2)}) copy-start(bf16[8,512,512]{2,1,0:T(8,128)(2,1)} %select_convert_fusion.1) | copy-start | bytes 12582916
  207.5 6.2 %copy-start.18 = (f32[768,8,128]{0,2,1:T(8,128)}, f32[768,8,128]{0,2,1:T(8,128)S(1)}, u32[]{:S(2)}) copy-start(f32[768,8,128]{0,2,1:T(8,128)S(1)} %convolution_bitcast_fusion) | copy-start | bytes 9437188
  208.5 5.3 %copy-start.4 = (bf16[8,512,512]{2,1,0:T(8,128)(2,1)S(1)}, bf16[8,512,512]{2,1,0:T(8,128)(2,1)}, u32[]{:S(2)}) copy-start(bf16[8,512,512]{2,1,0:T(8,128)(2,1)} %copy-done.3) | copy-start | bytes 12582916
  208.5 5.3 %copy-start.9 = (bf16[512,8,128]{0,2,1:T(8,128)(2,1)S(1)}, bf16[512,8,128]{0,2,1:T(8,128)(2,1)}, u32[]{:S(2)}) copy-start(bf16[512,8,128]{0,2,1:T(8,128)(2,1)} %copy.108) | copy-start | bytes 3145732
  208.5 116.1 %collective-permute-start.3 = (bf16[256,8,128]{0,2,1:T(8,128)(2,1)}, bf16[256,8,128]{0,2,1:T(8,128)(2,1)}, u32[]{:S(2)}, u32[]{:S(2)}) collective-permute-start(bf16[256,8,128]{0,2,1:T(8,128)(2,1)} %slice.43), channel_id=1, source_target_pairs={{2,0},{4,2},{6,4},{8,6},{10,8},{12,10},{14,12},{16,14},{18,16},{20... | collective-permute-start | bytes 1572872 | tf_op jit(solution)/shard_map/ppermute | solution.py:18
  210.0 120.7 %collective-permute-start.2 = (bf16[256,8,128]{0,2,1:T(8,128)(2,1)}, bf16[256,8,128]{0,2,1:T(8,128)(2,1)S(1)}, u32[]{:S(2)}, u32[]{:S(2)}) collective-permute-start(bf16[256,8,128]{0,2,1:T(8,128)(2,1)} %slice.44), channel_id=1, source_target_pairs={{2,0},{4,2},{6,4},{8,6},{10,8},{12,10},{14,12},{16,14},{18,16},{20... | collective-permute-start | bytes 1572872 | tf_op jit(solution)/shard_map/ppermute | solution.py:18
  306.6 18.0 %copy-start.13 = (bf16[512,1024]{1,0:T(8,128)(2,1)S(1)}, bf16[512,1024]{1,0:T(8,128)(2,1)}, u32[]{:S(2)}) copy-start(bf16[512,1024]{1,0:T(8,128)(2,1)} %param.10) | copy-start | bytes 3145732
Sparse Core Ops, SparseCore 0:
  13.9 124.4 all-gather.4
  166.1 140.3 all-gather.6
where the time goes:
time: 343 us; the launch traced here: 342 us
  waiting for transfers between devices  181 us (53%)
  matrix products  58.5 us (17%)
  local copies, waits for them, and re-layouts  39.2 us (11%)
  other arithmetic  32.7 us (10%)
  between operations  14.4 us (4%)
  starting transfers between devices  12.3 us (4%)
    all_gather x2, waiting for transfers between devices, prefix_2(): gathered = lax.all_gather(part, axis)  168 us
    dot_general x18, matrix products, mixed(): return jnp.einsum(form, left, right, preferred_element_type=jnp.float32)  58.5 us
    unnamed x56, local copies, waits for them, and re-layouts  19.3 us
    add x15, other arithmetic, add_states(): return earlier + later  17.6 us
    ppermute x4, waiting for transfers between devices, passed_along(): lax.ppermute(value, axis, [(source, source + steps) for source in range(i...  12.4 us
    ppermute x4, starting transfers between devices, passed_along(): lax.ppermute(value, axis, [(source, source + steps) for source in range(i...  12.2 us
  transfers between devices with their start and end apart: 6, of which 4 were waited for; matrix products, arithmetic and copies ran while one was open for 26% of the time, Pallas kernels for 0%

commit v1 on v0

v1 whole, which is shorter than its diff:
```python
import math

import jax
import jax.numpy as jnp
from jax import lax
from jax.experimental import pallas as pl
from jax.experimental.pallas import tpu as pltpu
from jax.sharding import PartitionSpec as P

HEAD_DIM = 128
WINDOW = 256
GROUP = 4
STATS = 8
EPSILON = 1e-06
SCALE = 1.0 / math.sqrt(HEAD_DIM)
SCALE_LOG2 = SCALE * math.log2(math.e)
LN2 = math.log(2.0)
MASKED = -1e30
BF16 = jnp.bfloat16
F32 = jnp.float32
VMEM_LIMIT = 24 * 1024 * 1024


def dot_nn(left, right):
    return lax.dot_general(left, right, (((1,), (0,)), ((), ())), preferred_element_type=F32)


def dot_nt(left, right):
    return lax.dot_general(left, right, (((1,), (1,)), ((), ())), preferred_element_type=F32)


def dot_tn(left, right):
    return lax.dot_general(left, right, (((0,), (0,)), ((), ())), preferred_element_type=F32)


def tile_iotas():
    keys_at = lax.broadcasted_iota(jnp.int32, (WINDOW, WINDOW), 0)
    queries_at = lax.broadcasted_iota(jnp.int32, (WINDOW, WINDOW), 1)
    return keys_at, queries_at


def coef_row(start, count):
    at = start + lax.broadcasted_iota(jnp.int32, (1, count), 1)
    return 1.0 / jnp.sqrt(HEAD_DIM * (at + 1).astype(F32))


def coef_column(start, count):
    at = start + lax.broadcasted_iota(jnp.int32, (count, HEAD_DIM), 0)
    return 1.0 / jnp.sqrt(HEAD_DIM * (at + 1).astype(F32))


def heads_a_step(heads):
    return 2 if heads % 2 == 0 else 1


def call(body, grid, in_specs, out_specs, out_shape, scratch, flops, moved):
    return pl.pallas_call(
        body,
        grid=grid,
        in_specs=in_specs,
        out_specs=out_specs,
        out_shape=out_shape,
        scratch_shapes=scratch,
        compiler_params=pltpu.CompilerParams(
            vmem_limit_bytes=VMEM_LIMIT,
            dimension_semantics=("arbitrary",) * len(grid),
        ),
        cost_estimate=pl.CostEstimate(flops=flops, bytes_accessed=moved, transcendentals=0),
    )


def whole(shape):
    return pl.BlockSpec(shape, lambda *_: (0,) * len(shape))


def put_state(held, head, state):
    rows = held.shape[1]
    step = min(rows, HEAD_DIM)
    for part in range(HEAD_DIM // step):
        at = head * HEAD_DIM + part * step
        held[at // rows, at % rows : at % rows + step, :] = state[part * step : (part + 1) * step]


def get_state(held, head):
    rows = held.shape[1]
    step = min(rows, HEAD_DIM)
    parts = []
    for part in range(HEAD_DIM // step):
        at = head * HEAD_DIM + part * step
        parts.append(held[at // rows, at % rows : at % rows + step, :])
    return parts[0] if len(parts) == 1 else jnp.concatenate(parts, 0)


def spread(held, outs):
    place = lax.rem(lax.axis_index("ctx"), GROUP)
    for other in range(GROUP):
        outs[other][...] = held[lax.bitwise_xor(place, jnp.int32(other))]


def collect(ins, held):
    place = lax.rem(lax.axis_index("ctx"), GROUP)
    for other in range(GROUP):
        held[lax.bitwise_xor(place, jnp.int32(other))] = ins[other][...]


def state_body(k_ref, v_ref, *rest):
    outs, held = rest[:GROUP], rest[GROUP]
    for head in range(k_ref.shape[1] // HEAD_DIM):
        cols = slice(head * HEAD_DIM, (head + 1) * HEAD_DIM)
        put_state(held, head, dot_tn(k_ref[:, cols], v_ref[:, cols]).astype(BF16))
    spread(held, outs)


def local_states(keys, values):
    rows, width = keys.shape
    piece = (width // GROUP, HEAD_DIM)
    return call(
        state_body,
        (1,),
        [whole((rows, width))] * 2,
        [whole(piece)] * GROUP,
        [jax.ShapeDtypeStruct(piece, BF16)] * GROUP,
        [pltpu.VMEM((GROUP,) + piece, BF16)],
        2 * rows * width * HEAD_DIM,
        2 * 2 * rows * width,
    )(keys, values)


def total_body(*refs):
    total = refs[0][...].astype(F32)
    for ref in refs[1:-1]:
        total = total + ref[...].astype(F32)
    refs[-1][...] = total.astype(refs[-1].dtype)


def merge_body(reverse, groups, *refs):
    block = lax.axis_index("ctx")
    group = block // GROUP
    place = lax.rem(block, GROUP)
    others = refs[: groups - 1]
    own = refs[groups - 1 : groups - 1 + GROUP]
    outs = refs[groups - 1 + GROUP :]
    total = jnp.zeros(outs[0].shape, F32)
    for step in range(1, groups):
        wanted = group - step < 0 if reverse else group - step >= 0
        total = total + others[step - 1][...].astype(F32) * wanted.astype(F32)
    for target in range(GROUP):
        to = lax.bitwise_xor(place, jnp.int32(target))
        result = total
        for source in range(GROUP):
            if source == target:
                continue
            of = lax.bitwise_xor(place, jnp.int32(source))
            wanted = of > to if reverse else of < to
            result = result + own[source][...].astype(F32) * wanted.astype(F32)
        outs[target][...] = result.astype(outs[target].dtype)


def swap(value, mask):
    count = lax.axis_size("ctx")
    return lax.ppermute(value, "ctx", [(at, at ^ mask) for at in range(count)])


def turn(value, steps):
    count = lax.axis_size("ctx")
    return lax.ppermute(value, "ctx", [(at, (at + steps) % count) for at in range(count)])


def scan(pieces, reverse):
    groups = lax.axis_size("ctx") // GROUP
    shape = pieces[0].shape
    full = whole(shape)
    size = shape[0] * shape[1]
    own = [pieces[0]] + [swap(pieces[other], other) for other in range(1, GROUP)]
    total = call(
        total_body, (1,), [full] * GROUP, full, jax.ShapeDtypeStruct(shape, BF16), [], GROUP * size, 2 * 5 * size
    )(*own)
    others = [turn(total, GROUP * step) for step in range(1, groups)]
    merged = call(
        lambda *refs: merge_body(reverse, groups, *refs),
        (1,),
        [full] * (groups - 1 + GROUP),
        [full] * GROUP,
        [jax.ShapeDtypeStruct(shape, BF16)] * GROUP,
        [],
        20 * size,
        2 * 11 * size,
    )(*others, *own)
    return [merged[0]] + [swap(merged[other], other) for other in range(1, GROUP)]


def attend(scores, masks, coef, linear):
    shown = [jnp.where(mask, score, MASKED) for score, mask in zip(scores, masks)]
    peak = jnp.max(shown[0], 0, keepdims=True)
    for tile in shown[1:]:
        peak = jnp.maximum(peak, jnp.max(tile, 0, keepdims=True))
    powers = [jnp.exp2((tile - peak) * SCALE_LOG2) for tile in shown]
    norm = jnp.sum(powers[0], 0, keepdims=True)
    for tile in powers[1:]:
        norm = norm + jnp.sum(tile, 0, keepdims=True)
    share = 1.0 / norm
    probs = [tile * share for tile in powers]
    sums = []
    for prob, score, mask, kind in zip(probs, scores, masks, linear):
        if kind == "none":
            sums.append(None)
        elif kind == "all":
            sums.append((prob + score * coef).astype(BF16))
        else:
            sums.append((prob + jnp.where(mask, score * coef, 0.0)).astype(BF16))
    lse = peak * SCALE + jnp.log(norm)
    return [prob.astype(BF16) for prob in probs], sums, lse


def late_body(q_ref, k_ref, v_ref, prob_ref, sum_ref, part_ref):
    rows = k_ref.shape[0]
    start = lax.axis_index("ctx") * rows
    keys_at, queries_at = tile_iotas()
    coef = coef_row(start + WINDOW, WINDOW)
    masks = [keys_at > queries_at, keys_at <= queries_at]
    for head in range(q_ref.shape[1] // HEAD_DIM):
        cols = slice(head * HEAD_DIM, (head + 1) * HEAD_DIM)
        query = q_ref[:, cols]
        scores = [dot_nt(k_ref[at * WINDOW : (at + 1) * WINDOW, cols], query) for at in range(2)]
        probs, sums, _ = attend(scores, masks, coef, ["all", "masked"])
        total = jnp.zeros((HEAD_DIM, WINDOW), F32)
        for at in range(2):
            prob_ref[head, at] = probs[at]
            sum_ref[head, at] = sums[at]
            total = total + dot_tn(v_ref[at * WINDOW : (at + 1) * WINDOW, cols], sums[at])
        part_ref[:, cols] = total.T


def late_rows(queries, keys, values):
    rows, width = keys.shape
    heads = width // HEAD_DIM
    step = heads_a_step(heads)
    tiles = (heads, 2, WINDOW, WINDOW)
    tile_spec = pl.BlockSpec((step,) + tiles[1:], lambda at: (at, 0, 0, 0))
    wide = step * HEAD_DIM
    return call(
        late_body,
        (heads // step,),
        [
            pl.BlockSpec((WINDOW, wide), lambda at: (1, at)),
            pl.BlockSpec((rows, wide), lambda at: (0, at)),
            pl.BlockSpec((rows, wide), lambda at: (0, at)),
        ],
        [tile_spec, tile_spec, pl.BlockSpec((WINDOW, wide), lambda at: (0, at))],
        [
            jax.ShapeDtypeStruct(tiles, BF16),
            jax.ShapeDtypeStruct(tiles, BF16),
            jax.ShapeDtypeStruct((WINDOW, width), F32),
        ],
        [],
        4 * 2 * WINDOW * WINDOW * width * 4,
        12 * WINDOW * width * 2,
    )(queries, keys, values)


def mid_body(steps, q_ref, k_ref, v_ref, kp_ref, vp_ref, part_ref, gain_ref, cot_ref, *rest):
    ins = rest[:GROUP]
    prob_ref, sum_ref, hidden_ref, window_ref, lse_ref, norm_ref, held, squares, crossed = rest[GROUP:]
    rows = q_ref.shape[0]
    block = lax.axis_index("ctx")
    start = block * rows
    at_step = pl.program_id(0)
    step = q_ref.shape[1] // HEAD_DIM

    @pl.when(at_step == 0)
    def _():
        collect(ins, held)
        squares[...] = jnp.zeros_like(squares)
        crossed[...] = jnp.zeros_like(crossed)
        lse_ref[...] = jnp.zeros_like(lse_ref)

    keys_at, queries_at = tile_iotas()
    beyond = jnp.where(block > 0, 0, 2 * WINDOW)
    masks = [keys_at > queries_at + beyond, keys_at <= queries_at]
    coef = coef_row(start, WINDOW)
    columns = coef_column(start, rows)
    for head in range(step):
        cols = slice(head * HEAD_DIM, (head + 1) * HEAD_DIM)
        query = q_ref[:WINDOW, cols]
        scores = [dot_nt(kp_ref[:, cols], query), dot_nt(k_ref[:, cols], query)]
        probs, sums, lse = attend(scores, masks, coef, ["none", "masked"])
        prob_ref[head, 0] = probs[0]
        prob_ref[head, 1] = probs[1]
        sum_ref[head] = sums[1]
        lse_ref[pl.ds(at_step * step + head, 1), :] = lse
        value = v_ref[:, cols]
        before = dot_tn(vp_ref[:, cols], probs[0])
        window = before + dot_tn(value, probs[1])
        window_ref[:, cols] = window.T
        inside = (before + dot_tn(value, sums[1])).T
        state = held_state(held, at_step * step + head)
        carried = columns * dot_nn(q_ref[:, cols], state)
        hidden = jnp.concatenate([inside, part_ref[:, cols]], 0) + carried
        hidden_ref[:, cols] = hidden
        scaled = gain_ref[:, cols].astype(F32) * cot_ref[:, cols].astype(F32)
        squares[...] += hidden * hidden
        crossed[...] += hidden * scaled

    @pl.when(at_step == steps - 1)
    def _():
        norm_ref[...] = jnp.zeros_like(norm_ref)
        norm_ref[0:1, :] = jnp.sum(squares[...].T, 0, keepdims=True)
        norm_ref[1:2, :] = jnp.sum(crossed[...].T, 0, keepdims=True)


def held_state(held, head):
    rows = held.shape[1]
    if rows >= HEAD_DIM:
        each = rows // HEAD_DIM
        at = pl.multiple_of(lax.rem(head, each) * HEAD_DIM, HEAD_DIM)
        return held[head // each, pl.ds(at, HEAD_DIM), :]
    each = HEAD_DIM // rows
    return jnp.concatenate([held[head * each + part] for part in range(each)], 0)


def middle(queries, keys, values, keys_before, values_before, part, gain, cotangent, prefix):
    rows, width = keys.shape
    heads = width // HEAD_DIM
    step = heads_a_step(heads)
    steps = heads // step
    wide = step * HEAD_DIM
    piece = prefix[0].shape
    half = pl.BlockSpec((WINDOW, wide), lambda at: (0, at))
    full = pl.BlockSpec((rows, wide), lambda at: (0, at))
    tiles = (heads, 2, WINDOW, WINDOW)
    return call(
        lambda *refs: mid_body(steps, *refs),
        (steps,),
        [full, half, half, half, half, half, pl.BlockSpec((1, wide), lambda at: (0, at)), full] + [whole(piece)] * GROUP,
        [
            pl.BlockSpec((step,) + tiles[1:], lambda at: (at, 0, 0, 0)),
            pl.BlockSpec((step, WINDOW, WINDOW), lambda at: (at, 0, 0)),
            full,
            half,
            whole((STATS, WINDOW)),
            whole((STATS, rows)),
        ],
        [
            jax.ShapeDtypeStruct(tiles, BF16),
            jax.ShapeDtypeStruct((heads, WINDOW, WINDOW), BF16),
            jax.ShapeDtypeStruct((rows, width), F32),
            jax.ShapeDtypeStruct((WINDOW, width), F32),
            jax.ShapeDtypeStruct((STATS, WINDOW), F32),
            jax.ShapeDtypeStruct((STATS, rows), F32),
        ],
        [
            pltpu.VMEM((GROUP,) + piece, BF16),
            pltpu.VMEM((rows, HEAD_DIM), F32),
            pltpu.VMEM((rows, HEAD_DIM), F32),
        ],
        6 * 2 * WINDOW * WINDOW * width * 4,
        16 * WINDOW * width * 2,
    )(queries, keys, values, keys_before, values_before, part, gain, cotangent, *prefix)


def norm_body(steps, features, norm_ref, hidden_ref, gain_ref, cot_ref, q_ref, window_ref, lse_ref, *rest):
    out_ref, grad_ref, first_ref, stat_ref = rest[:4]
    outs = rest[4 : 4 + GROUP]
    held, recip, pull = rest[4 + GROUP :]
    rows = q_ref.shape[0]
    start = lax.axis_index("ctx") * rows
    at_step = pl.program_id(0)
    step = q_ref.shape[1] // HEAD_DIM

    @pl.when(at_step == 0)
    def _():
        root = 1.0 / jnp.sqrt(norm_ref[0:1, :] / features + EPSILON)
        slope = root * root * root * norm_ref[1:2, :] / features
        recip[...] = jnp.broadcast_to(root, (HEAD_DIM, rows)).T
        pull[...] = jnp.broadcast_to(slope, (HEAD_DIM, rows)).T
        stat_ref[...] = jnp.zeros_like(stat_ref)
        stat_ref[:STATS, :] = lse_ref[...]

    columns = coef_column(start, rows)
    for head in range(step):
        cols = slice(head * HEAD_DIM, (head + 1) * HEAD_DIM)
        hidden = hidden_ref[:, cols]
        gain = gain_ref[:, cols].astype(F32)
        kept = recip[...]
        out_ref[:, cols] = (hidden * kept * gain).astype(BF16)
        full = kept * (gain * cot_ref[:, cols].astype(F32)) - hidden * pull[...]
        grad = full.astype(BF16)
        grad_ref[:, cols] = grad
        first_ref[:, cols] = grad[:WINDOW]
        delta = (grad[:WINDOW].astype(F32) * window_ref[:, cols]).T
        stat_ref[pl.ds(STATS + at_step * step + head, 1), :] = jnp.sum(delta, 0, keepdims=True)
        state = dot_tn(q_ref[:, cols], (full * columns).astype(BF16)).astype(BF16)
        store_state(held, at_step * step + head, state)

    @pl.when(at_step == steps - 1)
    def _():
        spread(held, outs)


def store_state(held, head, state):
    rows = held.shape[1]
    if rows >= HEAD_DIM:
        each = rows // HEAD_DIM
        at = pl.multiple_of(lax.rem(head, each) * HEAD_DIM, HEAD_DIM)
        held[head // each, pl.ds(at, HEAD_DIM), :] = state
    else:
        each = HEAD_DIM // rows
        for part in range(each):
            held[head * each + part] = state[part * rows : (part + 1) * rows]


def normalize(norms, hidden, gain, cotangent, queries, window, lse, features):
    rows, width = queries.shape
    heads = width // HEAD_DIM
    step = heads_a_step(heads)
    steps = heads // step
    wide = step * HEAD_DIM
    piece = (width // GROUP, HEAD_DIM)
    half = pl.BlockSpec((WINDOW, wide), lambda at: (0, at))
    full = pl.BlockSpec((rows, wide), lambda at: (0, at))
    return call(
        lambda *refs: norm_body(steps, features, *refs),
        (steps,),
        [
            whole((STATS, rows)),
            full,
            pl.BlockSpec((1, wide), lambda at: (0, at)),
            full,
            full,
            half,
            whole((STATS, WINDOW)),
        ],
        [full, full, half, whole((2 * STATS, WINDOW))] + [whole(piece)] * GROUP,
        [
            jax.ShapeDtypeStruct((rows, width), BF16),
            jax.ShapeDtypeStruct((rows, width), BF16),
            jax.ShapeDtypeStruct((WINDOW, width), BF16),
            jax.ShapeDtypeStruct((2 * STATS, WINDOW), F32),
        ]
        + [jax.ShapeDtypeStruct(piece, BF16)] * GROUP,
        [
            pltpu.VMEM((GROUP,) + piece, BF16),
            pltpu.VMEM((rows, HEAD_DIM), F32),
            pltpu.VMEM((rows, HEAD_DIM), F32),
        ],
        2 * rows * width * HEAD_DIM,
        14 * rows * width,
    )(norms, hidden, gain, cotangent, queries, window, lse)


def back_body(q_ref, k_ref, v_ref, g_ref, kp_ref, vp_ref, p0_ref, s0_ref, p1_ref, s1_ref, *rest):
    ins = rest[:GROUP]
    dq_ref, dk_ref, dv_ref, held = rest[GROUP:]
    rows = q_ref.shape[0]
    start = lax.axis_index("ctx") * rows
    at_step = pl.program_id(0)
    step = q_ref.shape[1] // HEAD_DIM

    @pl.when(at_step == 0)
    def _():
        collect(ins, held)

    keys_at, queries_at = tile_iotas()
    causal = keys_at <= queries_at
    columns = coef_column(start, rows)
    ratios = coef_row(start, rows) * (1.0 / SCALE)
    for head in range(step):
        cols = slice(head * HEAD_DIM, (head + 1) * HEAD_DIM)
        early, late = slice(0, WINDOW), slice(WINDOW, 2 * WINDOW)
        grads = g_ref[early, cols], g_ref[late, cols]
        queries = q_ref[early, cols], q_ref[late, cols]
        keys = kp_ref[:, cols], k_ref[early, cols], k_ref[late, cols]
        values = vp_ref[:, cols], v_ref[early, cols], v_ref[late, cols]
        probs = (
            (p0_ref[head, 0].astype(F32), p0_ref[head, 1].astype(F32)),
            (p1_ref[head, 0].astype(F32), p1_ref[head, 1].astype(F32)),
        )
        edges = []
        for half in range(2):
            ratio = ratios[:, half * WINDOW : (half + 1) * WINDOW]
            pulls = [dot_nt(values[half + at], grads[half]) for at in range(2)]
            delta = jnp.sum(probs[half][0] * pulls[0] + probs[half][1] * pulls[1], 0, keepdims=True)
            before = probs[half][0] * (pulls[0] - delta)
            if half == 1:
                before = before + pulls[0] * ratio
            here = probs[half][1] * (pulls[1] - delta) + jnp.where(causal, pulls[1] * ratio, 0.0)
            edges.append((before.astype(BF16), here.astype(BF16)))
        state = held_state(held, at_step * step + head)
        inner = [
            (dot_tn(keys[half], edges[half][0]) + dot_tn(keys[half + 1], edges[half][1])).T * SCALE for half in range(2)
        ]
        carried = columns * dot_nt(g_ref[:, cols], state)
        dq_ref[:, cols] = (jnp.concatenate(inner, 0) + carried).astype(BF16)
        dk_ref[early, cols] = SCALE * (dot_nn(edges[0][1], queries[0]) + dot_nn(edges[1][0], queries[1]))
        dk_ref[late, cols] = SCALE * dot_nn(edges[1][1], queries[1])
        dv_ref[early, cols] = dot_nn(s0_ref[head], grads[0]) + dot_nn(s1_ref[head, 0], grads[1])
        dv_ref[late, cols] = dot_nn(s1_ref[head, 1], grads[1])


def backward(queries, keys, values, grads, keys_before, values_before, probs0, sums0, probs1, sums1, prefix):
    rows, width = keys.shape
    heads = width // HEAD_DIM
    step = heads_a_step(heads)
    wide = step * HEAD_DIM
    piece = prefix[0].shape
    half = pl.BlockSpec((WINDOW, wide), lambda at: (0, at))
    full = pl.BlockSpec((rows, wide), lambda at: (0, at))
    pair = pl.BlockSpec((step, 2, WINDOW, WINDOW), lambda at: (at, 0, 0, 0))
    single = pl.BlockSpec((step, WINDOW, WINDOW), lambda at: (at, 0, 0))
    return call(
        back_body,
        (heads // step,),
        [full, full, full, full, half, half, pair, single, pair, pair] + [whole(piece)] * GROUP,
        [full, full, full],
        [
            jax.ShapeDtypeStruct((rows, width), BF16),
            jax.ShapeDtypeStruct((rows, width), F32),
            jax.ShapeDtypeStruct((rows, width), F32),
        ],
        [pltpu.VMEM((GROUP,) + piece, BF16)],
        16 * 2 * WINDOW * WINDOW * width * 2,
        40 * WINDOW * width * 2,
    )(queries, keys, values, grads, keys_before, values_before, probs0, sums0, probs1, sums1, *prefix)


def last_body(last, k_ref, v_ref, dk_in, dv_in, qn_ref, gn_ref, stat_ref, *rest):
    ins = rest[:GROUP]
    dk_ref, dv_ref, held = rest[GROUP:]
    at_step = pl.program_id(0)
    step = k_ref.shape[1] // HEAD_DIM

    @pl.when(at_step == 0)
    def _():
        collect(ins, held)

    keys_at, queries_at = tile_iotas()
    beyond = jnp.where(lax.axis_index("ctx") < last, 0, 2 * WINDOW)
    mask = keys_at > queries_at + beyond
    for head in range(step):
        cols = slice(head * HEAD_DIM, (head + 1) * HEAD_DIM)
        at = at_step * step + head
        early, late = slice(0, WINDOW), slice(WINDOW, 2 * WINDOW)
        query, grad = qn_ref[:, cols], gn_ref[:, cols]
        lse = stat_ref[pl.ds(at, 1), :] * (1.0 / LN2)
        delta = stat_ref[pl.ds(STATS + at, 1), :]
        scores = dot_nt(k_ref[late, cols], query) * SCALE_LOG2
        probs = jnp.where(mask, jnp.exp2(scores - lse), 0.0)
        edges = probs * (dot_nt(v_ref[late, cols], grad) - delta)
        state = held_state(held, at)
        keys = dk_in[:, cols] + dot_nt(v_ref[:, cols], state)
        values = dv_in[:, cols] + dot_nn(k_ref[:, cols], state)
        dk_ref[early, cols] = keys[early].astype(BF16)
        dv_ref[early, cols] = values[early].astype(BF16)
        dk_ref[late, cols] = (keys[late] + SCALE * dot_nn(edges.astype(BF16), query)).astype(BF16)
        dv_ref[late, cols] = (values[late] + dot_nn(probs.astype(BF16), grad)).astype(BF16)


def finish(keys, values, dk_part, dv_part, queries_after, grads_after, stats_after, suffix):
    rows, width = keys.shape
    heads = width // HEAD_DIM
    step = heads_a_step(heads)
    wide = step * HEAD_DIM
    piece = suffix[0].shape
    last = lax.axis_size("ctx") - 1
    half = pl.BlockSpec((WINDOW, wide), lambda at: (0, at))
    full = pl.BlockSpec((rows, wide), lambda at: (0, at))
    return call(
        lambda *refs: last_body(last, *refs),
        (heads // step,),
        [full, full, full, full, half, half, whole((2 * STATS, WINDOW))] + [whole(piece)] * GROUP,
        [full, full],
        [jax.ShapeDtypeStruct((rows, width), BF16)] * 2,
        [pltpu.VMEM((GROUP,) + piece, BF16)],
        8 * 2 * WINDOW * WINDOW * width,
        18 * rows * width,
    )(keys, values, dk_part, dv_part, queries_after, grads_after, stats_after, *suffix)


def on_device(queries, keys, values, gain, cotangent):
    rows, width = queries.shape
    features = width * lax.axis_size("head")
    gain = gain.reshape(1, width)
    keys_before = turn(keys[rows - WINDOW :], 1)
    values_before = turn(values[rows - WINDOW :], 1)
    prefix = scan(local_states(keys, values), False)
    queries_after = turn(queries[:WINDOW], -1)
    probs1, sums1, part = late_rows(queries, keys, values)
    probs0, sums0, hidden, window, lse, norms = middle(
        queries, keys, values, keys_before, values_before, part, gain, cotangent, prefix
    )
    norms = lax.psum(norms, "head")
    output, grads, first, stats, *states = normalize(norms, hidden, gain, cotangent, queries, window, lse, features)
    grads_after = turn(first, -1)
    stats_after = turn(stats, -1)
    suffix = scan(states, True)
    grad_queries, dk_part, dv_part = backward(
        queries, keys, values, grads, keys_before, values_before, probs0, sums0, probs1, sums1, prefix
    )
    grad_keys, grad_values = finish(
        keys, values, dk_part, dv_part, queries_after, grads_after, stats_after, suffix
    )
    return output, grad_queries, grad_keys, grad_values


def solution(mesh):
    wide = P("ctx", "head")
    return jax.shard_map(
        on_device,
        mesh=mesh,
        in_specs=(wide, wide, wide, P("head"), wide),
        out_specs=(wide, wide, wide, wide),
        check_vma=False,
    )
```

time: 343 us -> 129 us (0.38)
  waiting for transfers between devices: 181 us -> 42.6 us
  matrix products: 58.5 us -> 0 us
  other arithmetic: 32.7 us -> 0 us
  Pallas kernels: 0 us -> 30.3 us
  local copies, waits for them, and re-layouts: 39.2 us -> 17.4 us
  starting transfers between devices: 12.3 us -> 33.9 us
  between operations: 14.4 us -> 0.87 us
    all_gather x2 -> x0, waiting for transfers between devices: 168 us -> none  [prefix_2(): gathered = lax.all_gather(part, axis)]
    dot_general x18 -> x0, matrix products: 58.5 us -> none  [mixed(): return jnp.einsum(form, left, right, preferred_element_type=jnp.float32)]
    pallas_call x0 -> x10, Pallas kernels: none -> 30.3 us  [the longest x1 8.64 us: backward(): call(back_body, (heads // step,), [full, full, full, full, half, half, pa...]
    ppermute x4 -> x23, waiting for transfers between devices: 12.4 us -> 42.6 us  [the longest x12 26.2 us: swap(): return lax.ppermute(value, 'ctx', [(at, at ^ mask) for at in range(count)])]
    ppermute x4 -> x23, starting transfers between devices: 12.2 us -> 33.9 us  [the longest x11 22.7 us: turn(): lax.ppermute(value, 'ctx', [(at, (at + steps) % count) for at in range(co...]
    add x17 -> x0, other arithmetic: 17.6 us -> none  [the longest x15 17.6 us: add_states(): return earlier + later]
    reshape x4 -> x1, local copies, waits for them, and re-layouts: 9.42 us -> 0.01 us  [on_device(): gain = gain.reshape(1, width)]
    reduce_sum x3 -> x0, other arithmetic: 7.1 us -> none  [the longest x1 2.58 us: on_device(): jnp.sum(jnp.where(window_mask, jnp.exp(logits - row_peak[..., None]), 0.0...]
  transfers between devices with their start and end apart: 6 -> 23, of which waited for: 4 -> 10; matrix products, arithmetic and copies ran while one was open for 26% -> 1% of each run, Pallas kernels for 0% -> 20%
where the time goes in v1:
time: 129 us; the launch traced here: 128 us
  waiting for transfers between devices  42.6 us (33%)
  starting transfers between devices  33.9 us (26%)
  Pallas kernels  30.3 us (23%)
  local copies, waits for them, and re-layouts  17.4 us (13%)
  blocking collectives  3.35 us (3%)
    ppermute x12, waiting for transfers between devices, swap(): return lax.ppermute(value, 'ctx', [(at, at ^ mask) for at in range(count)])  26.2 us
    ppermute x11, starting transfers between devices, turn(): lax.ppermute(value, 'ctx', [(at, (at + steps) % count) for at in range(co...  22.7 us
    ppermute x11, waiting for transfers between devices, turn(): lax.ppermute(value, 'ctx', [(at, (at + steps) % count) for at in range(co...  16.3 us
    unnamed x44, local copies, waits for them, and re-layouts  14.2 us
    ppermute x12, starting transfers between devices, swap(): return lax.ppermute(value, 'ctx', [(at, at ^ mask) for at in range(count)])  11.1 us
    pallas_call x1, Pallas kernels, backward(): call(back_body, (heads // step,), [full, full, full, full, half, half, pa...  8.64 us
    pallas_call x1, Pallas kernels, middle(): call(lambda *refs: mid_body(steps, *refs), (steps,), [full, half, half, h...  6.54 us
    pallas_call x1, Pallas kernels, late_rows(): call(late_body, (heads // step,), [pl.BlockSpec((WINDOW, wide), lambda at...  5.22 us
  transfers between devices with their start and end apart: 23, of which 10 were waited for; matrix products, arithmetic and copies ran while one was open for 1% of the time, Pallas kernels for 20%

profile of v1, /device:TPU:0, one launch (start us, length us, event | category | flops | bytes accessed | tf_op | source)
XLA Modules:
  0.0 128.4 jit_solution(5642332933555155898)
XLA Ops:
  1.9 3.0 %collective-permute-start = (bf16[256,1024]{1,0:T(8,128)(2,1)S(1)}, bf16[256,1024]{1,0:T(8,128)(2,1)S(1)}, u32[]{:S(2)}, u32[]{:S(2)}) collective-permute-start(bf16[256,1024]{1,0:T(8,128)(2,1)S(1)} %slice.9), channel_id=1, source_target_pairs={{0,2},{2,4},{4,6},{6,8},{8,10},{10,12},{12,14},{14,16},{16,18},{18... | collective-permute-start | bytes 1572872 | tf_op jit(solution)/shard_map/ppermute | solution.py:166
  6.0 1.5 %collective-permute-start.1 = (bf16[256,1024]{1,0:T(8,128)(2,1)S(1)}, bf16[256,1024]{1,0:T(8,128)(2,1)S(1)}, u32[]{:S(2)}, u32[]{:S(2)}) collective-permute-start(bf16[256,1024]{1,0:T(8,128)(2,1)S(1)} %slice.10), channel_id=1, source_target_pairs={{0,2},{2,4},{4,6},{6,8},{8,10},{10,12},{12,14},{14,16},{16,18},{18... | collective-permute-start | bytes 1572872 | tf_op jit(solution)/shard_map/ppermute | solution.py:166
  8.0 1.6 %collective-permute-start.2 = (bf16[256,128]{1,0:T(8,128)(2,1)S(1)}, bf16[256,128]{1,0:T(8,128)(2,1)S(1)}, u32[]{:S(2)}, u32[]{:S(2)}) collective-permute-start(bf16[256,128]{1,0:T(8,128)(2,1)S(1)} %get-tuple-element.40), channel_id=1, source_target_pairs={{0,2},{2,0},{4,6},{6,4},{8,10},{10,8},{12,14},{14,12},{16,18},{18,... | collective-permute-start | bytes 196616 | tf_op jit(solution)/shard_map/ppermute | solution.py:161
  9.6 1.5 %collective-permute-start.3 = (bf16[256,128]{1,0:T(8,128)(2,1)S(1)}, bf16[256,128]{1,0:T(8,128)(2,1)S(1)}, u32[]{:S(2)}, u32[]{:S(2)}) collective-permute-start(bf16[256,128]{1,0:T(8,128)(2,1)S(1)} %get-tuple-element.41), channel_id=1, source_target_pairs={{0,4},{2,6},{4,0},{6,2},{8,12},{10,14},{12,8},{14,10},{16,20},{18,... | collective-permute-start | bytes 196616 | tf_op jit(solution)/shard_map/ppermute | solution.py:161
  11.6 19.8 %collective-permute-done.2.refs_1_.refs_4_ = bf16[256,128]{1,0:T(8,128)(2,1)S(1)} collective-permute-done((bf16[256,128]{1,0:T(8,128)(2,1)S(1)}, bf16[256,128]{1,0:T(8,128)(2,1)S(1)}, u32[]{:S(2)}, u32[]{:S(2)}) %collective-permute-start.2) | collective-permute-done | bytes 65568 | tf_op jit(solution)/shard_map/ppermute | solution.py:161
  31.4 2.2 %collective-permute-done.3.refs_2_.refs_5_ = bf16[256,128]{1,0:T(8,128)(2,1)S(1)} collective-permute-done((bf16[256,128]{1,0:T(8,128)(2,1)S(1)}, bf16[256,128]{1,0:T(8,128)(2,1)S(1)}, u32[]{:S(2)}, u32[]{:S(2)}) %collective-permute-start.3) | collective-permute-done | bytes 65568 | tf_op jit(solution)/shard_map/ppermute | solution.py:161
  35.0 2.3 %collective-permute-start.6 = (bf16[256,128]{1,0:T(8,128)(2,1)S(1)}, bf16[256,128]{1,0:T(8,128)(2,1)S(1)}, u32[]{:S(2)}, u32[]{:S(2)}) collective-permute-start(bf16[256,128]{1,0:T(8,128)(2,1)S(1)} %shard_map.86), channel_id=1, source_target_pairs={{0,16},{2,18},{4,20},{6,22},{8,24},{10,26},{12,28},{14,30},{16,0},... | collective-permute-start | bytes 196616 | tf_op jit(solution)/shard_map/ppermute | solution.py:166
  37.3 1.5 %collective-permute-start.7 = (bf16[256,128]{1,0:T(8,128)(2,1)S(1)}, bf16[256,128]{1,0:T(8,128)(2,1)S(1)}, u32[]{:S(2)}, u32[]{:S(2)}) collective-permute-start(bf16[256,128]{1,0:T(8,128)(2,1)S(1)} %shard_map.86), channel_id=1, source_target_pairs={{0,24},{2,26},{4,28},{6,30},{8,0},{10,2},{12,4},{14,6},{16,8},{18,... | collective-permute-start | bytes 196616 | tf_op jit(solution)/shard_map/ppermute | solution.py:166
  38.8 3.0 %collective-permute-done.5.refs_0_ = bf16[256,128]{1,0:T(8,128)(2,1)S(1)} collective-permute-done((bf16[256,128]{1,0:T(8,128)(2,1)S(1)}, bf16[256,128]{1,0:T(8,128)(2,1)S(1)}, u32[]{:S(2)}, u32[]{:S(2)}) %collective-permute-start.5) | collective-permute-done | bytes 65568 | tf_op jit(solution)/shard_map/ppermute | solution.py:166
  41.7 1.7 %collective-permute-done.6.refs_1_ = bf16[256,128]{1,0:T(8,128)(2,1)S(1)} collective-permute-done((bf16[256,128]{1,0:T(8,128)(2,1)S(1)}, bf16[256,128]{1,0:T(8,128)(2,1)S(1)}, u32[]{:S(2)}, u32[]{:S(2)}) %collective-permute-start.6) | collective-permute-done | bytes 65568 | tf_op jit(solution)/shard_map/ppermute | solution.py:166
  44.6 4.4 %collective-permute-start.11 = (bf16[256,1024]{1,0:T(8,128)(2,1)}, bf16[256,1024]{1,0:T(8,128)(2,1)}, u32[]{:S(2)}, u32[]{:S(2)}) collective-permute-start(bf16[256,1024]{1,0:T(8,128)(2,1)} %slice.11), channel_id=1, source_target_pairs={{0,30},{2,0},{4,2},{6,4},{8,6},{10,8},{12,10},{14,12},{16,14},{18,... | collective-permute-start | bytes 1572872 | tf_op jit(solution)/shard_map/ppermute | solution.py:166
  49.7 5.2 %shard_map.84 = (bf16[8,2,256,256]{3,2,1,0:T(8,128)(2,1)S(1)}, bf16[8,2,256,256]{3,2,1,0:T(8,128)(2,1)S(1)}, f32[256,1024]{1,0:T(8,128)S(1)}) custom-call(bf16[512,1024]{1,0:T(8,128)(2,1)S(1)} %copy-done.2, bf16[512,1024]{1,0:T(8,128)(2,1)S(1)} %copy-done, bf16[512,1024]{1,0:T(8,128)(2,1)S(1)} %copy-done.1), custom_call_target="tpu_custom_call" | custom-call | flops 2147483648 | bytes 6291456 | tf_op jit(solution)/shard_map/pallas_call | solution.py:241
  54.9 1.3 %copy-done.13 = bf16[8,2,256,256]{3,2,1,0:T(8,128)(2,1)} copy-done((bf16[8,2,256,256]{3,2,1,0:T(8,128)(2,1)}, bf16[8,2,256,256]{3,2,1,0:T(8,128)(2,1)S(1)}, u32[]{:S(2)}) %copy-start.13) | copy-done | bytes 2097176
  56.2 1.3 %copy-done.15 = bf16[8,2,256,256]{3,2,1,0:T(8,128)(2,1)} copy-done((bf16[8,2,256,256]{3,2,1,0:T(8,128)(2,1)}, bf16[8,2,256,256]{3,2,1,0:T(8,128)(2,1)S(1)}, u32[]{:S(2)}) %copy-start.15) | copy-done | bytes 2097176
  57.6 2.0 %collective-permute-done.8.refs_9_.rest_1_ = bf16[256,128]{1,0:T(8,128)(2,1)S(1)} collective-permute-done((bf16[256,128]{1,0:T(8,128)(2,1)S(1)}, bf16[256,128]{1,0:T(8,128)(2,1)S(1)}, u32[]{:S(2)}, u32[]{:S(2)}) %collective-permute-start.8) | collective-permute-done | bytes 65568 | tf_op jit(solution)/shard_map/ppermute | solution.py:161
  59.6 6.5 %shard_map.88 = (bf16[8,2,256,256]{3,2,1,0:T(8,128)(2,1)S(1)}, bf16[8,256,256]{2,1,0:T(8,128)(2,1)S(1)}, f32[512,1024]{1,0:T(8,128)S(1)}, f32[256,1024]{1,0:T(8,...) custom-call(bf16[512,1024]{1,0:T(8,128)(2,1)S(1)} %copy-done.2, bf16[512,1024]{1,0:T(8,128)(2,1)S(1)} %copy-done, ...), custom_call_target="tpu_custom_call" | custom-call | flops 3221225472 | bytes 8388608 | tf_op jit(solution)/shard_map/pallas_call | solution.py:331
  66.2 1.4 %copy-done.3 = f32[512,1024]{1,0:T(8,128)} copy-done((f32[512,1024]{1,0:T(8,128)}, f32[512,1024]{1,0:T(8,128)S(1)}, u32[]{:S(2)}) %copy-start.3) | copy-done | bytes 2097176
  68.5 1.4 %copy-done.17 = bf16[8,2,256,256]{3,2,1,0:T(8,128)(2,1)} copy-done((bf16[8,2,256,256]{3,2,1,0:T(8,128)(2,1)}, bf16[8,2,256,256]{3,2,1,0:T(8,128)(2,1)S(1)}, u32[]{:S(2)}) %copy-start.17) | copy-done | bytes 2097176
  70.9 3.3 %psum.7.refs_0_ = f32[8,512]{1,0:T(8,128)S(1)} all-reduce(f32[8,512]{1,0:T(8,128)S(1)} %get-tuple-element.47), channel_id=1, replica_groups=mesh['ctx'=16,'head'=2] {'head'}, use_global_device_ids=true, to_apply=%region_0.0 | all-reduce | flops 4096 | bytes 32768 | tf_op jit(solution)/shard_map/psum | solution.py:591
  74.2 1.6 %copy-done.4 = f32[512,1024]{1,0:T(8,128)S(1)} copy-done((f32[512,1024]{1,0:T(8,128)S(1)}, f32[512,1024]{1,0:T(8,128)}, u32[]{:S(2)}) %copy-start.4) | copy-done | bytes 2097176
  78.3 3.8 %shard_map.89 = (bf16[512,1024]{1,0:T(8,128)(2,1)}, bf16[512,1024]{1,0:T(8,128)(2,1)S(1)}, bf16[256,1024]{1,0:T(8,128)(2,1)S(1)}, f32[16,256]{1,0:T(8,128)S(1)},...) custom-call(f32[8,512]{1,0:T(8,128)S(1)} %psum.7.refs_0_, ...), custom_call_target="tpu_custom_call" | custom-call | flops 134217728 | bytes 7340032 | tf_op jit(solution)/shard_map/pallas_call | solution.py:421
  82.1 2.5 %collective-permute-start.14 = (bf16[256,128]{1,0:T(8,128)(2,1)S(1)}, bf16[256,128]{1,0:T(8,128)(2,1)S(1)}, u32[]{:S(2)}, u32[]{:S(2)}) collective-permute-start(bf16[256,128]{1,0:T(8,128)(2,1)S(1)} %get-tuple-element.63), channel_id=1, source_target_pairs={{0,2},{2,0},{4,6},{6,4},{8,10},{10,8},{12,14},{14,12},{16,18},{18,... | collective-permute-start | bytes 196616 | tf_op jit(solution)/shard_map/ppermute | solution.py:161
  84.6 1.5 %collective-permute-start.15 = (bf16[256,128]{1,0:T(8,128)(2,1)S(1)}, bf16[256,128]{1,0:T(8,128)(2,1)S(1)}, u32[]{:S(2)}, u32[]{:S(2)}) collective-permute-start(bf16[256,128]{1,0:T(8,128)(2,1)S(1)} %get-tuple-element.64), channel_id=1, source_target_pairs={{0,4},{2,6},{4,0},{6,2},{8,12},{10,14},{12,8},{14,10},{16,20},{18,... | collective-permute-start | bytes 196616 | tf_op jit(solution)/shard_map/ppermute | solution.py:161
  86.1 5.5 %collective-permute-start.12 = (bf16[256,1024]{1,0:T(8,128)(2,1)S(1)}, bf16[256,1024]{1,0:T(8,128)(2,1)S(1)}, u32[]{:S(2)}, u32[]{:S(2)}) collective-permute-start(bf16[256,1024]{1,0:T(8,128)(2,1)S(1)} %get-tuple-element.60), channel_id=1, source_target_pairs={{0,30},{2,0},{4,2},{6,4},{8,6},{10,8},{12,10},{14,12},{16,14},{18,... | collective-permute-start | bytes 1572872 | tf_op jit(solution)/shard_map/ppermute | solution.py:166
  92.0 1.8 %collective-permute-start.17 = (bf16[256,128]{1,0:T(8,128)(2,1)S(1)}, bf16[256,128]{1,0:T(8,128)(2,1)S(1)}, u32[]{:S(2)}, u32[]{:S(2)}) collective-permute-start(bf16[256,128]{1,0:T(8,128)(2,1)S(1)} %shard_map.91), channel_id=1, source_target_pairs={{0,8},{2,10},{4,12},{6,14},{8,16},{10,18},{12,20},{14,22},{16,24},... | collective-permute-start | bytes 196616 | tf_op jit(solution)/shard_map/ppermute | solution.py:166
  93.8 2.0 %collective-permute-start.18 = (bf16[256,128]{1,0:T(8,128)(2,1)S(1)}, bf16[256,128]{1,0:T(8,128)(2,1)S(1)}, u32[]{:S(2)}, u32[]{:S(2)}) collective-permute-start(bf16[256,128]{1,0:T(8,128)(2,1)S(1)} %shard_map.91), channel_id=1, source_target_pairs={{0,16},{2,18},{4,20},{6,22},{8,24},{10,26},{12,28},{14,30},{16,0},... | collective-permute-start | bytes 196616 | tf_op jit(solution)/shard_map/ppermute | solution.py:166
  96.4 9.1 %collective-permute-done.17.refs_0_ = bf16[256,128]{1,0:T(8,128)(2,1)S(1)} collective-permute-done((bf16[256,128]{1,0:T(8,128)(2,1)S(1)}, bf16[256,128]{1,0:T(8,128)(2,1)S(1)}, u32[]{:S(2)}, u32[]{:S(2)}) %collective-permute-start.17) | collective-permute-done | bytes 65568 | tf_op jit(solution)/shard_map/ppermute | solution.py:166
  105.5 2.5 %collective-permute-done.18.refs_1_ = bf16[256,128]{1,0:T(8,128)(2,1)S(1)} collective-permute-done((bf16[256,128]{1,0:T(8,128)(2,1)S(1)}, bf16[256,128]{1,0:T(8,128)(2,1)S(1)}, u32[]{:S(2)}, u32[]{:S(2)}) %collective-permute-start.18) | collective-permute-done | bytes 65568 | tf_op jit(solution)/shard_map/ppermute | solution.py:166
  108.4 3.4 %collective-permute-start.22 = (bf16[256,128]{1,0:T(8,128)(2,1)S(1)}, bf16[256,128]{1,0:T(8,128)(2,1)S(1)}, u32[]{:S(2)}, u32[]{:S(2)}) collective-permute-start(bf16[256,128]{1,0:T(8,128)(2,1)S(1)} %get-tuple-element.69), channel_id=1, source_target_pairs={{0,6},{2,4},{4,2},{6,0},{8,14},{10,12},{12,10},{14,8},{16,22},{18,... | collective-permute-start | bytes 196616 | tf_op jit(solution)/shard_map/ppermute | solution.py:161
  111.8 1.6 %copy-done.18 = bf16[8,2,256,256]{3,2,1,0:T(8,128)(2,1)S(1)} copy-done((bf16[8,2,256,256]{3,2,1,0:T(8,128)(2,1)S(1)}, bf16[8,2,256,256]{3,2,1,0:T(8,128)(2,1)}, u32[]{:S(2)}) %copy-start.18) | copy-done | bytes 2097176
  114.6 8.6 %shard_map.90 = (bf16[512,1024]{1,0:T(8,128)(2,1)}, f32[512,1024]{1,0:T(8,128)S(1)}, f32[512,1024]{1,0:T(8,128)S(1)}) custom-call(bf16[512,1024]{1,0:T(8,128)(2,1)S(1)} %copy-done.2, bf16[512,1024]{1,0:T(8,128)(2,1)S(1)} %copy-done, bf16[512,1024]{1,0:T(8,128)(2,1)S(1)} %copy-done.1, bf16[512,1024]{1,0:T(8,128)(2,1)S(1)} %get-tuple-element.52.g_ref, ...), custom_call_target="tpu_custom_call" | custom-call | flops 4294967296 | bytes 20971520 | tf_op jit(solution)/shard_map/pallas_call | solution.py:510
  123.3 5.0 %shard_map.93 = (bf16[512,1024]{1,0:T(8,128)(2,1)}, bf16[512,1024]{1,0:T(8,128)(2,1)}) custom-call(bf16[512,1024]{1,0:T(8,128)(2,1)S(1)} %copy-done, bf16[512,1024]{1,0:T(8,128)(2,1)S(1)} %copy-done.1, f32[512,1024]{1,0:T(8,128)S(1)} %get-tuple-element.58.refs_2_, f32[512,1024]{1,0:T(8,128)S(1)} %get-tuple-element.59.refs_3_, ...), custom_call_target="tpu_custom_call" | custom-call | flops 1073741824 | bytes 9437184 | tf_op jit(solution)/shard_map/pallas_call | solution.py:567
  (73 shorter events, 13.4 us)
Async XLA Ops:
  0.6 6.9 %copy-start = (bf16[512,1024]{1,0:T(8,128)(2,1)S(1)}, bf16[512,1024]{1,0:T(8,128)(2,1)}, u32[]{:S(2)}) copy-start(bf16[512,1024]{1,0:T(8,128)(2,1)} %refs_0_.3) | copy-start | bytes 3145732
  0.6 6.9 %copy-start.1 = (bf16[512,1024]{1,0:T(8,128)(2,1)S(1)}, bf16[512,1024]{1,0:T(8,128)(2,1)}, u32[]{:S(2)}) copy-start(bf16[512,1024]{1,0:T(8,128)(2,1)} %refs_1_.3) | copy-start | bytes 3145732
  1.9 41.9 %copy-start.2 = (bf16[512,1024]{1,0:T(8,128)(2,1)S(1)}, bf16[512,1024]{1,0:T(8,128)(2,1)}, u32[]{:S(2)}) copy-start(bf16[512,1024]{1,0:T(8,128)(2,1)} %q_ref.3) | copy-start | bytes 3145732
  1.9 57.7 %collective-permute-start = (bf16[256,1024]{1,0:T(8,128)(2,1)S(1)}, bf16[256,1024]{1,0:T(8,128)(2,1)S(1)}, u32[]{:S(2)}, u32[]{:S(2)}) collective-permute-start(bf16[256,1024]{1,0:T(8,128)(2,1)S(1)} %slice.9), channel_id=1, source_target_pairs={{0,2},{2,4},{4,6},{6,8},{8,10},{10,12},{12,14},{14,16},{16,18},{18... | collective-permute-start | bytes 1572872 | tf_op jit(solution)/shard_map/ppermute | solution.py:166
  6.0 53.6 %collective-permute-start.1 = (bf16[256,1024]{1,0:T(8,128)(2,1)S(1)}, bf16[256,1024]{1,0:T(8,128)(2,1)S(1)}, u32[]{:S(2)}, u32[]{:S(2)}) collective-permute-start(bf16[256,1024]{1,0:T(8,128)(2,1)S(1)} %slice.10), channel_id=1, source_target_pairs={{0,2},{2,4},{4,6},{6,8},{8,10},{10,12},{12,14},{14,16},{16,18},{18... | collective-permute-start | bytes 1572872 | tf_op jit(solution)/shard_map/ppermute | solution.py:166
  8.0 23.4 %collective-permute-start.2 = (bf16[256,128]{1,0:T(8,128)(2,1)S(1)}, bf16[256,128]{1,0:T(8,128)(2,1)S(1)}, u32[]{:S(2)}, u32[]{:S(2)}) collective-permute-start(bf16[256,128]{1,0:T(8,128)(2,1)S(1)} %get-tuple-element.40), channel_id=1, source_target_pairs={{0,2},{2,0},{4,6},{6,4},{8,10},{10,8},{12,14},{14,12},{16,18},{18,... | collective-permute-start | bytes 196616 | tf_op jit(solution)/shard_map/ppermute | solution.py:161
  9.6 24.0 %collective-permute-start.3 = (bf16[256,128]{1,0:T(8,128)(2,1)S(1)}, bf16[256,128]{1,0:T(8,128)(2,1)S(1)}, u32[]{:S(2)}, u32[]{:S(2)}) collective-permute-start(bf16[256,128]{1,0:T(8,128)(2,1)S(1)} %get-tuple-element.41), channel_id=1, source_target_pairs={{0,4},{2,6},{4,0},{6,2},{8,12},{10,14},{12,8},{14,10},{16,20},{18,... | collective-permute-start | bytes 196616 | tf_op jit(solution)/shard_map/ppermute | solution.py:161
  11.2 23.7 %collective-permute-start.4 = (bf16[256,128]{1,0:T(8,128)(2,1)S(1)}, bf16[256,128]{1,0:T(8,128)(2,1)S(1)}, u32[]{:S(2)}, u32[]{:S(2)}) collective-permute-start(bf16[256,128]{1,0:T(8,128)(2,1)S(1)} %get-tuple-element.42), channel_id=1, source_target_pairs={{0,6},{2,4},{4,2},{6,0},{8,14},{10,12},{12,10},{14,8},{16,22},{18,... | collective-permute-start | bytes 196616 | tf_op jit(solution)/shard_map/ppermute | solution.py:161
  34.9 6.8 %collective-permute-start.5 = (bf16[256,128]{1,0:T(8,128)(2,1)S(1)}, bf16[256,128]{1,0:T(8,128)(2,1)S(1)}, u32[]{:S(2)}, u32[]{:S(2)}) collective-permute-start(bf16[256,128]{1,0:T(8,128)(2,1)S(1)} %shard_map.86), channel_id=1, source_target_pairs={{0,8},{2,10},{4,12},{6,14},{8,16},{10,18},{12,20},{14,22},{16,24},... | collective-permute-start | bytes 196616 | tf_op jit(solution)/shard_map/ppermute | solution.py:166
  35.0 8.5 %collective-permute-start.6 = (bf16[256,128]{1,0:T(8,128)(2,1)S(1)}, bf16[256,128]{1,0:T(8,128)(2,1)S(1)}, u32[]{:S(2)}, u32[]{:S(2)}) collective-permute-start(bf16[256,128]{1,0:T(8,128)(2,1)S(1)} %shard_map.86), channel_id=1, source_target_pairs={{0,16},{2,18},{4,20},{6,22},{8,24},{10,26},{12,28},{14,30},{16,0},... | collective-permute-start | bytes 196616 | tf_op jit(solution)/shard_map/ppermute | solution.py:166
  37.3 6.2 %collective-permute-start.7 = (bf16[256,128]{1,0:T(8,128)(2,1)S(1)}, bf16[256,128]{1,0:T(8,128)(2,1)S(1)}, u32[]{:S(2)}, u32[]{:S(2)}) collective-permute-start(bf16[256,128]{1,0:T(8,128)(2,1)S(1)} %shard_map.86), channel_id=1, source_target_pairs={{0,24},{2,26},{4,28},{6,30},{8,0},{10,2},{12,4},{14,6},{16,8},{18,... | collective-permute-start | bytes 196616 | tf_op jit(solution)/shard_map/ppermute | solution.py:166
  43.7 6.0 %collective-permute-start.10 = (bf16[256,128]{1,0:T(8,128)(2,1)S(1)}, bf16[256,128]{1,0:T(8,128)(2,1)S(1)}, u32[]{:S(2)}, u32[]{:S(2)}) collective-permute-start(bf16[256,128]{1,0:T(8,128)(2,1)S(1)} %get-tuple-element.46), channel_id=1, source_target_pairs={{0,6},{2,4},{4,2},{6,0},{8,14},{10,12},{12,10},{14,8},{16,22},{18,... | collective-permute-start | bytes 196616 | tf_op jit(solution)/shard_map/ppermute | solution.py:161
  44.6 63.8 %collective-permute-start.11 = (bf16[256,1024]{1,0:T(8,128)(2,1)}, bf16[256,1024]{1,0:T(8,128)(2,1)}, u32[]{:S(2)}, u32[]{:S(2)}) collective-permute-start(bf16[256,1024]{1,0:T(8,128)(2,1)} %slice.11), channel_id=1, source_target_pairs={{0,30},{2,0},{4,2},{6,4},{8,6},{10,8},{12,10},{14,12},{16,14},{18,... | collective-permute-start | bytes 1572872 | tf_op jit(solution)/shard_map/ppermute | solution.py:166
  49.0 10.5 %collective-permute-start.8 = (bf16[256,128]{1,0:T(8,128)(2,1)S(1)}, bf16[256,128]{1,0:T(8,128)(2,1)S(1)}, u32[]{:S(2)}, u32[]{:S(2)}) collective-permute-start(bf16[256,128]{1,0:T(8,128)(2,1)S(1)} %get-tuple-element.44), channel_id=1, source_target_pairs={{0,2},{2,0},{4,6},{6,4},{8,10},{10,8},{12,14},{14,12},{16,18},{18,... | collective-permute-start | bytes 196616 | tf_op jit(solution)/shard_map/ppermute | solution.py:161
  49.7 7.9 %copy-start.21 = (bf16[1024]{0:T(1024)(128)(2,1)S(1)}, bf16[1024]{0:T(1024)(128)(2,1)}, u32[]{:S(2)}) copy-start(bf16[1024]{0:T(1024)(128)(2,1)} %param.8) | copy-start | bytes 6148
  49.7 9.9 %copy-start.5 = (bf16[512,1024]{1,0:T(8,128)(2,1)S(1)}, bf16[512,1024]{1,0:T(8,128)(2,1)}, u32[]{:S(2)}) copy-start(bf16[512,1024]{1,0:T(8,128)(2,1)} %refs_3_.1) | copy-start | bytes 3145732
  49.7 9.9 %collective-permute-start.9 = (bf16[256,128]{1,0:T(8,128)(2,1)S(1)}, bf16[256,128]{1,0:T(8,128)(2,1)S(1)}, u32[]{:S(2)}, u32[]{:S(2)}) collective-permute-start(bf16[256,128]{1,0:T(8,128)(2,1)S(1)} %get-tuple-element.45), channel_id=1, source_target_pairs={{0,4},{2,6},{4,0},{6,2},{8,12},{10,14},{12,8},{14,10},{16,20},{18,... | collective-permute-start | bytes 196616 | tf_op jit(solution)/shard_map/ppermute | solution.py:161
  78.3 33.5 %copy-start.10 = (bf16[256,1024]{1,0:T(8,128)(2,1)S(1)}, bf16[256,1024]{1,0:T(8,128)(2,1)}, u32[]{:S(2)}) copy-start(bf16[256,1024]{1,0:T(8,128)(2,1)} %copy-done.9) | copy-start | bytes 1572868
  78.3 33.5 %copy-start.12 = (bf16[256,1024]{1,0:T(8,128)(2,1)S(1)}, bf16[256,1024]{1,0:T(8,128)(2,1)}, u32[]{:S(2)}) copy-start(bf16[256,1024]{1,0:T(8,128)(2,1)} %copy-done.11) | copy-start | bytes 1572868
  78.3 33.5 %copy-start.14 = (bf16[8,2,256,256]{3,2,1,0:T(8,128)(2,1)S(1)}, bf16[8,2,256,256]{3,2,1,0:T(8,128)(2,1)}, u32[]{:S(2)}) copy-start(bf16[8,2,256,256]{3,2,1,0:T(8,128)(2,1)} %copy-done.13) | copy-start | bytes 6291460
  78.3 33.5 %copy-start.16 = (bf16[8,2,256,256]{3,2,1,0:T(8,128)(2,1)S(1)}, bf16[8,2,256,256]{3,2,1,0:T(8,128)(2,1)}, u32[]{:S(2)}) copy-start(bf16[8,2,256,256]{3,2,1,0:T(8,128)(2,1)} %copy-done.15) | copy-start | bytes 6291460
  82.1 9.5 %collective-permute-start.14 = (bf16[256,128]{1,0:T(8,128)(2,1)S(1)}, bf16[256,128]{1,0:T(8,128)(2,1)S(1)}, u32[]{:S(2)}, u32[]{:S(2)}) collective-permute-start(bf16[256,128]{1,0:T(8,128)(2,1)S(1)} %get-tuple-element.63), channel_id=1, source_target_pairs={{0,2},{2,0},{4,6},{6,4},{8,10},{10,8},{12,14},{14,12},{16,18},{18,... | collective-permute-start | bytes 196616 | tf_op jit(solution)/shard_map/ppermute | solution.py:161
  84.6 7.0 %collective-permute-start.15 = (bf16[256,128]{1,0:T(8,128)(2,1)S(1)}, bf16[256,128]{1,0:T(8,128)(2,1)S(1)}, u32[]{:S(2)}, u32[]{:S(2)}) collective-permute-start(bf16[256,128]{1,0:T(8,128)(2,1)S(1)} %get-tuple-element.64), channel_id=1, source_target_pairs={{0,4},{2,6},{4,0},{6,2},{8,12},{10,14},{12,8},{14,10},{16,20},{18,... | collective-permute-start | bytes 196616 | tf_op jit(solution)/shard_map/ppermute | solution.py:161
  86.1 5.9 %collective-permute-start.16 = (bf16[256,128]{1,0:T(8,128)(2,1)S(1)}, bf16[256,128]{1,0:T(8,128)(2,1)S(1)}, u32[]{:S(2)}, u32[]{:S(2)}) collective-permute-start(bf16[256,128]{1,0:T(8,128)(2,1)S(1)} %get-tuple-element.65), channel_id=1, source_target_pairs={{0,6},{2,4},{4,2},{6,0},{8,14},{10,12},{12,10},{14,8},{16,22},{18,... | collective-permute-start | bytes 196616 | tf_op jit(solution)/shard_map/ppermute | solution.py:161
  86.1 37.2 %collective-permute-start.12 = (bf16[256,1024]{1,0:T(8,128)(2,1)S(1)}, bf16[256,1024]{1,0:T(8,128)(2,1)S(1)}, u32[]{:S(2)}, u32[]{:S(2)}) collective-permute-start(bf16[256,1024]{1,0:T(8,128)(2,1)S(1)} %get-tuple-element.60), channel_id=1, source_target_pairs={{0,30},{2,0},{4,2},{6,4},{8,6},{10,8},{12,10},{14,12},{16,14},{18,... | collective-permute-start | bytes 1572872 | tf_op jit(solution)/shard_map/ppermute | solution.py:166
  92.0 13.5 %collective-permute-start.17 = (bf16[256,128]{1,0:T(8,128)(2,1)S(1)}, bf16[256,128]{1,0:T(8,128)(2,1)S(1)}, u32[]{:S(2)}, u32[]{:S(2)}) collective-permute-start(bf16[256,128]{1,0:T(8,128)(2,1)S(1)} %shard_map.91), channel_id=1, source_target_pairs={{0,8},{2,10},{4,12},{6,14},{8,16},{10,18},{12,20},{14,22},{16,24},... | collective-permute-start | bytes 196616 | tf_op jit(solution)/shard_map/ppermute | solution.py:166
  93.8 14.2 %collective-permute-start.18 = (bf16[256,128]{1,0:T(8,128)(2,1)S(1)}, bf16[256,128]{1,0:T(8,128)(2,1)S(1)}, u32[]{:S(2)}, u32[]{:S(2)}) collective-permute-start(bf16[256,128]{1,0:T(8,128)(2,1)S(1)} %shard_map.91), channel_id=1, source_target_pairs={{0,16},{2,18},{4,20},{6,22},{8,24},{10,26},{12,28},{14,30},{16,0},... | collective-permute-start | bytes 196616 | tf_op jit(solution)/shard_map/ppermute | solution.py:166
  95.8 12.2 %collective-permute-start.19 = (bf16[256,128]{1,0:T(8,128)(2,1)S(1)}, bf16[256,128]{1,0:T(8,128)(2,1)S(1)}, u32[]{:S(2)}, u32[]{:S(2)}) collective-permute-start(bf16[256,128]{1,0:T(8,128)(2,1)S(1)} %shard_map.91), channel_id=1, source_target_pairs={{0,24},{2,26},{4,28},{6,30},{8,0},{10,2},{12,4},{14,6},{16,8},{18,... | collective-permute-start | bytes 196616 | tf_op jit(solution)/shard_map/ppermute | solution.py:166
  105.5 17.8 %collective-permute-start.13 = (f32[16,256]{1,0:T(8,128)S(1)}, f32[16,256]{1,0:T(8,128)S(1)}, u32[]{:S(2)}, u32[]{:S(2)}) collective-permute-start(f32[16,256]{1,0:T(8,128)S(1)} %get-tuple-element.61), channel_id=1, source_target_pairs={{0,30},{2,0},{4,2},{6,4},{8,6},{10,8},{12,10},{14,12},{16,14},{18,... | collective-permute-start | bytes 49160 | tf_op jit(solution)/shard_map/ppermute | solution.py:166
  108.2 15.0 %collective-permute-start.20 = (bf16[256,128]{1,0:T(8,128)(2,1)S(1)}, bf16[256,128]{1,0:T(8,128)(2,1)S(1)}, u32[]{:S(2)}, u32[]{:S(2)}) collective-permute-start(bf16[256,128]{1,0:T(8,128)(2,1)S(1)} %get-tuple-element.67), channel_id=1, source_target_pairs={{0,2},{2,0},{4,6},{6,4},{8,10},{10,8},{12,14},{14,12},{16,18},{18,... | collective-permute-start | bytes 196616 | tf_op jit(solution)/shard_map/ppermute | solution.py:161
  108.3 15.0 %collective-permute-start.21 = (bf16[256,128]{1,0:T(8,128)(2,1)S(1)}, bf16[256,128]{1,0:T(8,128)(2,1)S(1)}, u32[]{:S(2)}, u32[]{:S(2)}) collective-permute-start(bf16[256,128]{1,0:T(8,128)(2,1)S(1)} %get-tuple-element.68), channel_id=1, source_target_pairs={{0,4},{2,6},{4,0},{6,2},{8,12},{10,14},{12,8},{14,10},{16,20},{18,... | collective-permute-start | bytes 196616 | tf_op jit(solution)/shard_map/ppermute | solution.py:161
  108.4 14.9 %collective-permute-start.22 = (bf16[256,128]{1,0:T(8,128)(2,1)S(1)}, bf16[256,128]{1,0:T(8,128)(2,1)S(1)}, u32[]{:S(2)}, u32[]{:S(2)}) collective-permute-start(bf16[256,128]{1,0:T(8,128)(2,1)S(1)} %get-tuple-element.69), channel_id=1, source_target_pairs={{0,6},{2,4},{4,2},{6,0},{8,14},{10,12},{12,10},{14,8},{16,22},{18,... | collective-permute-start | bytes 196616 | tf_op jit(solution)/shard_map/ppermute | solution.py:161
  (13 other events, 27.4 us)

commit v2 on v1

v2 whole, which is shorter than its diff:
```python
import math

import jax
import jax.numpy as jnp
from jax import lax
from jax.experimental import pallas as pl
from jax.experimental.pallas import tpu as pltpu
from jax.sharding import PartitionSpec as P

HEAD_DIM = 128
WINDOW = 256
GROUP = 4
HOLDERS = 3
STATS = 8
EPSILON = 1e-06
SCALE = 1.0 / math.sqrt(HEAD_DIM)
SCALE_LOG2 = SCALE * math.log2(math.e)
LN2 = math.log(2.0)
MASKED = -1e30
BF16 = jnp.bfloat16
F32 = jnp.float32
VMEM_LIMIT = 16 * 1024 * 1024
VMEM_MOST = 60 * 1024 * 1024


def dot_nn(left, right):
    return lax.dot_general(left, right, (((1,), (0,)), ((), ())), preferred_element_type=F32)


def dot_nt(left, right):
    return lax.dot_general(left, right, (((1,), (1,)), ((), ())), preferred_element_type=F32)


def dot_tn(left, right):
    return lax.dot_general(left, right, (((0,), (0,)), ((), ())), preferred_element_type=F32)


def tile_iotas():
    keys_at = lax.broadcasted_iota(jnp.int32, (WINDOW, WINDOW), 0)
    queries_at = lax.broadcasted_iota(jnp.int32, (WINDOW, WINDOW), 1)
    return keys_at, queries_at


def coef_row(start, count):
    at = start + lax.broadcasted_iota(jnp.int32, (1, count), 1)
    return 1.0 / jnp.sqrt(HEAD_DIM * (at + 1).astype(F32))


def coef_column(start, count):
    at = start + lax.broadcasted_iota(jnp.int32, (count, HEAD_DIM), 0)
    return 1.0 / jnp.sqrt(HEAD_DIM * (at + 1).astype(F32))


def heads_a_step(heads):
    return 2 if heads % 2 == 0 else 1


def chunks_of(heads):
    return 2 if heads % 4 == 0 else 1


def call(body, grid, in_specs, out_specs, out_shape, scratch, flops, moved, operands, aliases=None, along=(), after=(), vmem=VMEM_LIMIT):
    inputs, results, handed, skipped = len(operands), len(out_shape), len(along), len(after)

    def run(*refs):
        outs = inputs + handed + skipped
        body(*refs[:inputs], *refs[outs : outs + results], *refs[outs + results + handed :])

    given = pl.pallas_call(
        run,
        grid=grid,
        input_output_aliases={**(aliases or {}), **{inputs + at: results + at for at in range(handed)}},
        in_specs=list(in_specs) + [ANY] * (handed + skipped),
        out_specs=list(out_specs) + [ANY] * handed,
        out_shape=list(out_shape) + [jax.ShapeDtypeStruct(array.shape, array.dtype) for array in along],
        scratch_shapes=scratch,
        compiler_params=pltpu.CompilerParams(
            vmem_limit_bytes=vmem,
            dimension_semantics=("arbitrary",) * len(grid),
        ),
        cost_estimate=pl.CostEstimate(flops=flops, bytes_accessed=moved, transcendentals=0),
    )(*operands, *along, *after)
    return list(given[:results]), list(given[results:])


ANY = pl.BlockSpec(memory_space=pl.ANY)
HBM = pl.BlockSpec(memory_space=pltpu.HBM)


def chunk_spec(rows, wide, chunk, steps):
    return pl.BlockSpec((rows, wide), lambda at: (0, jnp.clip(at - chunk * steps, 0, steps - 1)))


def whole(shape):
    return pl.BlockSpec(shape, lambda *_: (0,) * len(shape))


def heads_a_part(heads):
    return -(-heads // HOLDERS)


def part_shape(heads):
    return (heads_a_part(heads) * HEAD_DIM, HEAD_DIM)


def part_at(held, head, reverse):
    each = held.shape[1] // HEAD_DIM
    at = lax.rem(head, each) * HEAD_DIM
    if not isinstance(at, int):
        at = pl.multiple_of(at, HEAD_DIM)
    return head // each + (GROUP - HOLDERS if reverse else 0), pl.ds(at, HEAD_DIM)


def store_state(held, head, state, reverse):
    slot, rows = part_at(held, head, reverse)
    held[slot, rows, :] = state


def held_state(held, head, reverse):
    slot, rows = part_at(held, head, reverse)
    return held[slot, rows, :]


def spread(held, outs):
    place = lax.rem(lax.axis_index("ctx"), GROUP)
    for other in range(GROUP):
        outs[other][...] = held[lax.bitwise_xor(place, jnp.int32(other))]


def collect(ins, held):
    place = lax.rem(lax.axis_index("ctx"), GROUP)
    for other in range(GROUP):
        held[lax.bitwise_xor(place, jnp.int32(other))] = ins[other][...]


def state_body(steps, k_ref, v_ref, *rest):
    outs, tails = rest[:GROUP], rest[GROUP:-4]
    k_held, v_held, held, done = rest[-4:]
    rows, width = k_held.shape
    wide = width // steps
    chunks = len(tails)
    columns = width // chunks
    loads, sends = [], {}
    for step in range(steps):
        cols = pl.ds(step * wide, wide)
        for at, (source, target) in enumerate(((k_ref, k_held), (v_ref, v_held))):
            loads.append(pltpu.make_async_copy(source.at[:, cols], target.at[:, cols], done.at[2 * step + at]))
    for step in range(steps):
        cols = pl.ds(step * wide, wide)
        chunk = step * wide // columns
        sends[step] = [
            pltpu.make_async_copy(
                source.at[pl.ds(rows - WINDOW, WINDOW), cols],
                tails[chunk].at[pl.ds(at * WINDOW, WINDOW), pl.ds(step * wide - chunk * columns, wide)],
                done.at[2 * (steps + step) + at],
            )
            for at, source in enumerate((k_held, v_held))
        ]
    held[...] = jnp.zeros_like(held)
    for copy in loads:
        copy.start()
    for step in range(steps):
        loads[2 * step].wait()
        loads[2 * step + 1].wait()
        for copy in sends[step]:
            copy.start()
        for head in range(step * wide // HEAD_DIM, (step + 1) * wide // HEAD_DIM):
            cols = slice(head * HEAD_DIM, (head + 1) * HEAD_DIM)
            store_state(held, head, dot_tn(k_held[:, cols], v_held[:, cols]).astype(BF16), False)
    spread(held, outs)
    for step in range(steps):
        for copy in sends[step]:
            copy.wait()


def local_states(keys, values):
    rows, width = keys.shape
    heads = width // HEAD_DIM
    chunks = chunks_of(heads)
    steps = heads // heads_a_step(heads)
    piece = part_shape(heads)
    tail = (2 * WINDOW, width // chunks)
    results, _ = call(
        lambda *refs: state_body(steps, *refs),
        (1,),
        [HBM] * 2,
        [whole(piece)] * GROUP + [ANY] * chunks,
        [jax.ShapeDtypeStruct(piece, BF16)] * GROUP + [jax.ShapeDtypeStruct(tail, BF16)] * chunks,
        [
            pltpu.VMEM((rows, width), BF16),
            pltpu.VMEM((rows, width), BF16),
            pltpu.VMEM((GROUP,) + piece, BF16),
            pltpu.SemaphoreType.DMA((4 * steps,)),
        ],
        2 * rows * width * HEAD_DIM,
        2 * 2 * rows * width,
        [keys, values],
        vmem=VMEM_MOST,
    )
    return results[:GROUP], results[GROUP:]


def total_body(*refs):
    total = refs[0][...].astype(F32)
    for ref in refs[1:-1]:
        total = total + ref[...].astype(F32)
    refs[-1][...] = total.astype(refs[-1].dtype)


def merge_body(reverse, groups, *refs):
    block = lax.axis_index("ctx")
    group = block // GROUP
    place = lax.rem(block, GROUP)
    others = refs[: groups - 1]
    own = refs[groups - 1 : groups - 1 + GROUP]
    outs = refs[groups - 1 + GROUP :]
    total = jnp.zeros(outs[0].shape, F32)
    for step in range(1, groups):
        wanted = group + step < groups if reverse else group - step >= 0
        total = total + others[step - 1][...].astype(F32) * wanted.astype(F32)
    for target in range(GROUP):
        to = lax.bitwise_xor(place, jnp.int32(target))
        result = total
        for source in range(GROUP):
            if source == target:
                continue
            of = lax.bitwise_xor(place, jnp.int32(source))
            wanted = of > to if reverse else of < to
            result = result + own[source][...].astype(F32) * wanted.astype(F32)
        outs[target][...] = result.astype(outs[target].dtype)


def swap(value, mask):
    count = lax.axis_size("ctx")
    return lax.ppermute(value, "ctx", [(at, at ^ mask) for at in range(count)])


def turn(value, steps):
    count = lax.axis_size("ctx")
    return lax.ppermute(value, "ctx", [(at, (at + steps) % count) for at in range(count)])


def shift(value, steps, places):
    count = lax.axis_size("ctx")
    return lax.ppermute(
        value, "ctx", [(at, at + steps) for at in range(count) if at % GROUP in places and 0 <= at + steps < count]
    )


def scan(pieces, reverse, first, second):
    groups = lax.axis_size("ctx") // GROUP
    shape = pieces[0].shape
    full = whole(shape)
    size = shape[0] * shape[1]
    out = jax.ShapeDtypeStruct(shape, BF16)
    own = [pieces[0]] + [swap(pieces[other], other) for other in range(1, GROUP)]
    along, after = first()
    (total,), held = call(
        total_body, (1,), [full] * GROUP, [full], [out], [], GROUP * size, 2 * 5 * size, own, None, along, after
    )
    holders = range(GROUP - HOLDERS, GROUP) if reverse else range(HOLDERS)
    others = [shift(total, (-GROUP if reverse else GROUP) * at, holders) for at in range(1, groups)]
    operands = others + own
    along, after = second(total, held)
    merged, held = call(
        lambda *refs: merge_body(reverse, groups, *refs),
        (1,),
        [full] * len(operands),
        [full] * GROUP,
        [out] * GROUP,
        [],
        20 * size,
        2 * 11 * size,
        operands,
        None,
        along,
        after,
    )
    return [merged[0]] + [swap(merged[other], other) for other in range(1, GROUP)], merged, held


def attend(scores, masks, coef, linear):
    shown = [jnp.where(mask, score, MASKED) for score, mask in zip(scores, masks)]
    peak = jnp.max(shown[0], 0, keepdims=True)
    for tile in shown[1:]:
        peak = jnp.maximum(peak, jnp.max(tile, 0, keepdims=True))
    powers = [jnp.exp2((tile - peak) * SCALE_LOG2) for tile in shown]
    norm = jnp.sum(powers[0], 0, keepdims=True)
    for tile in powers[1:]:
        norm = norm + jnp.sum(tile, 0, keepdims=True)
    share = 1.0 / norm
    probs = [tile * share for tile in powers]
    sums = []
    for prob, score, mask, kind in zip(probs, scores, masks, linear):
        if kind == "none":
            sums.append(None)
        elif kind == "all":
            sums.append((prob + score * coef).astype(BF16))
        else:
            sums.append((prob + jnp.where(mask, score * coef, 0.0)).astype(BF16))
    lse = peak * SCALE + jnp.log(norm)
    return [prob.astype(BF16) for prob in probs], sums, lse


def late_body(q_ref, k_ref, v_ref, *rest):
    prob_ref, sum_ref, part_ref = rest[-3:]
    rows = k_ref.shape[0]
    start = lax.axis_index("ctx") * rows
    keys_at, queries_at = tile_iotas()
    coef = coef_row(start + WINDOW, WINDOW)
    masks = [keys_at > queries_at, keys_at <= queries_at]
    for head in range(q_ref.shape[1] // HEAD_DIM):
        cols = slice(head * HEAD_DIM, (head + 1) * HEAD_DIM)
        query = q_ref[:, cols]
        scores = [dot_nt(k_ref[at * WINDOW : (at + 1) * WINDOW, cols], query) for at in range(2)]
        probs, sums, _ = attend(scores, masks, coef, ["all", "masked"])
        total = jnp.zeros((HEAD_DIM, WINDOW), F32)
        for at in range(2):
            prob_ref[head, at] = probs[at]
            sum_ref[head, at] = sums[at]
            total = total + dot_tn(v_ref[at * WINDOW : (at + 1) * WINDOW, cols], sums[at])
        part_ref[:, cols] = total.T


def late_rows(chunk, queries, keys, values, done, along, after):
    rows, width = keys.shape
    heads = width // HEAD_DIM
    step = heads_a_step(heads)
    steps = heads // step // chunks_of(heads)
    ahead = chunk * steps
    tiles = (heads, 2, WINDOW, WINDOW)
    tile_spec = pl.BlockSpec((step,) + tiles[1:], lambda at: (at + ahead, 0, 0, 0))
    wide = step * HEAD_DIM
    return call(
        late_body,
        (steps,),
        [
            pl.BlockSpec((WINDOW, wide), lambda at: (1, at + ahead)),
            pl.BlockSpec((rows, wide), lambda at: (0, at + ahead)),
            pl.BlockSpec((rows, wide), lambda at: (0, at + ahead)),
        ]
        + [ANY] * len(done),
        [tile_spec, tile_spec, pl.BlockSpec((WINDOW, wide), lambda at: (0, at + ahead))],
        [
            jax.ShapeDtypeStruct(tiles, BF16),
            jax.ShapeDtypeStruct(tiles, BF16),
            jax.ShapeDtypeStruct((WINDOW, width), F32),
        ],
        [],
        4 * 2 * WINDOW * WINDOW * width * 2,
        12 * WINDOW * width,
        [queries, keys, values, *done],
        {3 + at: at for at in range(3)} if done else None,
        along,
        after,
    )


def early_body(first, q_ref, k_ref, v_ref, tail_ref, *rest):
    prob_ref, sum_ref, inside_ref, window_ref, lse_ref = rest[-5:]
    done = rest[:-5]
    rows = k_ref.shape[0] * 2
    block = lax.axis_index("ctx")
    at_step = pl.program_id(0)

    @pl.when(at_step == 0)
    def _():
        lse_ref[...] = done[4][...] if done else jnp.zeros_like(lse_ref)

    keys_at, queries_at = tile_iotas()
    beyond = jnp.where(block > 0, 0, 2 * WINDOW)
    masks = [keys_at > queries_at + beyond, keys_at <= queries_at]
    coef = coef_row(block * rows, WINDOW)
    step = q_ref.shape[1] // HEAD_DIM
    for head in range(step):
        cols = slice(head * HEAD_DIM, (head + 1) * HEAD_DIM)
        query = q_ref[:, cols]
        scores = [dot_nt(tail_ref[:WINDOW, cols], query), dot_nt(k_ref[:, cols], query)]
        probs, sums, lse = attend(scores, masks, coef, ["none", "masked"])
        prob_ref[head, 0] = probs[0]
        prob_ref[head, 1] = probs[1]
        sum_ref[head] = sums[1]
        lse_ref[pl.ds(first + at_step * step + head, 1), :] = lse
        value = v_ref[:, cols]
        before = dot_tn(tail_ref[WINDOW:, cols], probs[0])
        window_ref[:, cols] = (before + dot_tn(value, probs[1])).T
        inside_ref[:, cols] = (before + dot_tn(value, sums[1])).T


def early_rows(chunk, queries, keys, values, before, done, along):
    rows, width = keys.shape
    heads = width // HEAD_DIM
    step = heads_a_step(heads)
    steps = heads // step // chunks_of(heads)
    ahead = chunk * steps
    wide = step * HEAD_DIM
    half = pl.BlockSpec((WINDOW, wide), lambda at: (0, at + ahead))
    own = pl.BlockSpec((2 * WINDOW, wide), lambda at: (0, at))
    tiles = (heads, 2, WINDOW, WINDOW)
    small = whole((STATS, WINDOW))
    return call(
        lambda *refs: early_body(ahead * step, *refs),
        (steps,),
        [half, half, half, own] + ([ANY] * 4 + [small] if done else []),
        [
            pl.BlockSpec((step,) + tiles[1:], lambda at: (at + ahead, 0, 0, 0)),
            pl.BlockSpec((step, WINDOW, WINDOW), lambda at: (at + ahead, 0, 0)),
            half,
            half,
            small,
        ],
        [
            jax.ShapeDtypeStruct(tiles, BF16),
            jax.ShapeDtypeStruct((heads, WINDOW, WINDOW), BF16),
            jax.ShapeDtypeStruct((WINDOW, width), F32),
            jax.ShapeDtypeStruct((WINDOW, width), F32),
            jax.ShapeDtypeStruct((STATS, WINDOW), F32),
        ],
        [],
        5 * 2 * WINDOW * WINDOW * width * 2,
        8 * WINDOW * width,
        [queries, keys, values, before, *done],
        {4 + at: at for at in range(4)} if done else None,
        along,
    )


def sum_body(steps, q_ref, inside_ref, part_ref, gain_ref, cot_ref, *rest):
    ins = rest[:GROUP]
    hidden_ref, norm_ref, held, squares, crossed = rest[GROUP:]
    rows = q_ref.shape[0]
    at_step = pl.program_id(0)
    step = q_ref.shape[1] // HEAD_DIM

    @pl.when(at_step == 0)
    def _():
        collect(ins, held)
        squares[...] = jnp.zeros_like(squares)
        crossed[...] = jnp.zeros_like(crossed)

    columns = coef_column(lax.axis_index("ctx") * rows, rows)
    for head in range(step):
        cols = slice(head * HEAD_DIM, (head + 1) * HEAD_DIM)
        carried = columns * dot_nn(q_ref[:, cols], held_state(held, at_step * step + head, False))
        hidden = jnp.concatenate([inside_ref[:, cols], part_ref[:, cols]], 0) + carried
        hidden_ref[:, cols] = hidden
        scaled = gain_ref[:, cols].astype(F32) * cot_ref[:, cols].astype(F32)
        squares[...] += hidden * hidden
        crossed[...] += hidden * scaled

    @pl.when(at_step == steps - 1)
    def _():
        norm_ref[...] = jnp.zeros_like(norm_ref)
        norm_ref[0:1, :] = jnp.sum(squares[...].T, 0, keepdims=True)
        norm_ref[1:2, :] = jnp.sum(crossed[...].T, 0, keepdims=True)


def add_prefix(queries, inside, part, gain, cotangent, prefix):
    rows, width = queries.shape
    heads = width // HEAD_DIM
    step = heads_a_step(heads)
    steps = heads // step
    wide = step * HEAD_DIM
    piece = prefix[0].shape
    half = pl.BlockSpec((WINDOW, wide), lambda at: (0, at))
    full = pl.BlockSpec((rows, wide), lambda at: (0, at))
    return call(
        lambda *refs: sum_body(steps, *refs),
        (steps,),
        [full, half, half, pl.BlockSpec((1, wide), lambda at: (0, at)), full] + [whole(piece)] * GROUP,
        [full, whole((STATS, rows))],
        [jax.ShapeDtypeStruct((rows, width), F32), jax.ShapeDtypeStruct((STATS, rows), F32)],
        [
            pltpu.VMEM((GROUP,) + piece, BF16),
            pltpu.VMEM((rows, HEAD_DIM), F32),
            pltpu.VMEM((rows, HEAD_DIM), F32),
        ],
        2 * rows * width * HEAD_DIM,
        12 * rows * width,
        [queries, inside, part, gain, cotangent, *prefix],
    )[0]


def stat_rows(width):
    return 2 * STATS * -(-3 * WINDOW // width)


def stat_place(width, part):
    across = width // WINDOW
    return (
        slice(WINDOW + part // across * 2 * STATS, WINDOW + (part // across + 1) * 2 * STATS),
        slice(part % across * WINDOW, (part % across + 1) * WINDOW),
    )


def norm_body(steps, features, norm_ref, hidden_ref, gain_ref, cot_ref, q_ref, window_ref, lse_ref, *rest):
    out_ref, grad_ref, first_ref = rest[:3]
    outs = rest[3 : 3 + GROUP]
    held, recip, pull, stats = rest[3 + GROUP :]
    rows, wide = q_ref.shape
    start = lax.axis_index("ctx") * rows
    at_step = pl.program_id(0)
    step = wide // HEAD_DIM

    @pl.when(at_step == 0)
    def _():
        root = 1.0 / jnp.sqrt(norm_ref[0:1, :] / features + EPSILON)
        slope = root * root * root * norm_ref[1:2, :] / features
        recip[...] = jnp.broadcast_to(root, (HEAD_DIM, rows)).T
        pull[...] = jnp.broadcast_to(slope, (HEAD_DIM, rows)).T
        stats[...] = jnp.zeros_like(stats)
        stats[:STATS, :] = lse_ref[...]
        held[...] = jnp.zeros_like(held)

    columns = coef_column(start, rows)
    for head in range(step):
        cols = slice(head * HEAD_DIM, (head + 1) * HEAD_DIM)
        hidden = hidden_ref[:, cols]
        gain = gain_ref[:, cols].astype(F32)
        kept = recip[...]
        out_ref[:, cols] = (hidden * kept * gain).astype(BF16)
        full = kept * (gain * cot_ref[:, cols].astype(F32)) - hidden * pull[...]
        grad = full.astype(BF16)
        grad_ref[:, cols] = grad
        first_ref[:WINDOW, pl.ds(pl.multiple_of(at_step * wide, HEAD_DIM) + head * HEAD_DIM, HEAD_DIM)] = grad[:WINDOW]
        delta = (grad[:WINDOW].astype(F32) * window_ref[:, cols]).T
        stats[pl.ds(STATS + at_step * step + head, 1), :] = jnp.sum(delta, 0, keepdims=True)
        state = dot_tn(q_ref[:, cols], (full * columns).astype(BF16)).astype(BF16)
        store_state(held, at_step * step + head, state, True)

    @pl.when(at_step == steps - 1)
    def _():
        spread(held, outs)
        left = stats[...]
        first_ref[WINDOW:, :] = jnp.zeros((first_ref.shape[0] - WINDOW, first_ref.shape[1]), BF16)
        for part in range(3):
            at_rows, at_cols = stat_place(first_ref.shape[1], part)
            taken = left.astype(BF16)
            first_ref[at_rows, at_cols] = taken
            left = left - taken.astype(F32)


def normalize(norms, hidden, gain, cotangent, queries, window, lse, features):
    rows, width = queries.shape
    heads = width // HEAD_DIM
    step = heads_a_step(heads)
    steps = heads // step
    wide = step * HEAD_DIM
    piece = part_shape(heads)
    first = (WINDOW + stat_rows(width), width)
    half = pl.BlockSpec((WINDOW, wide), lambda at: (0, at))
    full = pl.BlockSpec((rows, wide), lambda at: (0, at))
    return call(
        lambda *refs: norm_body(steps, features, *refs),
        (steps,),
        [
            whole((STATS, rows)),
            full,
            pl.BlockSpec((1, wide), lambda at: (0, at)),
            full,
            full,
            half,
            whole((STATS, WINDOW)),
        ],
        [full, full, whole(first)] + [whole(piece)] * GROUP,
        [
            jax.ShapeDtypeStruct((rows, width), BF16),
            jax.ShapeDtypeStruct((rows, width), BF16),
            jax.ShapeDtypeStruct(first, BF16),
        ]
        + [jax.ShapeDtypeStruct(piece, BF16)] * GROUP,
        [
            pltpu.VMEM((GROUP,) + piece, BF16),
            pltpu.VMEM((rows, HEAD_DIM), F32),
            pltpu.VMEM((rows, HEAD_DIM), F32),
            pltpu.VMEM((2 * STATS, WINDOW), F32),
        ],
        2 * rows * width * HEAD_DIM,
        14 * rows * width,
        [norms, hidden, gain, cotangent, queries, window, lse],
    )[0]


def back_body(first, q_ref, k_ref, v_ref, g_ref, tail_ref, p0_ref, s0_ref, p1_ref, s1_ref, *rest):
    ins = rest[:GROUP]
    dq_ref, dk_ref, dv_ref, held = rest[-4:]
    rows = q_ref.shape[0]
    start = lax.axis_index("ctx") * rows
    at_step = pl.program_id(0)
    step = q_ref.shape[1] // HEAD_DIM

    @pl.when(at_step == 0)
    def _():
        collect(ins, held)

    keys_at, queries_at = tile_iotas()
    causal = keys_at <= queries_at
    columns = coef_column(start, rows)
    ratios = coef_row(start, rows) * (1.0 / SCALE)
    for head in range(step):
        cols = slice(head * HEAD_DIM, (head + 1) * HEAD_DIM)
        early, late = slice(0, WINDOW), slice(WINDOW, 2 * WINDOW)
        grads = g_ref[early, cols], g_ref[late, cols]
        queries = q_ref[early, cols], q_ref[late, cols]
        keys = tail_ref[:WINDOW, cols], k_ref[early, cols], k_ref[late, cols]
        values = tail_ref[WINDOW:, cols], v_ref[early, cols], v_ref[late, cols]
        probs = (
            (p0_ref[head, 0].astype(F32), p0_ref[head, 1].astype(F32)),
            (p1_ref[head, 0].astype(F32), p1_ref[head, 1].astype(F32)),
        )
        edges = []
        for half in range(2):
            ratio = ratios[:, half * WINDOW : (half + 1) * WINDOW]
            pulls = [dot_nt(values[half + at], grads[half]) for at in range(2)]
            delta = jnp.sum(probs[half][0] * pulls[0] + probs[half][1] * pulls[1], 0, keepdims=True)
            before = probs[half][0] * (pulls[0] - delta)
            if half == 1:
                before = before + pulls[0] * ratio
            here = probs[half][1] * (pulls[1] - delta) + jnp.where(causal, pulls[1] * ratio, 0.0)
            edges.append((before.astype(BF16), here.astype(BF16)))
        state = held_state(held, first + at_step * step + head, False)
        inner = [
            (dot_tn(keys[half], edges[half][0]) + dot_tn(keys[half + 1], edges[half][1])).T * SCALE for half in range(2)
        ]
        carried = columns * dot_nt(g_ref[:, cols], state)
        dq_ref[:, cols] = (jnp.concatenate(inner, 0) + carried).astype(BF16)
        dk_ref[early, cols] = SCALE * (dot_nn(edges[0][1], queries[0]) + dot_nn(edges[1][0], queries[1]))
        dk_ref[late, cols] = SCALE * dot_nn(edges[1][1], queries[1])
        dv_ref[early, cols] = dot_nn(s0_ref[head], grads[0]) + dot_nn(s1_ref[head, 0], grads[1])
        dv_ref[late, cols] = dot_nn(s1_ref[head, 1], grads[1])


def backward(chunk, queries, keys, values, grads, before, probs0, sums0, probs1, sums1, prefix, done, along, after):
    rows, width = keys.shape
    heads = width // HEAD_DIM
    chunks = chunks_of(heads)
    step = heads_a_step(heads)
    steps = heads // step // chunks
    ahead = chunk * steps
    wide = step * HEAD_DIM
    piece = prefix[0].shape
    own_tail = pl.BlockSpec((2 * WINDOW, wide), lambda at: (0, at))
    own_full = pl.BlockSpec((rows, wide), lambda at: (0, at))
    full = pl.BlockSpec((rows, wide), lambda at: (0, at + ahead))
    pair = pl.BlockSpec((step, 2, WINDOW, WINDOW), lambda at: (at + ahead, 0, 0, 0))
    single = pl.BlockSpec((step, WINDOW, WINDOW), lambda at: (at + ahead, 0, 0))
    return call(
        lambda *refs: back_body(ahead * step, *refs),
        (steps,),
        [full, full, full, full, own_tail, pair, single, pair, pair] + [whole(piece)] * GROUP + [ANY] * len(done),
        [full, own_full, own_full],
        [
            jax.ShapeDtypeStruct((rows, width), BF16),
            jax.ShapeDtypeStruct((rows, width // chunks), F32),
            jax.ShapeDtypeStruct((rows, width // chunks), F32),
        ],
        [pltpu.VMEM((GROUP,) + piece, BF16)],
        8 * 2 * WINDOW * WINDOW * width * 2,
        20 * WINDOW * width * 2,
        [queries, keys, values, grads, before, probs0, sums0, probs1, sums1, *prefix, *done],
        {9 + GROUP: 0} if done else None,
        along,
        after,
    )


def last_body(first, last, k_ref, v_ref, dk_in, dv_in, qn_ref, gn_ref, sent_ref, *rest):
    ins = rest[:GROUP]
    dk_ref, dv_ref, held, stats = rest[-4:]
    at_step = pl.program_id(0)
    step = k_ref.shape[1] // HEAD_DIM

    @pl.when(at_step == 0)
    def _():
        collect(ins, held)
        total = jnp.zeros(stats.shape, F32)
        for part in range(3):
            at_rows, at_cols = stat_place(sent_ref.shape[1], 2 - part)
            total = total + sent_ref[at_rows, at_cols].astype(F32)
        stats[...] = total

    keys_at, queries_at = tile_iotas()
    beyond = jnp.where(lax.axis_index("ctx") < last, 0, 2 * WINDOW)
    mask = keys_at > queries_at + beyond
    for head in range(step):
        cols = slice(head * HEAD_DIM, (head + 1) * HEAD_DIM)
        at = first + at_step * step + head
        early, late = slice(0, WINDOW), slice(WINDOW, 2 * WINDOW)
        query, grad = qn_ref[:, cols], gn_ref[:, cols]
        lse = stats[pl.ds(at, 1), :] * (1.0 / LN2)
        delta = stats[pl.ds(STATS + at, 1), :]
        scores = dot_nt(k_ref[late, cols], query) * SCALE_LOG2
        probs = jnp.where(mask, jnp.exp2(scores - lse), 0.0)
        edges = probs * (dot_nt(v_ref[late, cols], grad) - delta)
        state = held_state(held, at, True)
        keys = dk_in[:, cols] + dot_nt(v_ref[:, cols], state)
        values = dv_in[:, cols] + dot_nn(k_ref[:, cols], state)
        dk_ref[early, cols] = keys[early].astype(BF16)
        dv_ref[early, cols] = values[early].astype(BF16)
        dk_ref[late, cols] = (keys[late] + SCALE * dot_nn(edges.astype(BF16), query)).astype(BF16)
        dv_ref[late, cols] = (values[late] + dot_nn(probs.astype(BF16), grad)).astype(BF16)


def finish(chunk, keys, values, dk_part, dv_part, queries_after, grads_after, suffix, done):
    rows, width = keys.shape
    heads = width // HEAD_DIM
    step = heads_a_step(heads)
    steps = heads // step // chunks_of(heads)
    ahead = chunk * steps
    wide = step * HEAD_DIM
    piece = suffix[0].shape
    last = lax.axis_size("ctx") - 1
    half = pl.BlockSpec((WINDOW, wide), lambda at: (0, at + ahead))
    own_full = pl.BlockSpec((rows, wide), lambda at: (0, at))
    full = pl.BlockSpec((rows, wide), lambda at: (0, at + ahead))
    return call(
        lambda *refs: last_body(ahead * step, last, *refs),
        (steps,),
        [full, full, own_full, own_full, half, half, whole(grads_after.shape)] + [whole(piece)] * GROUP + [ANY] * len(done),
        [full, full],
        [jax.ShapeDtypeStruct((rows, width), BF16)] * 2,
        [pltpu.VMEM((GROUP,) + piece, BF16), pltpu.VMEM((2 * STATS, WINDOW), F32)],
        4 * 2 * WINDOW * WINDOW * width,
        9 * rows * width,
        [keys, values, dk_part, dv_part, queries_after, grads_after, grads_after, *suffix, *done],
        {7 + GROUP: 0, 8 + GROUP: 1} if done else None,
    )[0]


def summed(value, axis):
    count = lax.axis_size(axis)
    mask = 1
    while mask < count:
        value = value + lax.ppermute(value, axis, [(at, at ^ mask) for at in range(count)])
        mask *= 2
    return value


def on_device(queries, keys, values, gain, cotangent):
    rows, width = queries.shape
    features = width * lax.axis_size("head")
    chunks = chunks_of(width // HEAD_DIM)
    gain = gain.reshape(1, width)
    before, own = [], {}

    pieces, tails = local_states(keys, values)

    def send_tails(total, held):
        before.extend(turn(tail, 1) for tail in held)
        return [], []

    prefix, merged, _ = scan(pieces, False, lambda: (tails, []), send_tails)
    late = []
    for chunk in range(chunks):
        late, _ = late_rows(chunk, queries, keys, values, late, [], merged[:1])
    probs1, sums1, part = late
    early, handed = [], [queries[:WINDOW]]
    for chunk in range(chunks):
        early, sent = early_rows(chunk, queries, keys, values, before[chunk], early, handed)
        if chunk == 0:
            after, handed = turn(sent[0], -1), []
    probs0, sums0, inside, window, lse = early
    hidden, norms = add_prefix(queries, inside, part, gain, cotangent, prefix)
    norms = summed(norms, "head")
    output, grads, first, *states = normalize(norms, hidden, gain, cotangent, queries, window, lse, features)

    def own_chunk(chunk, after):
        own[chunk], _ = backward(
            chunk, queries, keys, values, grads, before[chunk], probs0, sums0, probs1, sums1, prefix,
            own[chunk - 1][:1] if chunk else [], [], after,
        )

    def send_grads(total, held):
        grads_after.append(turn(held[0], -1))
        return [], []

    grads_after = []
    own_chunk(0, [])
    suffix, merged, _ = scan(states, True, lambda: ([first], [after, own[0][1]]), send_grads)
    for chunk in range(1, chunks):
        own_chunk(chunk, merged[:1])
    result = []
    for chunk in range(chunks):
        _, dk_part, dv_part = own[chunk]
        result = finish(chunk, keys, values, dk_part, dv_part, after, grads_after[0], suffix, result)
    return output, own[chunks - 1][0], *result


def solution(mesh):
    wide = P("ctx", "head")
    return jax.shard_map(
        on_device,
        mesh=mesh,
        in_specs=(wide, wide, wide, P("head"), wide),
        out_specs=(wide, wide, wide, wide),
        check_vma=False,
    )
```

time: 129 us -> 97.1 us (0.75)
  waiting for transfers between devices: 42.6 us -> 17.7 us
  local copies, waits for them, and re-layouts: 17.4 us -> 0.96 us
  starting transfers between devices: 33.9 us -> 42.2 us
  Pallas kernels: 30.3 us -> 35.2 us
  blocking collectives: 3.35 us -> 0 us
    ppermute x12, waiting for transfers between devices: 26.2 us -> 6.48 us  [swap(): return lax.ppermute(value, 'ctx', [(at, at ^ mask) for at in range(count)])]
    unnamed x44 -> x12, local copies, waits for them, and re-layouts: 14.2 us -> 0.92 us
    ppermute x11 -> x4, starting transfers between devices: 22.7 us -> 9.64 us  [turn(): lax.ppermute(value, 'ctx', [(at, (at + steps) % count) for at in range(co...]
    ppermute x0 -> x7, starting transfers between devices: none -> 11.5 us  [the longest x6 11.4 us: shift(): lax.ppermute(value, 'ctx', [(at, at + steps) for at in range(count) if at...]
    ppermute x12, starting transfers between devices: 11.1 us -> 21.1 us  [swap(): return lax.ppermute(value, 'ctx', [(at, at ^ mask) for at in range(count)])]
    ppermute x11 -> x4, waiting for transfers between devices: 16.3 us -> 7.93 us  [turn(): lax.ppermute(value, 'ctx', [(at, (at + steps) % count) for at in range(co...]
    pallas_call x10 -> x15, Pallas kernels: 30.3 us -> 35.2 us  [call(): pl.pallas_call(run, grid=grid, input_output_aliases={**(aliases or {}), *...]
    psum x1 -> x0, blocking collectives: 3.35 us -> none  [on_device(): norms = lax.psum(norms, 'head')]
  transfers between devices with their start and end apart: 23 -> 23, of which waited for: 10 -> 9; matrix products, arithmetic and copies ran while one was open for 1% -> 0% of each run, Pallas kernels for 20% -> 27%
where the time goes in v2:
time: 97.1 us; the launch traced here: 96.9 us
  starting transfers between devices  42.2 us (43%)
  Pallas kernels  35.2 us (36%)
  waiting for transfers between devices  17.7 us (18%)
    pallas_call x15, Pallas kernels, call(): pl.pallas_call(run, grid=grid, input_output_aliases={**(aliases or {}), *...  35.2 us
    ppermute x12, starting transfers between devices, swap(): return lax.ppermute(value, 'ctx', [(at, at ^ mask) for at in range(count)])  21.1 us
    ppermute x6, starting transfers between devices, shift(): lax.ppermute(value, 'ctx', [(at, at + steps) for at in range(count) if at...  11.4 us
    ppermute x4, starting transfers between devices, turn(): lax.ppermute(value, 'ctx', [(at, (at + steps) % count) for at in range(co...  9.64 us
    ppermute x4, waiting for transfers between devices, turn(): lax.ppermute(value, 'ctx', [(at, (at + steps) % count) for at in range(co...  7.93 us
    ppermute x12, waiting for transfers between devices, swap(): return lax.ppermute(value, 'ctx', [(at, at ^ mask) for at in range(count)])  6.48 us
    ppermute x6, waiting for transfers between devices, shift(): lax.ppermute(value, 'ctx', [(at, at + steps) for at in range(count) if at...  2.11 us
  transfers between devices with their start and end apart: 23, of which 9 were waited for; matrix products, arithmetic and copies ran while one was open for 0% of the time, Pallas kernels for 27%

profile of v2, /device:TPU:0, one launch (start us, length us, event | category | flops | bytes accessed | tf_op | source)
XLA Modules:
  0.0 96.9 jit_solution(16517717548285410675)
XLA Ops:
  0.7 3.6 %shard_map.84 = (bf16[384,128]{1,0:T(8,128)(2,1)}, bf16[384,128]{1,0:T(8,128)(2,1)}, bf16[384,128]{1,0:T(8,128)(2,1)}, bf16[384,128]{1,0:T(8,128)(2,1)}, bf16[51...) custom-call(bf16[512,1024]{1,0:T(8,128)(2,1)} %refs_0_.19, bf16[512,1024]{1,0:T(8,128)(2,1)} %refs_1_.17), custom_call_target="tpu_custom_call" | custom-call | flops 134217728 | bytes 2097152 | tf_op jit(solution)/shard_map/pallas_call | solution.py:69
  4.3 3.0 %collective-permute-start = (bf16[384,128]{1,0:T(8,128)(2,1)}, bf16[384,128]{1,0:T(8,128)(2,1)S(1)}, u32[]{:S(2)}, u32[]{:S(2)}) collective-permute-start(bf16[384,128]{1,0:T(8,128)(2,1)} %get-tuple-element.60), channel_id=1, source_target_pairs={{0,2},{2,0},{4,6},{6,4},{8,10},{10,8},{12,14},{14,12},{16,18},{18,... | collective-permute-start | bytes 294920 | tf_op jit(solution)/shard_map/ppermute | solution.py:235
  7.3 1.5 %collective-permute-start.1 = (bf16[384,128]{1,0:T(8,128)(2,1)}, bf16[384,128]{1,0:T(8,128)(2,1)S(1)}, u32[]{:S(2)}, u32[]{:S(2)}) collective-permute-start(bf16[384,128]{1,0:T(8,128)(2,1)} %get-tuple-element.61), channel_id=1, source_target_pairs={{0,4},{2,6},{4,0},{6,2},{8,12},{10,14},{12,8},{14,10},{16,20},{18,... | collective-permute-start | bytes 294920 | tf_op jit(solution)/shard_map/ppermute | solution.py:235
  8.8 1.8 %collective-permute-done.refs_1_.refs_4_ = bf16[384,128]{1,0:T(8,128)(2,1)S(1)} collective-permute-done((bf16[384,128]{1,0:T(8,128)(2,1)}, bf16[384,128]{1,0:T(8,128)(2,1)S(1)}, u32[]{:S(2)}, u32[]{:S(2)}) %collective-permute-start) | collective-permute-done | bytes 98336 | tf_op jit(solution)/shard_map/ppermute | solution.py:235
  10.7 2.5 %collective-permute-done.1.refs_2_.refs_5_ = bf16[384,128]{1,0:T(8,128)(2,1)S(1)} collective-permute-done((bf16[384,128]{1,0:T(8,128)(2,1)}, bf16[384,128]{1,0:T(8,128)(2,1)S(1)}, u32[]{:S(2)}, u32[]{:S(2)}) %collective-permute-start.1) | collective-permute-done | bytes 98336 | tf_op jit(solution)/shard_map/ppermute | solution.py:235
  13.2 1.4 %collective-permute-done.2.refs_3_.refs_6_ = bf16[384,128]{1,0:T(8,128)(2,1)S(1)} collective-permute-done((bf16[384,128]{1,0:T(8,128)(2,1)}, bf16[384,128]{1,0:T(8,128)(2,1)S(1)}, u32[]{:S(2)}, u32[]{:S(2)}) %collective-permute-start.2) | collective-permute-done | bytes 98336 | tf_op jit(solution)/shard_map/ppermute | solution.py:235
  16.2 1.7 %collective-permute-start.3 = (bf16[512,512]{1,0:T(8,128)(2,1)}, bf16[512,512]{1,0:T(8,128)(2,1)S(1)}, u32[]{:S(2)}, u32[]{:S(2)}) collective-permute-start(bf16[512,512]{1,0:T(8,128)(2,1)} %get-tuple-element.65), channel_id=1, source_target_pairs={{0,2},{2,4},{4,6},{6,8},{8,10},{10,12},{12,14},{14,16},{16,18},{18... | collective-permute-start | bytes 1572872 | tf_op jit(solution)/shard_map/ppermute | solution.py:240
  17.9 5.5 %collective-permute-start.7 = (bf16[384,128]{1,0:T(8,128)(2,1)S(1)}, bf16[384,128]{1,0:T(8,128)(2,1)S(1)}, u32[]{:S(2)}, u32[]{:S(2)}) collective-permute-start(bf16[384,128]{1,0:T(8,128)(2,1)S(1)} %get-tuple-element.73), channel_id=1, source_target_pairs={{0,24},{2,26},{4,28},{1,25},{3,27},{5,29}} | collective-permute-start | bytes 294920 | tf_op jit(solution)/shard_map/ppermute | solution.py:245
  23.4 1.3 %collective-permute-start.6 = (bf16[384,128]{1,0:T(8,128)(2,1)S(1)}, bf16[384,128]{1,0:T(8,128)(2,1)S(1)}, u32[]{:S(2)}, u32[]{:S(2)}) collective-permute-start(bf16[384,128]{1,0:T(8,128)(2,1)S(1)} %get-tuple-element.73), channel_id=1, source_target_pairs={{0,16},{2,18},{4,20},{8,24},{10,26},{12,28},{1,17},{3,19},{5,21},{... | collective-permute-start | bytes 294920 | tf_op jit(solution)/shard_map/ppermute | solution.py:245
  24.7 2.5 %collective-permute-start.5 = (bf16[384,128]{1,0:T(8,128)(2,1)S(1)}, bf16[384,128]{1,0:T(8,128)(2,1)S(1)}, u32[]{:S(2)}, u32[]{:S(2)}) collective-permute-start(bf16[384,128]{1,0:T(8,128)(2,1)S(1)} %get-tuple-element.73), channel_id=1, source_target_pairs={{0,8},{2,10},{4,12},{8,16},{10,18},{12,20},{16,24},{18,26},{20,28}... | collective-permute-start | bytes 294920 | tf_op jit(solution)/shard_map/ppermute | solution.py:245
  27.5 1.9 %collective-permute-done.5.refs_0_ = bf16[384,128]{1,0:T(8,128)(2,1)S(1)} collective-permute-done((bf16[384,128]{1,0:T(8,128)(2,1)S(1)}, bf16[384,128]{1,0:T(8,128)(2,1)S(1)}, u32[]{:S(2)}, u32[]{:S(2)}) %collective-permute-start.5) | collective-permute-done | bytes 98336 | tf_op jit(solution)/shard_map/ppermute | solution.py:245
  30.6 2.6 %collective-permute-start.10 = (bf16[384,128]{1,0:T(8,128)(2,1)S(1)}, bf16[384,128]{1,0:T(8,128)(2,1)S(1)}, u32[]{:S(2)}, u32[]{:S(2)}) collective-permute-start(bf16[384,128]{1,0:T(8,128)(2,1)S(1)} %get-tuple-element.81), channel_id=1, source_target_pairs={{0,6},{2,4},{4,2},{6,0},{8,14},{10,12},{12,10},{14,8},{16,22},{18,... | collective-permute-start | bytes 294920 | tf_op jit(solution)/shard_map/ppermute | solution.py:235
  33.3 1.1 %collective-permute-done.4.refs_3_.refs_4_ = bf16[512,512]{1,0:T(8,128)(2,1)S(1)} collective-permute-done((bf16[512,512]{1,0:T(8,128)(2,1)}, bf16[512,512]{1,0:T(8,128)(2,1)S(1)}, u32[]{:S(2)}, u32[]{:S(2)}) %collective-permute-start.4) | collective-permute-done | bytes 524320 | tf_op jit(solution)/shard_map/ppermute | solution.py:240
  34.4 2.6 %shard_map.86 = (bf16[8,2,256,256]{3,2,1,0:T(8,128)(2,1)S(1)}, bf16[8,256,256]{2,1,0:T(8,128)(2,1)S(1)}, f32[256,1024]{1,0:T(8,128)S(1)}, f32[256,1024]{1,0:T(8,...) custom-call(bf16[512,1024]{1,0:T(8,128)(2,1)S(1)} %copy-done.2, ...), custom_call_target="tpu_custom_call", output_to_operand_aliasing={{5}: (4, {})} | custom-call | flops 1342177280 | bytes 2097152 | tf_op jit(solution)/shard_map/pallas_call | solution.py:69
  37.0 2.3 %collective-permute-start.15 = (bf16[256,1024]{1,0:T(8,128)(2,1)S(1)}, bf16[256,1024]{1,0:T(8,128)(2,1)S(1)}, u32[]{:S(2)}, u32[]{:S(2)}) collective-permute-start(bf16[256,1024]{1,0:T(8,128)(2,1)S(1)} %get-tuple-element.98), channel_id=1, source_target_pairs={{0,30},{2,0},{4,2},{6,4},{8,6},{10,8},{12,10},{14,12},{16,14},{18,... | collective-permute-start | bytes 1572872 | tf_op jit(solution)/shard_map/ppermute | solution.py:240
  39.3 2.6 %shard_map.89 = (bf16[8,2,256,256]{3,2,1,0:T(8,128)(2,1)S(1)}, bf16[8,2,256,256]{3,2,1,0:T(8,128)(2,1)S(1)}, f32[256,1024]{1,0:T(8,128)S(1)}) custom-call(bf16[512,1024]{1,0:T(8,128)(2,1)S(1)} %copy-done.2, bf16[512,1024]{1,0:T(8,128)(2,1)S(1)} %copy-done, bf16[512,1024]{1,0:T(8,128)(2,1)S(1)} %copy-done.1, ...), custom_call_target="tpu_custom_call" | custom-call | flops 1073741824 | bytes 3145728 | tf_op jit(solution)/shard_map/pallas_call | solution.py:69
  41.9 2.6 %shard_map.90 = (bf16[8,2,256,256]{3,2,1,0:T(8,128)(2,1)S(1)}, bf16[8,2,256,256]{3,2,1,0:T(8,128)(2,1)S(1)}, f32[256,1024]{1,0:T(8,128)S(1)}) custom-call(bf16[512,1024]{1,0:T(8,128)(2,1)S(1)} %copy-done.2, bf16[512,1024]{1,0:T(8,128)(2,1)S(1)} %copy-done, ...), custom_call_target="tpu_custom_call", output_to_operand_aliasing={{0}: (3, {}), {1}: (4, {}), {2}: (5, {})} | custom-call | flops 1073741824 | bytes 3145728 | tf_op jit(solution)/shard_map/pallas_call | solution.py:69
  44.5 6.8 %collective-permute-done.3.refs_3_.refs_4_ = bf16[512,512]{1,0:T(8,128)(2,1)S(1)} collective-permute-done((bf16[512,512]{1,0:T(8,128)(2,1)}, bf16[512,512]{1,0:T(8,128)(2,1)S(1)}, u32[]{:S(2)}, u32[]{:S(2)}) %collective-permute-start.3) | collective-permute-done | bytes 524320 | tf_op jit(solution)/shard_map/ppermute | solution.py:240
  51.4 2.6 %shard_map.87 = (bf16[8,2,256,256]{3,2,1,0:T(8,128)(2,1)S(1)}, bf16[8,256,256]{2,1,0:T(8,128)(2,1)S(1)}, f32[256,1024]{1,0:T(8,128)S(1)}, f32[256,1024]{1,0:T(8,128)S(1)}, f32[8,256]{1,0:T(8,128)S(1)}) custom-call(bf16[512,1024]{1,0:T(8,128)(2,1)S(1)} %copy-done.2, ...), custom_call_target="tpu_custom_call", output_to_operand_aliasing={{0}: (4, {}), {1}: (5, {}), {2}: (6, {}), {3}: (7, {})} | custom-call | flops 1342177280 | bytes 2097152 | tf_op jit(solution)/shard_map/pallas_call | solution.py:69
  54.0 2.5 %shard_map.91 = (f32[512,1024]{1,0:T(8,128)S(1)}, f32[8,512]{1,0:T(8,128)S(1)}) custom-call(bf16[512,1024]{1,0:T(8,128)(2,1)S(1)} %copy-done.2, f32[256,1024]{1,0:T(8,128)S(1)} %get-tuple-element.72.refs_1_, f32[256,1024]{1,0:T(8,128)S(1)} %get-tuple-element.78.refs_2_, bf16[1,1024]{1,0:T(2,128)(2,1)S(1)} %reshape.11.refs_3_.refs_2_, ...), custom_call_target="tpu_custom_call" | custom-call | flops 134217728 | bytes 6291456 | tf_op jit(solution)/shard_map/pallas_call | solution.py:69
  56.6 1.2 %collective-permute-done.11 = f32[8,512]{1,0:T(8,128)S(1)} collective-permute-done((f32[8,512]{1,0:T(8,128)S(1)}, f32[8,512]{1,0:T(8,128)S(1)}, u32[]{:S(2)}, u32[]{:S(2)}) %collective-permute-start.11) | collective-permute-done | bytes 16416 | tf_op jit(solution)/shard_map/ppermute | solution.py:734
  57.8 3.8 %shard_map.92 = (bf16[512,1024]{1,0:T(8,128)(2,1)}, bf16[512,1024]{1,0:T(8,128)(2,1)S(1)}, bf16[272,1024]{1,0:T(8,128)(2,1)S(1)}, bf16[384,128]{1,0:T(8,128)(2,1...) custom-call(f32[8,512]{1,0:T(8,128)S(1)} %add.3.refs_0_, ...), custom_call_target="tpu_custom_call" | custom-call | flops 134217728 | bytes 7340032 | tf_op jit(solution)/shard_map/pallas_call | solution.py:69
  61.6 2.4 %collective-permute-start.12 = (bf16[384,128]{1,0:T(8,128)(2,1)S(1)}, bf16[384,128]{1,0:T(8,128)(2,1)S(1)}, u32[]{:S(2)}, u32[]{:S(2)}) collective-permute-start(bf16[384,128]{1,0:T(8,128)(2,1)S(1)} %get-tuple-element.94), channel_id=1, source_target_pairs={{0,2},{2,0},{4,6},{6,4},{8,10},{10,8},{12,14},{14,12},{16,18},{18,... | collective-permute-start | bytes 294920 | tf_op jit(solution)/shard_map/ppermute | solution.py:235
  63.9 1.1 %collective-permute-start.13 = (bf16[384,128]{1,0:T(8,128)(2,1)S(1)}, bf16[384,128]{1,0:T(8,128)(2,1)S(1)}, u32[]{:S(2)}, u32[]{:S(2)}) collective-permute-start(bf16[384,128]{1,0:T(8,128)(2,1)S(1)} %get-tuple-element.95), channel_id=1, source_target_pairs={{0,4},{2,6},{4,0},{6,2},{8,12},{10,14},{12,8},{14,10},{16,20},{18,... | collective-permute-start | bytes 294920 | tf_op jit(solution)/shard_map/ppermute | solution.py:235
  65.4 4.5 %shard_map.93 = (bf16[512,1024]{1,0:T(8,128)(2,1)}, f32[512,512]{1,0:T(8,128)S(1)}, f32[512,512]{1,0:T(8,128)S(1)}) custom-call(bf16[512,1024]{1,0:T(8,128)(2,1)S(1)} %copy-done.2, bf16[512,1024]{1,0:T(8,128)(2,1)S(1)} %copy-done, bf16[512,1024]{1,0:T(8,128)(2,1)S(1)} %copy-done.1, bf16[512,1024]{1,0:T(8,128)(2,1)S(1)} %get-tuple-element.87.refs_3_, ...), custom_call_target="tpu_custom_call" | custom-call | flops 2147483648 | bytes 10485760 | tf_op jit(solution)/shard_map/pallas_call | solution.py:69
  70.7 4.9 %collective-permute-start.19 = (bf16[272,1024]{1,0:T(8,128)(2,1)S(1)}, bf16[272,1024]{1,0:T(8,128)(2,1)S(1)}, u32[]{:S(2)}, u32[]{:S(2)}) collective-permute-start(bf16[272,1024]{1,0:T(8,128)(2,1)S(1)} %get-tuple-element.105), channel_id=1, source_target_pairs={{0,30},{2,0},{4,2},{6,4},{8,6},{10,8},{12,10},{14,12},{16,14},{18,... | collective-permute-start | bytes 1671176 | tf_op jit(solution)/shard_map/ppermute | solution.py:240
  78.2 6.5 %collective-permute-start.20 = (bf16[384,128]{1,0:T(8,128)(2,1)S(1)}, bf16[384,128]{1,0:T(8,128)(2,1)S(1)}, u32[]{:S(2)}, u32[]{:S(2)}) collective-permute-start(bf16[384,128]{1,0:T(8,128)(2,1)S(1)} %get-tuple-element.106), channel_id=1, source_target_pairs={{0,2},{2,0},{4,6},{6,4},{8,10},{10,8},{12,14},{14,12},{16,18},{18,... | collective-permute-start | bytes 294920 | tf_op jit(solution)/shard_map/ppermute | solution.py:235
  84.7 1.2 %collective-permute-start.21 = (bf16[384,128]{1,0:T(8,128)(2,1)S(1)}, bf16[384,128]{1,0:T(8,128)(2,1)S(1)}, u32[]{:S(2)}, u32[]{:S(2)}) collective-permute-start(bf16[384,128]{1,0:T(8,128)(2,1)S(1)} %get-tuple-element.107), channel_id=1, source_target_pairs={{0,4},{2,6},{4,0},{6,2},{8,12},{10,14},{12,8},{14,10},{16,20},{18,... | collective-permute-start | bytes 294920 | tf_op jit(solution)/shard_map/ppermute | solution.py:235
  85.9 1.4 %collective-permute-start.22 = (bf16[384,128]{1,0:T(8,128)(2,1)S(1)}, bf16[384,128]{1,0:T(8,128)(2,1)S(1)}, u32[]{:S(2)}, u32[]{:S(2)}) collective-permute-start(bf16[384,128]{1,0:T(8,128)(2,1)S(1)} %get-tuple-element.108), channel_id=1, source_target_pairs={{0,6},{2,4},{4,2},{6,0},{8,14},{10,12},{12,10},{14,8},{16,22},{18,... | collective-permute-start | bytes 294920 | tf_op jit(solution)/shard_map/ppermute | solution.py:235
  87.3 4.5 %shard_map.96 = (bf16[512,1024]{1,0:T(8,128)(2,1)}, f32[512,512]{1,0:T(8,128)S(1)}, f32[512,512]{1,0:T(8,128)S(1)}) custom-call(bf16[512,1024]{1,0:T(8,128)(2,1)S(1)} %copy-done.2, bf16[512,1024]{1,0:T(8,128)(2,1)S(1)} %copy-done, bf16[512,1024]{1,0:T(8,128)(2,1)S(1)} %copy-done.1, ...), custom_call_target="tpu_custom_call", output_to_operand_aliasing={{0}: (13, {})} | custom-call | flops 2147483648 | bytes 10485760 | tf_op jit(solution)/shard_map/pallas_call | solution.py:69
  91.9 2.5 %shard_map.97 = (bf16[512,1024]{1,0:T(8,128)(2,1)}, bf16[512,1024]{1,0:T(8,128)(2,1)}) custom-call(bf16[512,1024]{1,0:T(8,128)(2,1)S(1)} %copy-done, bf16[512,1024]{1,0:T(8,128)(2,1)S(1)} %copy-done.1, f32[512,512]{1,0:T(8,128)S(1)} %get-tuple-element.99.refs_6_.refs_2_, f32[512,512]{1,0:T(8,128)S(1)} %get-tuple-element.109.refs_3_, ...), custom_call_target="tpu_custom_call" | custom-call | flops 536870912 | bytes 4718592 | tf_op jit(solution)/shard_map/pallas_call | solution.py:69
  94.4 2.5 %shard_map.98 = (bf16[512,1024]{1,0:T(8,128)(2,1)}, bf16[512,1024]{1,0:T(8,128)(2,1)}) custom-call(bf16[512,1024]{1,0:T(8,128)(2,1)S(1)} %copy-done, bf16[512,1024]{1,0:T(8,128)(2,1)S(1)} %copy-done.1, f32[512,512]{1,0:T(8,128)S(1)} %get-tuple-element.103.refs_2_, ...), custom_call_target="tpu_custom_call", output_to_operand_aliasing={{0}: (11, {}), {1}: (12, {})} | custom-call | flops 536870912 | bytes 4718592 | tf_op jit(solution)/shard_map/pallas_call | solution.py:69
  (44 shorter events, 6.9 us)
Async XLA Ops:
  0.6 26.6 %copy-start.5 = (bf16[1024]{0:T(1024)(128)(2,1)S(1)}, bf16[1024]{0:T(1024)(128)(2,1)}, u32[]{:S(2)}) copy-start(bf16[1024]{0:T(1024)(128)(2,1)} %param.8) | copy-start | bytes 6148
  0.6 26.6 %copy-start.2 = (bf16[512,1024]{1,0:T(8,128)(2,1)S(1)}, bf16[512,1024]{1,0:T(8,128)(2,1)}, u32[]{:S(2)}) copy-start(bf16[512,1024]{1,0:T(8,128)(2,1)} %refs_0_.17) | copy-start | bytes 3145732
  4.3 30.1 %copy-start = (bf16[512,1024]{1,0:T(8,128)(2,1)S(1)}, bf16[512,1024]{1,0:T(8,128)(2,1)}, u32[]{:S(2)}) copy-start(bf16[512,1024]{1,0:T(8,128)(2,1)} %refs_0_.19) | copy-start | bytes 3145732
  4.3 30.1 %copy-start.1 = (bf16[512,1024]{1,0:T(8,128)(2,1)S(1)}, bf16[512,1024]{1,0:T(8,128)(2,1)}, u32[]{:S(2)}) copy-start(bf16[512,1024]{1,0:T(8,128)(2,1)} %refs_1_.17) | copy-start | bytes 3145732
  4.3 6.4 %collective-permute-start = (bf16[384,128]{1,0:T(8,128)(2,1)}, bf16[384,128]{1,0:T(8,128)(2,1)S(1)}, u32[]{:S(2)}, u32[]{:S(2)}) collective-permute-start(bf16[384,128]{1,0:T(8,128)(2,1)} %get-tuple-element.60), channel_id=1, source_target_pairs={{0,2},{2,0},{4,6},{6,4},{8,10},{10,8},{12,14},{14,12},{16,18},{18,... | collective-permute-start | bytes 294920 | tf_op jit(solution)/shard_map/ppermute | solution.py:235
  7.3 5.9 %collective-permute-start.1 = (bf16[384,128]{1,0:T(8,128)(2,1)}, bf16[384,128]{1,0:T(8,128)(2,1)S(1)}, u32[]{:S(2)}, u32[]{:S(2)}) collective-permute-start(bf16[384,128]{1,0:T(8,128)(2,1)} %get-tuple-element.61), channel_id=1, source_target_pairs={{0,4},{2,6},{4,0},{6,2},{8,12},{10,14},{12,8},{14,10},{16,20},{18,... | collective-permute-start | bytes 294920 | tf_op jit(solution)/shard_map/ppermute | solution.py:235
  8.8 5.7 %collective-permute-start.2 = (bf16[384,128]{1,0:T(8,128)(2,1)}, bf16[384,128]{1,0:T(8,128)(2,1)S(1)}, u32[]{:S(2)}, u32[]{:S(2)}) collective-permute-start(bf16[384,128]{1,0:T(8,128)(2,1)} %get-tuple-element.62), channel_id=1, source_target_pairs={{0,6},{2,4},{4,2},{6,0},{8,14},{10,12},{12,10},{14,8},{16,22},{18,... | collective-permute-start | bytes 294920 | tf_op jit(solution)/shard_map/ppermute | solution.py:235
  14.5 0.9 copy-start.4
  15.5 18.9 %collective-permute-start.4 = (bf16[512,512]{1,0:T(8,128)(2,1)}, bf16[512,512]{1,0:T(8,128)(2,1)S(1)}, u32[]{:S(2)}, u32[]{:S(2)}) collective-permute-start(bf16[512,512]{1,0:T(8,128)(2,1)} %get-tuple-element.66), channel_id=1, source_target_pairs={{0,2},{2,4},{4,6},{6,8},{8,10},{10,12},{12,14},{14,16},{16,18},{18... | collective-permute-start | bytes 1572872 | tf_op jit(solution)/shard_map/ppermute | solution.py:240
  16.2 35.2 %collective-permute-start.3 = (bf16[512,512]{1,0:T(8,128)(2,1)}, bf16[512,512]{1,0:T(8,128)(2,1)S(1)}, u32[]{:S(2)}, u32[]{:S(2)}) collective-permute-start(bf16[512,512]{1,0:T(8,128)(2,1)} %get-tuple-element.65), channel_id=1, source_target_pairs={{0,2},{2,4},{4,6},{6,8},{8,10},{10,12},{12,14},{14,16},{16,18},{18... | collective-permute-start | bytes 1572872 | tf_op jit(solution)/shard_map/ppermute | solution.py:240
  17.9 9.4 %collective-permute-start.7 = (bf16[384,128]{1,0:T(8,128)(2,1)S(1)}, bf16[384,128]{1,0:T(8,128)(2,1)S(1)}, u32[]{:S(2)}, u32[]{:S(2)}) collective-permute-start(bf16[384,128]{1,0:T(8,128)(2,1)S(1)} %get-tuple-element.73), channel_id=1, source_target_pairs={{0,24},{2,26},{4,28},{1,25},{3,27},{5,29}} | collective-permute-start | bytes 294920 | tf_op jit(solution)/shard_map/ppermute | solution.py:245
  23.4 4.0 %collective-permute-start.6 = (bf16[384,128]{1,0:T(8,128)(2,1)S(1)}, bf16[384,128]{1,0:T(8,128)(2,1)S(1)}, u32[]{:S(2)}, u32[]{:S(2)}) collective-permute-start(bf16[384,128]{1,0:T(8,128)(2,1)S(1)} %get-tuple-element.73), channel_id=1, source_target_pairs={{0,16},{2,18},{4,20},{8,24},{10,26},{12,28},{1,17},{3,19},{5,21},{... | collective-permute-start | bytes 294920 | tf_op jit(solution)/shard_map/ppermute | solution.py:245
  24.7 4.7 %collective-permute-start.5 = (bf16[384,128]{1,0:T(8,128)(2,1)S(1)}, bf16[384,128]{1,0:T(8,128)(2,1)S(1)}, u32[]{:S(2)}, u32[]{:S(2)}) collective-permute-start(bf16[384,128]{1,0:T(8,128)(2,1)S(1)} %get-tuple-element.73), channel_id=1, source_target_pairs={{0,8},{2,10},{4,12},{8,16},{10,18},{12,20},{16,24},{18,26},{20,28}... | collective-permute-start | bytes 294920 | tf_op jit(solution)/shard_map/ppermute | solution.py:245
  29.7 24.3 %collective-permute-start.8 = (bf16[384,128]{1,0:T(8,128)(2,1)S(1)}, bf16[384,128]{1,0:T(8,128)(2,1)S(1)}, u32[]{:S(2)}, u32[]{:S(2)}) collective-permute-start(bf16[384,128]{1,0:T(8,128)(2,1)S(1)} %get-tuple-element.79), channel_id=1, source_target_pairs={{0,2},{2,0},{4,6},{6,4},{8,10},{10,8},{12,14},{14,12},{16,18},{18,... | collective-permute-start | bytes 294920 | tf_op jit(solution)/shard_map/ppermute | solution.py:235
  30.5 23.5 %collective-permute-start.9 = (bf16[384,128]{1,0:T(8,128)(2,1)S(1)}, bf16[384,128]{1,0:T(8,128)(2,1)S(1)}, u32[]{:S(2)}, u32[]{:S(2)}) collective-permute-start(bf16[384,128]{1,0:T(8,128)(2,1)S(1)} %get-tuple-element.80), channel_id=1, source_target_pairs={{0,4},{2,6},{4,0},{6,2},{8,12},{10,14},{12,8},{14,10},{16,20},{18,... | collective-permute-start | bytes 294920 | tf_op jit(solution)/shard_map/ppermute | solution.py:235
  30.6 23.4 %collective-permute-start.10 = (bf16[384,128]{1,0:T(8,128)(2,1)S(1)}, bf16[384,128]{1,0:T(8,128)(2,1)S(1)}, u32[]{:S(2)}, u32[]{:S(2)}) collective-permute-start(bf16[384,128]{1,0:T(8,128)(2,1)S(1)} %get-tuple-element.81), channel_id=1, source_target_pairs={{0,6},{2,4},{4,2},{6,0},{8,14},{10,12},{12,10},{14,8},{16,22},{18,... | collective-permute-start | bytes 294920 | tf_op jit(solution)/shard_map/ppermute | solution.py:235
  37.0 33.7 %collective-permute-start.15 = (bf16[256,1024]{1,0:T(8,128)(2,1)S(1)}, bf16[256,1024]{1,0:T(8,128)(2,1)S(1)}, u32[]{:S(2)}, u32[]{:S(2)}) collective-permute-start(bf16[256,1024]{1,0:T(8,128)(2,1)S(1)} %get-tuple-element.98), channel_id=1, source_target_pairs={{0,30},{2,0},{4,2},{6,4},{8,6},{10,8},{12,10},{14,12},{16,14},{18,... | collective-permute-start | bytes 1572872 | tf_op jit(solution)/shard_map/ppermute | solution.py:240
  51.4 2.7 %copy-start.3 = (bf16[512,1024]{1,0:T(8,128)(2,1)S(1)}, bf16[512,1024]{1,0:T(8,128)(2,1)}, u32[]{:S(2)}) copy-start(bf16[512,1024]{1,0:T(8,128)(2,1)} %refs_3_.1) | copy-start | bytes 3145732
  56.5 1.2 %collective-permute-start.11 = (f32[8,512]{1,0:T(8,128)S(1)}, f32[8,512]{1,0:T(8,128)S(1)}, u32[]{:S(2)}, u32[]{:S(2)}) collective-permute-start(f32[8,512]{1,0:T(8,128)S(1)} %get-tuple-element.82), channel_id=1, source_target_pairs={{0,1},{1,0},{2,3},{3,2},{4,5},{5,4},{6,7},{7,6},{8,9},{9,8},{10,11... | collective-permute-start | bytes 49160 | tf_op jit(solution)/shard_map/ppermute | solution.py:734
  61.6 8.4 %collective-permute-start.12 = (bf16[384,128]{1,0:T(8,128)(2,1)S(1)}, bf16[384,128]{1,0:T(8,128)(2,1)S(1)}, u32[]{:S(2)}, u32[]{:S(2)}) collective-permute-start(bf16[384,128]{1,0:T(8,128)(2,1)S(1)} %get-tuple-element.94), channel_id=1, source_target_pairs={{0,2},{2,0},{4,6},{6,4},{8,10},{10,8},{12,14},{14,12},{16,18},{18,... | collective-permute-start | bytes 294920 | tf_op jit(solution)/shard_map/ppermute | solution.py:235
  63.9 6.7 %collective-permute-start.13 = (bf16[384,128]{1,0:T(8,128)(2,1)S(1)}, bf16[384,128]{1,0:T(8,128)(2,1)S(1)}, u32[]{:S(2)}, u32[]{:S(2)}) collective-permute-start(bf16[384,128]{1,0:T(8,128)(2,1)S(1)} %get-tuple-element.95), channel_id=1, source_target_pairs={{0,4},{2,6},{4,0},{6,2},{8,12},{10,14},{12,8},{14,10},{16,20},{18,... | collective-permute-start | bytes 294920 | tf_op jit(solution)/shard_map/ppermute | solution.py:235
  65.0 5.7 %collective-permute-start.14 = (bf16[384,128]{1,0:T(8,128)(2,1)S(1)}, bf16[384,128]{1,0:T(8,128)(2,1)S(1)}, u32[]{:S(2)}, u32[]{:S(2)}) collective-permute-start(bf16[384,128]{1,0:T(8,128)(2,1)S(1)} %get-tuple-element.96), channel_id=1, source_target_pairs={{0,6},{2,4},{4,2},{6,0},{8,14},{10,12},{12,10},{14,8},{16,22},{18,... | collective-permute-start | bytes 294920 | tf_op jit(solution)/shard_map/ppermute | solution.py:235
  70.7 21.2 %collective-permute-start.19 = (bf16[272,1024]{1,0:T(8,128)(2,1)S(1)}, bf16[272,1024]{1,0:T(8,128)(2,1)S(1)}, u32[]{:S(2)}, u32[]{:S(2)}) collective-permute-start(bf16[272,1024]{1,0:T(8,128)(2,1)S(1)} %get-tuple-element.105), channel_id=1, source_target_pairs={{0,30},{2,0},{4,2},{6,4},{8,6},{10,8},{12,10},{14,12},{16,14},{18,... | collective-permute-start | bytes 1671176 | tf_op jit(solution)/shard_map/ppermute | solution.py:240
  75.6 2.2 %collective-permute-start.18 = (bf16[384,128]{1,0:T(8,128)(2,1)S(1)}, bf16[384,128]{1,0:T(8,128)(2,1)S(1)}, u32[]{:S(2)}, u32[]{:S(2)}) collective-permute-start(bf16[384,128]{1,0:T(8,128)(2,1)S(1)} %get-tuple-element.100), channel_id=1, source_target_pairs={{26,2},{28,4},{30,6},{27,3},{29,5},{31,7}} | collective-permute-start | bytes 294920 | tf_op jit(solution)/shard_map/ppermute | solution.py:245
  76.3 1.5 %collective-permute-start.17 = (bf16[384,128]{1,0:T(8,128)(2,1)S(1)}, bf16[384,128]{1,0:T(8,128)(2,1)S(1)}, u32[]{:S(2)}, u32[]{:S(2)}) collective-permute-start(bf16[384,128]{1,0:T(8,128)(2,1)S(1)} %get-tuple-element.100), channel_id=1, source_target_pairs={{18,2},{20,4},{22,6},{26,10},{28,12},{30,14},{19,3},{21,5},{23,7},... | collective-permute-start | bytes 294920 | tf_op jit(solution)/shard_map/ppermute | solution.py:245
  77.0 0.9 collective-permute-start.16
  78.2 13.7 %collective-permute-start.20 = (bf16[384,128]{1,0:T(8,128)(2,1)S(1)}, bf16[384,128]{1,0:T(8,128)(2,1)S(1)}, u32[]{:S(2)}, u32[]{:S(2)}) collective-permute-start(bf16[384,128]{1,0:T(8,128)(2,1)S(1)} %get-tuple-element.106), channel_id=1, source_target_pairs={{0,2},{2,0},{4,6},{6,4},{8,10},{10,8},{12,14},{14,12},{16,18},{18,... | collective-permute-start | bytes 294920 | tf_op jit(solution)/shard_map/ppermute | solution.py:235
  84.7 7.2 %collective-permute-start.21 = (bf16[384,128]{1,0:T(8,128)(2,1)S(1)}, bf16[384,128]{1,0:T(8,128)(2,1)S(1)}, u32[]{:S(2)}, u32[]{:S(2)}) collective-permute-start(bf16[384,128]{1,0:T(8,128)(2,1)S(1)} %get-tuple-element.107), channel_id=1, source_target_pairs={{0,4},{2,6},{4,0},{6,2},{8,12},{10,14},{12,8},{14,10},{16,20},{18,... | collective-permute-start | bytes 294920 | tf_op jit(solution)/shard_map/ppermute | solution.py:235
  85.9 6.0 %collective-permute-start.22 = (bf16[384,128]{1,0:T(8,128)(2,1)S(1)}, bf16[384,128]{1,0:T(8,128)(2,1)S(1)}, u32[]{:S(2)}, u32[]{:S(2)}) collective-permute-start(bf16[384,128]{1,0:T(8,128)(2,1)S(1)} %get-tuple-element.108), channel_id=1, source_target_pairs={{0,6},{2,4},{4,2},{6,0},{8,14},{10,12},{12,10},{14,8},{16,22},{18,... | collective-permute-start | bytes 294920 | tf_op jit(solution)/shard_map/ppermute | solution.py:235

commit v3 on v2

v3 whole, which is shorter than its diff:
```python
import math

import jax
import jax.numpy as jnp
from jax import lax
from jax.experimental import pallas as pl
from jax.experimental.pallas import tpu as pltpu
from jax.sharding import PartitionSpec as P

HEAD_DIM = 128
WINDOW = 256
GROUP = 4
HOLDERS = 3
STATS = 8
AHEAD = 192
EPSILON = 1e-06
SCALE = 1.0 / math.sqrt(HEAD_DIM)
SCALE_LOG2 = SCALE * math.log2(math.e)
LN2 = math.log(2.0)
MASKED = -1e30
BF16 = jnp.bfloat16
F32 = jnp.float32
VMEM_LIMIT = 24 * 1024 * 1024
VMEM_MOST = 60 * 1024 * 1024


def dot_nn(left, right):
    return lax.dot_general(left, right, (((1,), (0,)), ((), ())), preferred_element_type=F32)


def dot_nt(left, right):
    return lax.dot_general(left, right, (((1,), (1,)), ((), ())), preferred_element_type=F32)


def dot_tn(left, right):
    return lax.dot_general(left, right, (((0,), (0,)), ((), ())), preferred_element_type=F32)


def tile_iotas():
    keys_at = lax.broadcasted_iota(jnp.int32, (WINDOW, WINDOW), 0)
    queries_at = lax.broadcasted_iota(jnp.int32, (WINDOW, WINDOW), 1)
    return keys_at, queries_at


def coef_row(start, count):
    at = start + lax.broadcasted_iota(jnp.int32, (1, count), 1)
    return 1.0 / jnp.sqrt(HEAD_DIM * (at + 1).astype(F32))


def coef_column(start, count):
    at = start + lax.broadcasted_iota(jnp.int32, (count, HEAD_DIM), 0)
    return 1.0 / jnp.sqrt(HEAD_DIM * (at + 1).astype(F32))


def heads_a_step(heads):
    return 2 if heads % 2 == 0 else 1


def sent_chunks(heads):
    return [(0, 2), (2, heads - 2)] if heads > 2 else [(0, heads)]


def even_chunks(heads):
    return [(0, heads // 2), (heads // 2, heads - heads // 2)] if heads > 1 else [(0, 1)]


def picked(chunks, refs, head):
    for (first, count), ref in zip(chunks, refs):
        if first <= head < first + count:
            return ref, head - first
    raise ValueError


def columns_of(head):
    return slice(head * HEAD_DIM, (head + 1) * HEAD_DIM)


def call(body, grid, in_specs, out_specs, out_shape, scratch, flops, moved, operands, aliases=None, along=(), after=(), vmem=VMEM_LIMIT):
    inputs, results, handed, skipped = len(operands), len(out_shape), len(along), len(after)

    def run(*refs):
        outs = inputs + handed + skipped
        body(*refs[:inputs], *refs[outs : outs + results], *refs[outs + results + handed :])

    given = pl.pallas_call(
        run,
        grid=grid,
        input_output_aliases={**(aliases or {}), **{inputs + at: results + at for at in range(handed)}},
        in_specs=list(in_specs) + [ANY] * (handed + skipped),
        out_specs=list(out_specs) + [ANY] * handed,
        out_shape=list(out_shape) + [jax.ShapeDtypeStruct(array.shape, array.dtype) for array in along],
        scratch_shapes=scratch,
        compiler_params=pltpu.CompilerParams(
            vmem_limit_bytes=vmem,
            dimension_semantics=("arbitrary",) * len(grid),
        ),
        cost_estimate=pl.CostEstimate(flops=flops, bytes_accessed=moved, transcendentals=0),
    )(*operands, *along, *after)
    return list(given[:results]), list(given[results:])


def run_once(body, operands, results, scratch, flops, moved, along=(), after=(), pushed=()):
    return call(
        body,
        (1,),
        [whole(array.shape) for array in operands],
        [HBM if at in pushed else whole(shape) for at, (shape, _) in enumerate(results)],
        [jax.ShapeDtypeStruct(shape, kind) for shape, kind in results],
        scratch,
        flops,
        moved,
        operands,
        None,
        along,
        after,
    )


def push(held, out, done, head, copies):
    step = heads_a_step(held.shape[1] // HEAD_DIM)
    if head % step == step - 1:
        cols = pl.ds((head + 1 - step) * HEAD_DIM, step * HEAD_DIM)
        copy = pltpu.make_async_copy(held.at[:, cols], out.at[:, cols], done.at[head // step])
        copy.start()
        copies.append(copy)


ANY = pl.BlockSpec(memory_space=pl.ANY)
HBM = pl.BlockSpec(memory_space=pltpu.HBM)


def whole(shape):
    return pl.BlockSpec(shape, lambda *_: (0,) * len(shape))


def heads_a_part(heads):
    return -(-heads // HOLDERS)


def part_shape(heads):
    return (heads_a_part(heads) * HEAD_DIM, HEAD_DIM)


def part_at(held, head, reverse):
    each = held.shape[1] // HEAD_DIM
    at = lax.rem(head, each) * HEAD_DIM
    if not isinstance(at, int):
        at = pl.multiple_of(at, HEAD_DIM)
    return head // each + (GROUP - HOLDERS if reverse else 0), pl.ds(at, HEAD_DIM)


def store_state(held, head, state, reverse):
    slot, rows = part_at(held, head, reverse)
    held[slot, rows, :] = state


def held_state(held, head, reverse):
    slot, rows = part_at(held, head, reverse)
    return held[slot, rows, :]


def spread(held, outs):
    place = lax.rem(lax.axis_index("ctx"), GROUP)
    for other in range(GROUP):
        outs[other][...] = held[lax.bitwise_xor(place, jnp.int32(other))]


def collect(ins, held):
    place = lax.rem(lax.axis_index("ctx"), GROUP)
    for other in range(GROUP):
        held[lax.bitwise_xor(place, jnp.int32(other))] = ins[other][...]


def state_body(steps, k_ref, v_ref, *rest):
    outs, tails = rest[:GROUP], rest[GROUP:-4]
    k_held, v_held, held, done = rest[-4:]
    rows, width = k_held.shape
    wide = width // steps
    chunks = sent_chunks(width // HEAD_DIM)
    loads, sends = [], {}
    for step in range(steps):
        cols = pl.ds(step * wide, wide)
        for at, (source, target) in enumerate(((k_ref, k_held), (v_ref, v_held))):
            loads.append(pltpu.make_async_copy(source.at[:, cols], target.at[:, cols], done.at[2 * step + at]))
    for step in range(steps):
        cols = pl.ds(step * wide, wide)
        tail, place = picked(chunks, tails, step * wide // HEAD_DIM)
        sends[step] = [
            pltpu.make_async_copy(
                source.at[pl.ds(rows - WINDOW, WINDOW), cols],
                tail.at[pl.ds(at * WINDOW, WINDOW), pl.ds(place * HEAD_DIM, wide)],
                done.at[2 * (steps + step) + at],
            )
            for at, source in enumerate((k_held, v_held))
        ]
    held[...] = jnp.zeros_like(held)
    for copy in loads:
        copy.start()
    for step in range(steps):
        loads[2 * step].wait()
        loads[2 * step + 1].wait()
        for copy in sends[step]:
            copy.start()
        for head in range(step * wide // HEAD_DIM, (step + 1) * wide // HEAD_DIM):
            cols = slice(head * HEAD_DIM, (head + 1) * HEAD_DIM)
            store_state(held, head, dot_tn(k_held[:, cols], v_held[:, cols]).astype(BF16), False)
    spread(held, outs)
    for step in range(steps):
        for copy in sends[step]:
            copy.wait()


def local_states(keys, values):
    rows, width = keys.shape
    heads = width // HEAD_DIM
    tails = [(2 * WINDOW, count * HEAD_DIM) for _, count in sent_chunks(heads)]
    steps = heads // heads_a_step(heads)
    piece = part_shape(heads)
    results, _ = call(
        lambda *refs: state_body(steps, *refs),
        (1,),
        [HBM] * 2,
        [whole(piece)] * GROUP + [ANY] * len(tails),
        [jax.ShapeDtypeStruct(piece, BF16)] * GROUP + [jax.ShapeDtypeStruct(tail, BF16) for tail in tails],
        [
            pltpu.VMEM((rows, width), BF16),
            pltpu.VMEM((rows, width), BF16),
            pltpu.VMEM((GROUP,) + piece, BF16),
            pltpu.SemaphoreType.DMA((4 * steps,)),
        ],
        2 * rows * width * HEAD_DIM,
        2 * 2 * rows * width,
        [keys, values],
        vmem=VMEM_MOST,
    )
    return results[:GROUP], results[GROUP:]


def total_body(*refs):
    total = refs[0][...].astype(F32)
    for ref in refs[1:-1]:
        total = total + ref[...].astype(F32)
    refs[-1][...] = total.astype(refs[-1].dtype)


def merge_body(reverse, groups, *refs):
    block = lax.axis_index("ctx")
    group = block // GROUP
    place = lax.rem(block, GROUP)
    others = refs[: groups - 1]
    own = refs[groups - 1 : groups - 1 + GROUP]
    outs = refs[groups - 1 + GROUP :]
    total = jnp.zeros(outs[0].shape, F32)
    for step in range(1, groups):
        wanted = group + step < groups if reverse else group - step >= 0
        total = total + others[step - 1][...].astype(F32) * wanted.astype(F32)
    for target in range(GROUP):
        to = lax.bitwise_xor(place, jnp.int32(target))
        result = total
        for source in range(GROUP):
            if source == target:
                continue
            of = lax.bitwise_xor(place, jnp.int32(source))
            wanted = of > to if reverse else of < to
            result = result + own[source][...].astype(F32) * wanted.astype(F32)
        outs[target][...] = result.astype(outs[target].dtype)


def swap(value, mask):
    count = lax.axis_size("ctx")
    return lax.ppermute(value, "ctx", [(at, at ^ mask) for at in range(count)])


def turn(value, steps):
    count = lax.axis_size("ctx")
    return lax.ppermute(value, "ctx", [(at, (at + steps) % count) for at in range(count)])


def shift(value, steps, places):
    count = lax.axis_size("ctx")
    return lax.ppermute(
        value, "ctx", [(at, at + steps) for at in range(count) if at % GROUP in places and 0 <= at + steps < count]
    )


def scan(pieces, reverse, first, second):
    groups = lax.axis_size("ctx") // GROUP
    shape = pieces[0].shape
    full = whole(shape)
    size = shape[0] * shape[1]
    out = jax.ShapeDtypeStruct(shape, BF16)
    own = [pieces[0]] + [swap(pieces[other], other) for other in range(1, GROUP)]
    along, after = first()
    (total,), held = call(
        total_body, (1,), [full] * GROUP, [full], [out], [], GROUP * size, 2 * 5 * size, own, None, along, after
    )
    holders = range(GROUP - HOLDERS, GROUP) if reverse else range(HOLDERS)
    others = [shift(total, (-GROUP if reverse else GROUP) * at, holders) for at in range(1, groups)]
    operands = others + own
    along, after = second(total, held)
    merged, held = call(
        lambda *refs: merge_body(reverse, groups, *refs),
        (1,),
        [full] * len(operands),
        [full] * GROUP,
        [out] * GROUP,
        [],
        20 * size,
        2 * 11 * size,
        operands,
        None,
        along,
        after,
    )
    return [merged[0]] + [swap(merged[other], other) for other in range(1, GROUP)], merged, held


def attend(scores, masks, coef, linear):
    shown = [jnp.where(mask, score, MASKED) for score, mask in zip(scores, masks)]
    peak = jnp.max(shown[0], 0, keepdims=True)
    for tile in shown[1:]:
        peak = jnp.maximum(peak, jnp.max(tile, 0, keepdims=True))
    powers = [jnp.exp2((tile - peak) * SCALE_LOG2) for tile in shown]
    norm = jnp.sum(powers[0], 0, keepdims=True)
    for tile in powers[1:]:
        norm = norm + jnp.sum(tile, 0, keepdims=True)
    share = 1.0 / norm
    probs = [tile * share for tile in powers]
    sums = []
    for prob, score, mask, kind in zip(probs, scores, masks, linear):
        if kind == "none":
            sums.append(None)
        elif kind == "all":
            sums.append((prob + score * coef).astype(BF16))
        else:
            sums.append((prob + jnp.where(mask, score * coef, 0.0)).astype(BF16))
    lse = peak * SCALE + jnp.log(norm)
    return [prob.astype(BF16) for prob in probs], sums, lse


def late_body(first, count, q_ref, k_ref, v_ref, prob_ref, sum_ref, part_ref):
    rows = k_ref.shape[0]
    start = lax.axis_index("ctx") * rows
    keys_at, queries_at = tile_iotas()
    coef = coef_row(start + WINDOW, WINDOW)
    masks = [keys_at > queries_at, keys_at <= queries_at]
    for at in range(count):
        cols = columns_of(first + at)
        query = q_ref[WINDOW : 2 * WINDOW, cols]
        scores = [dot_nt(k_ref[tile * WINDOW : (tile + 1) * WINDOW, cols], query) for tile in range(2)]
        probs, sums, _ = attend(scores, masks, coef, ["all", "masked"])
        total = jnp.zeros((HEAD_DIM, WINDOW), F32)
        for tile in range(2):
            prob_ref[at, tile] = probs[tile]
            sum_ref[at, tile] = sums[tile]
            total = total + dot_tn(v_ref[tile * WINDOW : (tile + 1) * WINDOW, cols], sums[tile])
        part_ref[:, columns_of(at)] = total.T


def late_rows(first, count, queries, keys, values, after):
    tiles = (count, 2, WINDOW, WINDOW)
    wide = count * HEAD_DIM
    return run_once(
        lambda *refs: late_body(first, count, *refs),
        [queries, keys, values],
        [(tiles, BF16), (tiles, BF16), ((WINDOW, wide), F32)],
        [],
        4 * 2 * WINDOW * WINDOW * wide * 4,
        24 * WINDOW * wide,
        after=after,
    )[0]


def early_body(first, count, q_ref, k_ref, v_ref, tail_ref, *rest):
    prob_ref, sum_ref, inside_ref, window_ref, lse_ref = rest[-5:]
    rows = k_ref.shape[0]
    block = lax.axis_index("ctx")
    lse_ref[...] = rest[0][...] if len(rest) > 5 else jnp.zeros_like(lse_ref)
    keys_at, queries_at = tile_iotas()
    beyond = jnp.where(block > 0, 0, 2 * WINDOW)
    masks = [keys_at > queries_at + beyond, keys_at <= queries_at]
    coef = coef_row(block * rows, WINDOW)
    for at in range(count):
        cols, own = columns_of(first + at), columns_of(at)
        query = q_ref[:WINDOW, cols]
        scores = [dot_nt(tail_ref[:WINDOW, own], query), dot_nt(k_ref[:WINDOW, cols], query)]
        probs, sums, lse = attend(scores, masks, coef, ["none", "masked"])
        prob_ref[at, 0] = probs[0]
        prob_ref[at, 1] = probs[1]
        sum_ref[at] = sums[1]
        lse_ref[first + at : first + at + 1, :] = lse
        value = v_ref[:WINDOW, cols]
        before = dot_tn(tail_ref[WINDOW:, own], probs[0])
        window_ref[:, own] = (before + dot_tn(value, probs[1])).T
        inside_ref[:, own] = (before + dot_tn(value, sums[1])).T


def early_rows(first, count, queries, keys, values, before, done, after):
    wide = count * HEAD_DIM
    return run_once(
        lambda *refs: early_body(first, count, *refs),
        [queries, keys, values, before, *done],
        [
            ((count, 2, WINDOW, WINDOW), BF16),
            ((count, WINDOW, WINDOW), BF16),
            ((WINDOW, wide), F32),
            ((WINDOW, wide), F32),
            ((STATS, WINDOW), F32),
        ],
        [],
        5 * 2 * WINDOW * WINDOW * wide * 4,
        24 * WINDOW * wide,
        after=after,
    )[0]


def sum_body(sent, even, q_ref, gain_ref, cot_ref, *rest):
    ins, rest = rest[:GROUP], rest[GROUP:]
    insides, rest = rest[: len(sent)], rest[len(sent) :]
    parts, rest = rest[: len(even)], rest[len(even) :]
    hidden_ref, norm_ref, held, squares, crossed, columns = rest
    rows, width = q_ref.shape
    collect(ins, held)
    columns[...] = coef_column(lax.axis_index("ctx") * rows, rows)
    for head in range(width // HEAD_DIM):
        cols = columns_of(head)
        inside, at = picked(sent, insides, head)
        part, late = picked(even, parts, head)
        carried = columns[...] * dot_nn(q_ref[:, cols], held_state(held, head, False))
        hidden = jnp.concatenate([inside[:, columns_of(at)], part[:, columns_of(late)]], 0) + carried
        hidden_ref[:, cols] = hidden
        scaled = gain_ref[:, cols].astype(F32) * cot_ref[:, cols].astype(F32)
        if head == 0:
            squares[...] = hidden * hidden
            crossed[...] = hidden * scaled
        else:
            squares[...] += hidden * hidden
            crossed[...] += hidden * scaled
    norm_ref[...] = jnp.zeros_like(norm_ref)
    norm_ref[0:1, :] = jnp.sum(squares[...].T, 0, keepdims=True)
    norm_ref[1:2, :] = jnp.sum(crossed[...].T, 0, keepdims=True)


def add_prefix(queries, insides, parts, gain, cotangent, prefix, along):
    rows, width = queries.shape
    heads = width // HEAD_DIM
    return run_once(
        lambda *refs: sum_body(sent_chunks(heads), even_chunks(heads), *refs),
        [queries, gain, cotangent, *prefix, *insides, *parts],
        [((rows, width), F32), ((STATS, rows), F32)],
        [pltpu.VMEM((GROUP,) + prefix[0].shape, BF16)] + [pltpu.VMEM((rows, HEAD_DIM), F32)] * 3,
        2 * rows * width * HEAD_DIM,
        12 * rows * width,
        along,
    )


def stat_rows(width):
    return 2 * STATS * -(-3 * WINDOW // width)


def stat_place(width, part):
    across = width // WINDOW
    return (
        slice(WINDOW + part // across * 2 * STATS, WINDOW + (part // across + 1) * 2 * STATS),
        slice(part % across * WINDOW, (part % across + 1) * WINDOW),
    )


def norm_body(sent, features, norm_ref, hidden_ref, gain_ref, cot_ref, q_ref, lse_ref, *rest):
    windows, rest = rest[: len(sent)], rest[len(sent) :]
    out_ref, grad_ref, first_ref = rest[:3]
    outs = rest[3 : 3 + GROUP]
    held, recip, pull, columns, stats, out_held, done = rest[3 + GROUP :]
    rows, width = q_ref.shape
    root = 1.0 / jnp.sqrt(norm_ref[0:1, :] / features + EPSILON)
    slope = root * root * root * norm_ref[1:2, :] / features
    recip[...] = jnp.broadcast_to(root, (HEAD_DIM, rows)).T
    pull[...] = jnp.broadcast_to(slope, (HEAD_DIM, rows)).T
    columns[...] = coef_column(lax.axis_index("ctx") * rows, rows)
    stats[...] = jnp.zeros_like(stats)
    stats[:STATS, :] = lse_ref[...]
    held[...] = jnp.zeros_like(held)
    copies = []
    for head in range(width // HEAD_DIM):
        cols = columns_of(head)
        hidden = hidden_ref[:, cols]
        gain = gain_ref[:, cols].astype(F32)
        kept = recip[...]
        out_held[:, cols] = (hidden * kept * gain).astype(BF16)
        push(out_held, out_ref, done, head, copies)
        full = kept * (gain * cot_ref[:, cols].astype(F32)) - hidden * pull[...]
        grad = full.astype(BF16)
        grad_ref[:, cols] = grad
        first_ref[:WINDOW, cols] = grad[:WINDOW]
        window, at = picked(sent, windows, head)
        delta = (grad[:WINDOW].astype(F32) * window[:, columns_of(at)]).T
        stats[STATS + head : STATS + head + 1, :] = jnp.sum(delta, 0, keepdims=True)
        state = dot_tn(q_ref[:, cols], (full * columns[...]).astype(BF16)).astype(BF16)
        store_state(held, head, state, True)
    spread(held, outs)
    left = stats[...]
    below = WINDOW + stat_rows(width)
    first_ref[WINDOW:below, :] = jnp.zeros((below - WINDOW, width), BF16)
    first_ref[below:, :] = q_ref[AHEAD:WINDOW, :]
    for part in range(3):
        at_rows, at_cols = stat_place(width, part)
        taken = left.astype(BF16)
        first_ref[at_rows, at_cols] = taken
        left = left - taken.astype(F32)
    for copy in copies:
        copy.wait()


def normalize(norms, hidden, gain, cotangent, queries, windows, lse, features):
    rows, width = queries.shape
    heads = width // HEAD_DIM
    piece = part_shape(heads)
    return run_once(
        lambda *refs: norm_body(sent_chunks(heads), features, *refs),
        [norms, hidden, gain, cotangent, queries, lse, *windows],
        [((rows, width), BF16), ((rows, width), BF16), ((2 * WINDOW - AHEAD + stat_rows(width), width), BF16)] + [(piece, BF16)] * GROUP,
        [pltpu.VMEM((GROUP,) + piece, BF16)]
        + [pltpu.VMEM((rows, HEAD_DIM), F32)] * 3
        + [
            pltpu.VMEM((2 * STATS, WINDOW), F32),
            pltpu.VMEM((rows, width), BF16),
            pltpu.SemaphoreType.DMA((heads // heads_a_step(heads),)),
        ],
        2 * rows * width * HEAD_DIM,
        14 * rows * width,
        pushed=(0,),
    )[0]


def back_body(first, count, sent, even, q_ref, k_ref, v_ref, g_ref, *rest):
    heads = q_ref.shape[1] // HEAD_DIM
    rows = q_ref.shape[0]
    last = first + count == heads
    ins, rest = rest[:GROUP], rest[GROUP:]
    tails, rest = rest[: len(sent)], rest[len(sent) :]
    probs0, rest = rest[: len(sent)], rest[len(sent) :]
    sums0, rest = rest[: len(sent)], rest[len(sent) :]
    probs1, sums1 = rest[0], rest[1]
    made = rest[2:-3] if not last else rest[2:-5]
    if last:
        dk_ref, dv_ref, held, dq_held, done = rest[-5:]
        dq_ref, made = made[-1], made[:-1]
    else:
        dq_held, dk_ref, dv_ref, held = made[-1], *rest[-3:]
        dq_ref, made = None, made[:-1]
    collect(ins, held)
    keys_at, queries_at = tile_iotas()
    causal = keys_at <= queries_at
    start = lax.axis_index("ctx") * rows
    ratios = coef_row(start, rows) * (1.0 / SCALE)
    early, late = slice(0, WINDOW), slice(WINDOW, 2 * WINDOW)
    copies = []
    if last and made:
        dq_held[:, : first * HEAD_DIM] = made[0][...]
        for head in range(first):
            push(dq_held, dq_ref, done, head, copies)
    for at in range(count):
        head = first + at
        cols, own = columns_of(head), columns_of(at)
        before_ref, place = picked(sent, tails, head)
        prob0 = picked(sent, probs0, head)[0]
        sum0 = picked(sent, sums0, head)[0]
        grads = g_ref[early, cols], g_ref[late, cols]
        queries = q_ref[early, cols], q_ref[late, cols]
        keys = before_ref[:WINDOW, columns_of(place)], k_ref[early, cols], k_ref[late, cols]
        values = before_ref[WINDOW:, columns_of(place)], v_ref[early, cols], v_ref[late, cols]
        probs = (
            (prob0[place, 0].astype(F32), prob0[place, 1].astype(F32)),
            (probs1[at, 0].astype(F32), probs1[at, 1].astype(F32)),
        )
        edges = []
        for half in range(2):
            ratio = ratios[:, half * WINDOW : (half + 1) * WINDOW]
            pulls = [dot_nt(values[half + tile], grads[half]) for tile in range(2)]
            delta = jnp.sum(probs[half][0] * pulls[0] + probs[half][1] * pulls[1], 0, keepdims=True)
            before = probs[half][0] * (pulls[0] - delta)
            if half == 1:
                before = before + pulls[0] * ratio
            here = probs[half][1] * (pulls[1] - delta) + jnp.where(causal, pulls[1] * ratio, 0.0)
            edges.append((before.astype(BF16), here.astype(BF16)))
        state = held_state(held, head, False)
        for half, part in enumerate((early, late)):
            inner = dot_tn(keys[half], edges[half][0]) + dot_tn(keys[half + 1], edges[half][1])
            carried = (coef_row(start + half * WINDOW, WINDOW) * (1.0 / SCALE)) * dot_nt(state, grads[half])
            dq_held[part, cols if last else own] = ((inner + carried).T * SCALE).astype(BF16)
        if last:
            push(dq_held, dq_ref, done, head, copies)
        dk_ref[early, own] = SCALE * (dot_nn(edges[0][1], queries[0]) + dot_nn(edges[1][0], queries[1]))
        dk_ref[late, own] = SCALE * dot_nn(edges[1][1], queries[1])
        dv_ref[early, own] = dot_nn(sum0[place], grads[0]) + dot_nn(sums1[at, 0], grads[1])
        dv_ref[late, own] = dot_nn(sums1[at, 1], grads[1])
    for copy in copies:
        copy.wait()


def backward(first, count, queries, keys, values, grads, before, probs0, sums0, probs1, sums1, prefix, made, after):
    rows, width = keys.shape
    heads = width // HEAD_DIM
    last = first + count == heads
    wide = count * HEAD_DIM
    scratch = [pltpu.VMEM((GROUP,) + prefix[0].shape, BF16)]
    if last:
        scratch += [pltpu.VMEM((rows, width), BF16), pltpu.SemaphoreType.DMA((heads // heads_a_step(heads),))]
    return run_once(
        lambda *refs: back_body(first, count, sent_chunks(heads), even_chunks(heads), *refs),
        [queries, keys, values, grads, *prefix, *before, *probs0, *sums0, probs1, sums1, *made],
        [((rows, width if last else wide), BF16), ((rows, wide), F32), ((rows, wide), F32)],
        scratch,
        16 * 2 * WINDOW * WINDOW * wide * 2,
        40 * WINDOW * wide * 2,
        after=after,
        pushed=(0,) if last else (),
    )[0]


def edge_body(last, k_ref, v_ref, qn_ref, sent_ref, dk_ref, dv_ref):
    width = k_ref.shape[1]
    stats = jnp.zeros((2 * STATS, WINDOW), F32)
    for part in range(3):
        at_rows, at_cols = stat_place(width, 2 - part)
        stats = stats + sent_ref[at_rows, at_cols].astype(F32)
    keys_at, queries_at = tile_iotas()
    beyond = jnp.where(lax.axis_index("ctx") < last, 0, 2 * WINDOW)
    mask = keys_at > queries_at + beyond
    late = slice(WINDOW, 2 * WINDOW)
    for head in range(width // HEAD_DIM):
        cols = columns_of(head)
        query = jnp.concatenate([qn_ref[:, cols], sent_ref[WINDOW + stat_rows(width) :, cols]], 0)
        grad = sent_ref[:WINDOW, cols]
        lse = stats[head : head + 1, :] * (1.0 / LN2)
        delta = stats[STATS + head : STATS + head + 1, :]
        scores = dot_nt(k_ref[late, cols], query) * SCALE_LOG2
        probs = jnp.where(mask, jnp.exp2(scores - lse), 0.0)
        edges = probs * (dot_nt(v_ref[late, cols], grad) - delta)
        dk_ref[:, cols] = SCALE * dot_nn(edges.astype(BF16), query)
        dv_ref[:, cols] = dot_nn(probs.astype(BF16), grad)


def edge(keys, values, queries_after, grads_after, after):
    width = keys.shape[1]
    last = lax.axis_size("ctx") - 1
    return run_once(
        lambda *refs: edge_body(last, *refs),
        [keys, values, queries_after, grads_after],
        [((WINDOW, width), F32)] * 2,
        [],
        4 * 2 * WINDOW * WINDOW * width,
        12 * WINDOW * width,
        after=after,
    )[0]


def last_body(even, k_ref, v_ref, ek_ref, ev_ref, *rest):
    ins, rest = rest[:GROUP], rest[GROUP:]
    dk_in, dv_in = rest[: len(even)], rest[len(even) : 2 * len(even)]
    dk_ref, dv_ref, held, dk_held, dv_held, dk_done, dv_done = rest[2 * len(even) :]
    early, late = slice(0, WINDOW), slice(WINDOW, 2 * WINDOW)
    collect(ins, held)
    copies = []
    for head in range(k_ref.shape[1] // HEAD_DIM):
        cols = columns_of(head)
        dk_ref_in, at = picked(even, dk_in, head)
        dv_ref_in = picked(even, dv_in, head)[0]
        state = held_state(held, head, True)
        keys = dk_ref_in[:, columns_of(at)] + dot_nt(v_ref[:, cols], state)
        dk_held[early, cols] = keys[early].astype(BF16)
        dk_held[late, cols] = (keys[late] + ek_ref[:, cols]).astype(BF16)
        push(dk_held, dk_ref, dk_done, head, copies)
        values = dv_ref_in[:, columns_of(at)] + dot_nn(k_ref[:, cols], state)
        dv_held[early, cols] = values[early].astype(BF16)
        dv_held[late, cols] = (values[late] + ev_ref[:, cols]).astype(BF16)
        push(dv_held, dv_ref, dv_done, head, copies)
    for copy in copies:
        copy.wait()


def finish(keys, values, dk_parts, dv_parts, edges, suffix):
    rows, width = keys.shape
    heads = width // HEAD_DIM
    done = pltpu.SemaphoreType.DMA((heads // heads_a_step(heads),))
    return run_once(
        lambda *refs: last_body(even_chunks(heads), *refs),
        [keys, values, *edges, *suffix, *dk_parts, *dv_parts],
        [((rows, width), BF16)] * 2,
        [pltpu.VMEM((GROUP,) + suffix[0].shape, BF16)] + [pltpu.VMEM((rows, width), BF16)] * 2 + [done, done],
        4 * rows * width * HEAD_DIM,
        18 * rows * width,
        pushed=(0, 1),
    )[0]


def summed(value, axis):
    count = lax.axis_size(axis)
    mask = 1
    while mask < count:
        value = value + lax.ppermute(value, axis, [(at, at ^ mask) for at in range(count)])
        mask *= 2
    return value


def on_device(queries, keys, values, gain, cotangent):
    rows, width = queries.shape
    heads = width // HEAD_DIM
    features = width * lax.axis_size("head")
    sent, even = sent_chunks(heads), even_chunks(heads)
    gain = gain.reshape(1, width)
    late, own, grads_after = [], [], []

    pieces, tails = local_states(keys, values)
    before = [turn(tails[0], 1)]

    def first_round():
        late.append(late_rows(*even[0], queries, keys, values, pieces[:1]))
        return tails[1:], [before[0], late[0][2]]

    def second_round(total, held):
        before.extend(turn(tail, 1) for tail in held)
        late.extend(late_rows(*chunk, queries, keys, values, [total]) for chunk in even[1:])
        return [], [late[-1][2]]

    prefix, merged, _ = scan(pieces, False, first_round, second_round)
    early = []
    for chunk, tail in zip(sent, before):
        done = [early[-1][4]] if early else []
        early.append(early_rows(*chunk, queries, keys, values, tail, done, merged[:1]))
    probs0, sums0, insides, windows, lses = zip(*early)
    probs1, sums1, parts = zip(*late)
    (hidden, norms), handed = add_prefix(queries, insides, parts, gain, cotangent, prefix, [queries[:AHEAD]])
    after = turn(handed[0], -1)
    norms = summed(norms, "head")
    output, grads, first, *states = normalize(norms, hidden, gain, cotangent, queries, windows, lses[-1], features)

    def own_chunk(at, after):
        made = [own[0][0]] if own else []
        own.append(
            backward(
                *even[at], queries, keys, values, grads, before, probs0, sums0, probs1[at], sums1[at], prefix, made, after
            )
        )

    def first_back():
        own_chunk(0, [])
        return [first], [after, own[0][1]]

    def second_back(total, held):
        grads_after.append(turn(held[0], -1))
        for at in range(1, len(even)):
            own_chunk(at, [total])
        return [], [own[-1][1]]

    suffix, merged, _ = scan(states, True, first_back, second_back)
    edges = edge(keys, values, after, grads_after[0], merged[:1])
    grad_queries, dk_parts, dv_parts = zip(*own)
    grad_keys, grad_values = finish(keys, values, dk_parts, dv_parts, edges, suffix)
    return output, grad_queries[-1], grad_keys, grad_values


def solution(mesh):
    wide = P("ctx", "head")
    return jax.shard_map(
        on_device,
        mesh=mesh,
        in_specs=(wide, wide, wide, P("head"), wide),
        out_specs=(wide, wide, wide, wide),
        check_vma=False,
    )
```

time: 97.1 us -> 89.4 us (0.921); the launches traced: 96.9 us -> 87.9 us
  Pallas kernels: 35.2 us -> 27.2 us
  starting transfers between devices: 42.2 us -> 35.7 us
  waiting for transfers between devices: 17.7 us -> 21.7 us
  local copies, waits for them, and re-layouts: 0.96 us -> 2.18 us
    pallas_call x15, Pallas kernels: 35.2 us -> 27.2 us  [call(): pl.pallas_call(run, grid=grid, input_output_aliases={**(aliases or {}), *...]
    ppermute x12, starting transfers between devices: 21.1 us -> 15.2 us  [swap(): return lax.ppermute(value, 'ctx', [(at, at ^ mask) for at in range(count)])]
    ppermute x12, waiting for transfers between devices: 6.48 us -> 10.7 us  [swap(): return lax.ppermute(value, 'ctx', [(at, at ^ mask) for at in range(count)])]
    ppermute x6, waiting for transfers between devices: 2.11 us -> 0.12 us  [shift(): lax.ppermute(value, 'ctx', [(at, at + steps) for at in range(count) if at...]
    ppermute x4, waiting for transfers between devices: 7.93 us -> 9.72 us  [turn(): lax.ppermute(value, 'ctx', [(at, (at + steps) % count) for at in range(co...]
    unnamed x12 -> x16, local copies, waits for them, and re-layouts: 0.92 us -> 2.15 us
  transfers between devices with their start and end apart: 23 -> 23, of which waited for: 9 -> 9; matrix products, arithmetic and copies ran while one was open for 0% -> 0% of each run, Pallas kernels for 27% -> 23%
where the time goes in v3:
time: 89.4 us; the launch traced here: 87.9 us
  starting transfers between devices  35.7 us (40%)
  Pallas kernels  27.2 us (30%)
  waiting for transfers between devices  21.7 us (24%)
  local copies, waits for them, and re-layouts  2.18 us (2%)
  between operations  1.12 us (1%)
    pallas_call x15, Pallas kernels, call(): pl.pallas_call(run, grid=grid, input_output_aliases={**(aliases or {}), *...  27.2 us
    ppermute x12, starting transfers between devices, swap(): return lax.ppermute(value, 'ctx', [(at, at ^ mask) for at in range(count)])  15.2 us
    ppermute x6, starting transfers between devices, shift(): lax.ppermute(value, 'ctx', [(at, at + steps) for at in range(count) if at...  11.1 us
    ppermute x12, waiting for transfers between devices, swap(): return lax.ppermute(value, 'ctx', [(at, at ^ mask) for at in range(count)])  10.7 us
    ppermute x4, waiting for transfers between devices, turn(): lax.ppermute(value, 'ctx', [(at, (at + steps) % count) for at in range(co...  9.72 us
    ppermute x4, starting transfers between devices, turn(): lax.ppermute(value, 'ctx', [(at, (at + steps) % count) for at in range(co...  9.4 us
    unnamed x16, local copies, waits for them, and re-layouts  2.15 us
  transfers between devices with their start and end apart: 23, of which 9 were waited for; matrix products, arithmetic and copies ran while one was open for 0% of the time, Pallas kernels for 23%

profile of v3, /device:TPU:0, one launch (start us, length us, event | category | flops | bytes accessed | tf_op | source)
XLA Modules:
  0.0 87.9 jit_solution(18158945639888116519)
XLA Ops:
  0.7 3.7 %shard_map.84 = (bf16[384,128]{1,0:T(8,128)(2,1)}, bf16[384,128]{1,0:T(8,128)(2,1)}, bf16[384,128]{1,0:T(8,128)(2,1)}, bf16[384,128]{1,0:T(8,128)(2,1)}, bf16[51...) custom-call(bf16[512,1024]{1,0:T(8,128)(2,1)} %refs_0_.19, bf16[512,1024]{1,0:T(8,128)(2,1)} %refs_1_.17), custom_call_target="tpu_custom_call" | custom-call | flops 134217728 | bytes 2097152 | tf_op jit(solution)/shard_map/pallas_call | solution.py:85
  4.3 3.0 %collective-permute-start.3 = (bf16[512,256]{1,0:T(8,128)(2,1)}, bf16[512,256]{1,0:T(8,128)(2,1)S(1)}, u32[]{:S(2)}, u32[]{:S(2)}) collective-permute-start(bf16[512,256]{1,0:T(8,128)(2,1)} %get-tuple-element.63), channel_id=1, source_target_pairs={{0,2},{2,4},{4,6},{6,8},{8,10},{10,12},{12,14},{14,16},{16,18},{18... | collective-permute-start | bytes 786440 | tf_op jit(solution)/shard_map/ppermute | solution.py:276
  7.3 1.5 %collective-permute-start = (bf16[384,128]{1,0:T(8,128)(2,1)}, bf16[384,128]{1,0:T(8,128)(2,1)S(1)}, u32[]{:S(2)}, u32[]{:S(2)}) collective-permute-start(bf16[384,128]{1,0:T(8,128)(2,1)} %get-tuple-element.59), channel_id=1, source_target_pairs={{0,2},{2,0},{4,6},{6,4},{8,10},{10,8},{12,14},{14,12},{16,18},{18,... | collective-permute-start | bytes 294920 | tf_op jit(solution)/shard_map/ppermute | solution.py:271
  8.8 1.5 %collective-permute-start.1 = (bf16[384,128]{1,0:T(8,128)(2,1)}, bf16[384,128]{1,0:T(8,128)(2,1)S(1)}, u32[]{:S(2)}, u32[]{:S(2)}) collective-permute-start(bf16[384,128]{1,0:T(8,128)(2,1)} %get-tuple-element.60), channel_id=1, source_target_pairs={{0,4},{2,6},{4,0},{6,2},{8,12},{10,14},{12,8},{14,10},{16,20},{18,... | collective-permute-start | bytes 294920 | tf_op jit(solution)/shard_map/ppermute | solution.py:271
  10.8 1.2 %copy-done.2 = bf16[512,1024]{1,0:T(8,128)(2,1)S(1)} copy-done((bf16[512,1024]{1,0:T(8,128)(2,1)S(1)}, bf16[512,1024]{1,0:T(8,128)(2,1)}, u32[]{:S(2)}) %copy-start.2) | copy-done | bytes 1048600
  12.9 2.1 %shard_map.85 = (bf16[4,2,256,256]{3,2,1,0:T(8,128)(2,1)S(1)}, bf16[4,2,256,256]{3,2,1,0:T(8,128)(2,1)S(1)}, f32[256,512]{1,0:T(8,128)S(1)}) custom-call(bf16[512,1024]{1,0:T(8,128)(2,1)S(1)} %copy-done.2, bf16[512,1024]{1,0:T(8,128)(2,1)S(1)} %copy-done, bf16[512,1024]{1,0:T(8,128)(2,1)S(1)} %copy-done.1, bf16[384,128]{1,0:T(8,128)(2,1)S(1)} %copy-done.6), custom_call_target="tpu_custom_call" | custom-call | flops 1073741824 | bytes 3145728 | tf_op jit(solution)/shard_map/pallas_call | solution.py:85
  15.1 3.2 %collective-permute-done.refs_1_.refs_4_ = bf16[384,128]{1,0:T(8,128)(2,1)S(1)} collective-permute-done((bf16[384,128]{1,0:T(8,128)(2,1)}, bf16[384,128]{1,0:T(8,128)(2,1)S(1)}, u32[]{:S(2)}, u32[]{:S(2)}) %collective-permute-start) | collective-permute-done | bytes 98336 | tf_op jit(solution)/shard_map/ppermute | solution.py:271
  18.2 2.8 %collective-permute-done.1.refs_2_.refs_5_ = bf16[384,128]{1,0:T(8,128)(2,1)S(1)} collective-permute-done((bf16[384,128]{1,0:T(8,128)(2,1)}, bf16[384,128]{1,0:T(8,128)(2,1)S(1)}, u32[]{:S(2)}, u32[]{:S(2)}) %collective-permute-start.1) | collective-permute-done | bytes 98336 | tf_op jit(solution)/shard_map/ppermute | solution.py:271
  21.3 5.1 %collective-permute-start.6 = (bf16[384,128]{1,0:T(8,128)(2,1)S(1)}, bf16[384,128]{1,0:T(8,128)(2,1)S(1)}, u32[]{:S(2)}, u32[]{:S(2)}) collective-permute-start(bf16[384,128]{1,0:T(8,128)(2,1)S(1)} %get-tuple-element.65.refs_3_), channel_id=1, source_target_pairs={{0,24},{2,26},{4,28},{1,25},{3,27},{5,29}} | collective-permute-start | bytes 294920 | tf_op jit(solution)/shard_map/ppermute | solution.py:281
  26.4 1.3 %collective-permute-start.5 = (bf16[384,128]{1,0:T(8,128)(2,1)S(1)}, bf16[384,128]{1,0:T(8,128)(2,1)S(1)}, u32[]{:S(2)}, u32[]{:S(2)}) collective-permute-start(bf16[384,128]{1,0:T(8,128)(2,1)S(1)} %get-tuple-element.65.refs_3_), channel_id=1, source_target_pairs={{0,16},{2,18},{4,20},{8,24},{10,26},{12,28},{1,17},{3,19},{5,21},{... | collective-permute-start | bytes 294920 | tf_op jit(solution)/shard_map/ppermute | solution.py:281
  27.7 2.5 %collective-permute-start.4 = (bf16[384,128]{1,0:T(8,128)(2,1)S(1)}, bf16[384,128]{1,0:T(8,128)(2,1)S(1)}, u32[]{:S(2)}, u32[]{:S(2)}) collective-permute-start(bf16[384,128]{1,0:T(8,128)(2,1)S(1)} %get-tuple-element.65.refs_3_), channel_id=1, source_target_pairs={{0,8},{2,10},{4,12},{8,16},{10,18},{12,20},{16,24},{18,26},{20,28}... | collective-permute-start | bytes 294920 | tf_op jit(solution)/shard_map/ppermute | solution.py:281
  30.2 2.1 %shard_map.87 = (bf16[4,2,256,256]{3,2,1,0:T(8,128)(2,1)S(1)}, bf16[4,2,256,256]{3,2,1,0:T(8,128)(2,1)S(1)}, f32[256,512]{1,0:T(8,128)S(1)}) custom-call(bf16[512,1024]{1,0:T(8,128)(2,1)S(1)} %copy-done.3, bf16[512,1024]{1,0:T(8,128)(2,1)S(1)} %copy-done, bf16[512,1024]{1,0:T(8,128)(2,1)S(1)} %copy-done.1, bf16[384,128]{1,0:T(8,128)(2,1)S(1)} %get-tuple-element.65.refs_3_), custom_call_target="tpu_custom_call" | custom-call | flops 1073741824 | bytes 3145728 | tf_op jit(solution)/shard_map/pallas_call | solution.py:85
  32.8 1.5 %collective-permute-start.7 = (bf16[384,128]{1,0:T(8,128)(2,1)S(1)}, bf16[384,128]{1,0:T(8,128)(2,1)S(1)}, u32[]{:S(2)}, u32[]{:S(2)}) collective-permute-start(bf16[384,128]{1,0:T(8,128)(2,1)S(1)} %get-tuple-element.68), channel_id=1, source_target_pairs={{0,2},{2,0},{4,6},{6,4},{8,10},{10,8},{12,14},{14,12},{16,18},{18,... | collective-permute-start | bytes 294920 | tf_op jit(solution)/shard_map/ppermute | solution.py:271
  34.3 2.1 %collective-permute-start.9 = (bf16[384,128]{1,0:T(8,128)(2,1)S(1)}, bf16[384,128]{1,0:T(8,128)(2,1)S(1)}, u32[]{:S(2)}, u32[]{:S(2)}) collective-permute-start(bf16[384,128]{1,0:T(8,128)(2,1)S(1)} %get-tuple-element.70), channel_id=1, source_target_pairs={{0,6},{2,4},{4,2},{6,0},{8,14},{10,12},{12,10},{14,8},{16,22},{18,... | collective-permute-start | bytes 294920 | tf_op jit(solution)/shard_map/ppermute | solution.py:271
  36.3 1.1 %shard_map.89 = (bf16[2,2,256,256]{3,2,1,0:T(8,128)(2,1)S(1)}, bf16[2,256,256]{2,1,0:T(8,128)(2,1)S(1)}, f32[256,256]{1,0:T(8,128)S(1)}, f32[256,256]{1,0:T(8,128)S(1)}, f32[8,256]{1,0:T(8,128)S(1)}) custom-call(bf16[512,1024]{1,0:T(8,128)(2,1)S(1)} %copy-done.3, bf16[512,1024]{1,0:T(8,128)(2,1)S(1)} %copy-done, bf16[512,1024]{1,0:T(8,128)(2,1)S(1)} %copy-done.1, ...), custom_call_target="tpu_custom_call" | custom-call | flops 671088640 | bytes 1572864 | tf_op jit(solution)/shard_map/pallas_call | solution.py:85
  37.5 6.0 %collective-permute-done.10.refs_3_.refs_9_ = bf16[512,768]{1,0:T(8,128)(2,1)S(1)} collective-permute-done((bf16[512,768]{1,0:T(8,128)(2,1)S(1)}, bf16[512,768]{1,0:T(8,128)(2,1)S(1)}, u32[]{:S(2)}, u32[]{:S(2)}) %collective-permute-start.10) | collective-permute-done | bytes 786464 | tf_op jit(solution)/shard_map/ppermute | solution.py:276
  43.5 2.9 %shard_map.90 = (bf16[6,2,256,256]{3,2,1,0:T(8,128)(2,1)S(1)}, bf16[6,256,256]{2,1,0:T(8,128)(2,1)S(1)}, f32[256,768]{1,0:T(8,128)S(1)}, f32[256,768]{1,0:T(8,128)S(1)}, f32[8,256]{1,0:T(8,128)S(1)}) custom-call(bf16[512,1024]{1,0:T(8,128)(2,1)S(1)} %copy-done.3, bf16[512,1024]{1,0:T(8,128)(2,1)S(1)} %copy-done, bf16[512,1024]{1,0:T(8,128)(2,1)S(1)} %copy-done.1, ...), custom_call_target="tpu_custom_call" | custom-call | flops 2013265920 | bytes 4718592 | tf_op jit(solution)/shard_map/pallas_call | solution.py:85
  46.4 1.2 %collective-permute-done.9.refs_6_.refs_7_ = bf16[384,128]{1,0:T(8,128)(2,1)S(1)} collective-permute-done((bf16[384,128]{1,0:T(8,128)(2,1)S(1)}, bf16[384,128]{1,0:T(8,128)(2,1)S(1)}, u32[]{:S(2)}, u32[]{:S(2)}) %collective-permute-start.9) | collective-permute-done | bytes 98336 | tf_op jit(solution)/shard_map/ppermute | solution.py:271
  47.7 1.0 %shard_map.91 = (f32[512,1024]{1,0:T(8,128)S(1)}, f32[8,512]{1,0:T(8,128)S(1)}, bf16[192,1024]{1,0:T(8,128)(2,1)S(1)}) custom-call(bf16[512,1024]{1,0:T(8,128)(2,1)S(1)} %copy-done.3, bf16[1,1024]{1,0:T(2,128)(2,1)S(1)} %reshape.11.refs_1_.refs_2_, bf16[512,1024]{1,0:T(8,128)(2,1)S(1)} %copy-done.4, ...), custom_call_target="tpu_custom_call", output_to_operand_aliasing={{2}: (11, {})} | custom-call | flops 134217728 | bytes 6291456 | tf_op jit(solution)/shard_map/pallas_call | solution.py:85
  49.6 1.2 %collective-permute-done.11 = f32[8,512]{1,0:T(8,128)S(1)} collective-permute-done((f32[8,512]{1,0:T(8,128)S(1)}, f32[8,512]{1,0:T(8,128)S(1)}, u32[]{:S(2)}, u32[]{:S(2)}) %collective-permute-start.11) | collective-permute-done | bytes 16416 | tf_op jit(solution)/shard_map/ppermute | solution.py:702
  50.8 2.3 %shard_map.92 = (bf16[512,1024]{1,0:T(8,128)(2,1)}, bf16[512,1024]{1,0:T(8,128)(2,1)S(1)}, bf16[336,1024]{1,0:T(8,128)(2,1)S(1)}, bf16[384,128]{1,0:T(8,128)(2,1...) custom-call(f32[8,512]{1,0:T(8,128)S(1)} %add.3.refs_0_, ...), custom_call_target="tpu_custom_call" | custom-call | flops 134217728 | bytes 7340032 | tf_op jit(solution)/shard_map/pallas_call | solution.py:85
  53.0 1.4 %collective-permute-start.12 = (bf16[384,128]{1,0:T(8,128)(2,1)S(1)}, bf16[384,128]{1,0:T(8,128)(2,1)S(1)}, u32[]{:S(2)}, u32[]{:S(2)}) collective-permute-start(bf16[384,128]{1,0:T(8,128)(2,1)S(1)} %get-tuple-element.92), channel_id=1, source_target_pairs={{0,2},{2,0},{4,6},{6,4},{8,10},{10,8},{12,14},{14,12},{16,18},{18,... | collective-permute-start | bytes 294920 | tf_op jit(solution)/shard_map/ppermute | solution.py:271
  54.5 2.1 %collective-permute-start.14 = (bf16[384,128]{1,0:T(8,128)(2,1)S(1)}, bf16[384,128]{1,0:T(8,128)(2,1)S(1)}, u32[]{:S(2)}, u32[]{:S(2)}) collective-permute-start(bf16[384,128]{1,0:T(8,128)(2,1)S(1)} %get-tuple-element.94), channel_id=1, source_target_pairs={{0,6},{2,4},{4,2},{6,0},{8,14},{10,12},{12,10},{14,8},{16,22},{18,... | collective-permute-start | bytes 294920 | tf_op jit(solution)/shard_map/ppermute | solution.py:271
  56.6 3.3 %shard_map.93 = (bf16[512,512]{1,0:T(8,128)(2,1)S(1)}, f32[512,512]{1,0:T(8,128)S(1)}, f32[512,512]{1,0:T(8,128)S(1)}) custom-call(bf16[512,1024]{1,0:T(8,128)(2,1)S(1)} %copy-done.3, bf16[512,1024]{1,0:T(8,128)(2,1)S(1)} %copy-done, bf16[512,1024]{1,0:T(8,128)(2,1)S(1)} %copy-done.1, bf16[512,1024]{1,0:T(8,128)(2,1)S(1)} %get-tuple-element.81.refs_3_, ...), custom_call_target="tpu_custom_call" | custom-call | flops 2147483648 | bytes 10485760 | tf_op jit(solution)/shard_map/pallas_call | solution.py:85
  59.9 3.2 %collective-permute-done.12.refs_1_.refs_4_ = bf16[384,128]{1,0:T(8,128)(2,1)S(1)} collective-permute-done((bf16[384,128]{1,0:T(8,128)(2,1)S(1)}, bf16[384,128]{1,0:T(8,128)(2,1)S(1)}, u32[]{:S(2)}, u32[]{:S(2)}) %collective-permute-start.12) | collective-permute-done | bytes 98336 | tf_op jit(solution)/shard_map/ppermute | solution.py:271
  63.1 5.5 %collective-permute-start.16 = (bf16[336,1024]{1,0:T(8,128)(2,1)S(1)}, bf16[336,1024]{1,0:T(8,128)(2,1)S(1)}, u32[]{:S(2)}, u32[]{:S(2)}) collective-permute-start(bf16[336,1024]{1,0:T(8,128)(2,1)S(1)} %get-tuple-element.100), channel_id=1, source_target_pairs={{0,30},{2,0},{4,2},{6,4},{8,6},{10,8},{12,10},{14,12},{16,14},{18,... | collective-permute-start | bytes 2064392 | tf_op jit(solution)/shard_map/ppermute | solution.py:276
  70.8 4.1 %shard_map.95 = (bf16[512,1024]{1,0:T(8,128)(2,1)}, f32[512,512]{1,0:T(8,128)S(1)}, f32[512,512]{1,0:T(8,128)S(1)}) custom-call(bf16[512,1024]{1,0:T(8,128)(2,1)S(1)} %copy-done.3, bf16[512,1024]{1,0:T(8,128)(2,1)S(1)} %copy-done, bf16[512,1024]{1,0:T(8,128)(2,1)S(1)} %copy-done.1, bf16[512,1024]{1,0:T(8,128)(2,1)S(1)} %get-tuple-element.81.refs_3_, ...), custom_call_target="tpu_custom_call" | custom-call | flops 2147483648 | bytes 10485760 | tf_op jit(solution)/shard_map/pallas_call | solution.py:85
  75.2 2.0 %collective-permute-start.20 = (bf16[384,128]{1,0:T(8,128)(2,1)S(1)}, bf16[384,128]{1,0:T(8,128)(2,1)S(1)}, u32[]{:S(2)}, u32[]{:S(2)}) collective-permute-start(bf16[384,128]{1,0:T(8,128)(2,1)S(1)} %get-tuple-element.105), channel_id=1, source_target_pairs={{0,2},{2,0},{4,6},{6,4},{8,10},{10,8},{12,14},{14,12},{16,18},{18,... | collective-permute-start | bytes 294920 | tf_op jit(solution)/shard_map/ppermute | solution.py:271
  77.2 2.6 %collective-permute-start.21 = (bf16[384,128]{1,0:T(8,128)(2,1)S(1)}, bf16[384,128]{1,0:T(8,128)(2,1)S(1)}, u32[]{:S(2)}, u32[]{:S(2)}) collective-permute-start(bf16[384,128]{1,0:T(8,128)(2,1)S(1)} %get-tuple-element.106), channel_id=1, source_target_pairs={{0,4},{2,6},{4,0},{6,2},{8,12},{10,14},{12,8},{14,10},{16,20},{18,... | collective-permute-start | bytes 294920 | tf_op jit(solution)/shard_map/ppermute | solution.py:271
  79.8 3.7 %collective-permute-done.16.refs_3_ = bf16[336,1024]{1,0:T(8,128)(2,1)S(1)} collective-permute-done((bf16[336,1024]{1,0:T(8,128)(2,1)S(1)}, bf16[336,1024]{1,0:T(8,128)(2,1)S(1)}, u32[]{:S(2)}, u32[]{:S(2)}) %collective-permute-start.16) | collective-permute-done | bytes 688160 | tf_op jit(solution)/shard_map/ppermute | solution.py:276
  83.4 2.0 %shard_map.97 = (f32[256,1024]{1,0:T(8,128)S(1)}, f32[256,1024]{1,0:T(8,128)S(1)}) custom-call(bf16[512,1024]{1,0:T(8,128)(2,1)S(1)} %copy-done, bf16[512,1024]{1,0:T(8,128)(2,1)S(1)} %copy-done.1, bf16[192,1024]{1,0:T(8,128)(2,1)S(1)} %collective-permute-done.15.refs_5_.refs_2_, bf16[336,1024]{1,0:T(8,128)(2,1)S(1)} %collective-permute-done.16.refs_3_, ...), custom_call_target="tpu_custom_call" | custom-call | flops 536870912 | bytes 3145728 | tf_op jit(solution)/shard_map/pallas_call | solution.py:85
  85.8 1.9 %shard_map.98 = (bf16[512,1024]{1,0:T(8,128)(2,1)}, bf16[512,1024]{1,0:T(8,128)(2,1)}) custom-call(bf16[512,1024]{1,0:T(8,128)(2,1)S(1)} %copy-done, bf16[512,1024]{1,0:T(8,128)(2,1)S(1)} %copy-done.1, f32[256,1024]{1,0:T(8,128)S(1)} %get-tuple-element.103.refs_2_, f32[256,1024]{1,0:T(8,128)S(1)} %get-tuple-element.104.refs_3_, ...), custom_call_target="tpu_custom_call" | custom-call | flops 268435456 | bytes 9437184 | tf_op jit(solution)/shard_map/pallas_call | solution.py:85
  (48 shorter events, 5.8 us)
Async XLA Ops:
  0.6 10.2 %copy-start.1 = (bf16[512,1024]{1,0:T(8,128)(2,1)S(1)}, bf16[512,1024]{1,0:T(8,128)(2,1)}, u32[]{:S(2)}) copy-start(bf16[512,1024]{1,0:T(8,128)(2,1)} %refs_1_.17) | copy-start | bytes 3145732
  0.6 10.2 %copy-start = (bf16[512,1024]{1,0:T(8,128)(2,1)S(1)}, bf16[512,1024]{1,0:T(8,128)(2,1)}, u32[]{:S(2)}) copy-start(bf16[512,1024]{1,0:T(8,128)(2,1)} %refs_0_.19) | copy-start | bytes 3145732
  4.3 16.8 %collective-permute-start.3 = (bf16[512,256]{1,0:T(8,128)(2,1)}, bf16[512,256]{1,0:T(8,128)(2,1)S(1)}, u32[]{:S(2)}, u32[]{:S(2)}) collective-permute-start(bf16[512,256]{1,0:T(8,128)(2,1)} %get-tuple-element.63), channel_id=1, source_target_pairs={{0,2},{2,4},{4,6},{6,8},{8,10},{10,12},{12,14},{14,16},{16,18},{18... | collective-permute-start | bytes 786440 | tf_op jit(solution)/shard_map/ppermute | solution.py:276
  7.3 10.9 %collective-permute-start = (bf16[384,128]{1,0:T(8,128)(2,1)}, bf16[384,128]{1,0:T(8,128)(2,1)S(1)}, u32[]{:S(2)}, u32[]{:S(2)}) collective-permute-start(bf16[384,128]{1,0:T(8,128)(2,1)} %get-tuple-element.59), channel_id=1, source_target_pairs={{0,2},{2,0},{4,6},{6,4},{8,10},{10,8},{12,14},{14,12},{16,18},{18,... | collective-permute-start | bytes 294920 | tf_op jit(solution)/shard_map/ppermute | solution.py:271
  8.8 12.3 %collective-permute-start.1 = (bf16[384,128]{1,0:T(8,128)(2,1)}, bf16[384,128]{1,0:T(8,128)(2,1)S(1)}, u32[]{:S(2)}, u32[]{:S(2)}) collective-permute-start(bf16[384,128]{1,0:T(8,128)(2,1)} %get-tuple-element.60), channel_id=1, source_target_pairs={{0,4},{2,6},{4,0},{6,2},{8,12},{10,14},{12,8},{14,10},{16,20},{18,... | collective-permute-start | bytes 294920 | tf_op jit(solution)/shard_map/ppermute | solution.py:271
  10.3 10.8 %collective-permute-start.2 = (bf16[384,128]{1,0:T(8,128)(2,1)}, bf16[384,128]{1,0:T(8,128)(2,1)S(1)}, u32[]{:S(2)}, u32[]{:S(2)}) collective-permute-start(bf16[384,128]{1,0:T(8,128)(2,1)} %get-tuple-element.61), channel_id=1, source_target_pairs={{0,6},{2,4},{4,2},{6,0},{8,14},{10,12},{12,10},{14,8},{16,22},{18,... | collective-permute-start | bytes 294920 | tf_op jit(solution)/shard_map/ppermute | solution.py:271
  10.8 1.2 %copy-start.2 = (bf16[512,1024]{1,0:T(8,128)(2,1)S(1)}, bf16[512,1024]{1,0:T(8,128)(2,1)}, u32[]{:S(2)}) copy-start(bf16[512,1024]{1,0:T(8,128)(2,1)} %refs_0_.17) | copy-start | bytes 3145732
  12.0 0.9 %copy-start.6 = (bf16[384,128]{1,0:T(8,128)(2,1)S(1)}, bf16[384,128]{1,0:T(8,128)(2,1)}, u32[]{:S(2)}) copy-start(bf16[384,128]{1,0:T(8,128)(2,1)} %get-tuple-element.58.refs_3_.refs_0_) | copy-start | bytes 294916
  12.9 8.2 %copy-start.5 = (bf16[512,768]{1,0:T(8,128)(2,1)S(1)}, bf16[512,768]{1,0:T(8,128)(2,1)}, u32[]{:S(2)}) copy-start(bf16[512,768]{1,0:T(8,128)(2,1)} %get-tuple-element.62.refs_4_) | copy-start | bytes 2359300
  15.1 6.2 %copy-start.7 = (bf16[1024]{0:T(1024)(128)(2,1)S(1)}, bf16[1024]{0:T(1024)(128)(2,1)}, u32[]{:S(2)}) copy-start(bf16[1024]{0:T(1024)(128)(2,1)} %param.8) | copy-start | bytes 6148
  15.1 15.1 %copy-start.3 = (bf16[512,1024]{1,0:T(8,128)(2,1)S(1)}, bf16[512,1024]{1,0:T(8,128)(2,1)}, u32[]{:S(2)}) copy-start(bf16[512,1024]{1,0:T(8,128)(2,1)} %refs_0_.17) | copy-start | bytes 3145732
  21.2 22.4 %collective-permute-start.10 = (bf16[512,768]{1,0:T(8,128)(2,1)S(1)}, bf16[512,768]{1,0:T(8,128)(2,1)S(1)}, u32[]{:S(2)}, u32[]{:S(2)}) collective-permute-start(bf16[512,768]{1,0:T(8,128)(2,1)S(1)} %get-tuple-element.72), channel_id=1, source_target_pairs={{0,2},{2,4},{4,6},{6,8},{8,10},{10,12},{12,14},{14,16},{16,18},{18... | collective-permute-start | bytes 2359304 | tf_op jit(solution)/shard_map/ppermute | solution.py:276
  21.3 11.1 %collective-permute-start.6 = (bf16[384,128]{1,0:T(8,128)(2,1)S(1)}, bf16[384,128]{1,0:T(8,128)(2,1)S(1)}, u32[]{:S(2)}, u32[]{:S(2)}) collective-permute-start(bf16[384,128]{1,0:T(8,128)(2,1)S(1)} %get-tuple-element.65.refs_3_), channel_id=1, source_target_pairs={{0,24},{2,26},{4,28},{1,25},{3,27},{5,29}} | collective-permute-start | bytes 294920 | tf_op jit(solution)/shard_map/ppermute | solution.py:281
  26.4 5.9 %collective-permute-start.5 = (bf16[384,128]{1,0:T(8,128)(2,1)S(1)}, bf16[384,128]{1,0:T(8,128)(2,1)S(1)}, u32[]{:S(2)}, u32[]{:S(2)}) collective-permute-start(bf16[384,128]{1,0:T(8,128)(2,1)S(1)} %get-tuple-element.65.refs_3_), channel_id=1, source_target_pairs={{0,16},{2,18},{4,20},{8,24},{10,26},{12,28},{1,17},{3,19},{5,21},{... | collective-permute-start | bytes 294920 | tf_op jit(solution)/shard_map/ppermute | solution.py:281
  27.7 4.7 %collective-permute-start.4 = (bf16[384,128]{1,0:T(8,128)(2,1)S(1)}, bf16[384,128]{1,0:T(8,128)(2,1)S(1)}, u32[]{:S(2)}, u32[]{:S(2)}) collective-permute-start(bf16[384,128]{1,0:T(8,128)(2,1)S(1)} %get-tuple-element.65.refs_3_), channel_id=1, source_target_pairs={{0,8},{2,10},{4,12},{8,16},{10,18},{12,20},{16,24},{18,26},{20,28}... | collective-permute-start | bytes 294920 | tf_op jit(solution)/shard_map/ppermute | solution.py:281
  32.8 13.6 %collective-permute-start.7 = (bf16[384,128]{1,0:T(8,128)(2,1)S(1)}, bf16[384,128]{1,0:T(8,128)(2,1)S(1)}, u32[]{:S(2)}, u32[]{:S(2)}) collective-permute-start(bf16[384,128]{1,0:T(8,128)(2,1)S(1)} %get-tuple-element.68), channel_id=1, source_target_pairs={{0,2},{2,0},{4,6},{6,4},{8,10},{10,8},{12,14},{14,12},{16,18},{18,... | collective-permute-start | bytes 294920 | tf_op jit(solution)/shard_map/ppermute | solution.py:271
  34.3 12.2 %collective-permute-start.8 = (bf16[384,128]{1,0:T(8,128)(2,1)S(1)}, bf16[384,128]{1,0:T(8,128)(2,1)S(1)}, u32[]{:S(2)}, u32[]{:S(2)}) collective-permute-start(bf16[384,128]{1,0:T(8,128)(2,1)S(1)} %get-tuple-element.69), channel_id=1, source_target_pairs={{0,4},{2,6},{4,0},{6,2},{8,12},{10,14},{12,8},{14,10},{16,20},{18,... | collective-permute-start | bytes 294920 | tf_op jit(solution)/shard_map/ppermute | solution.py:271
  34.3 13.4 %collective-permute-start.9 = (bf16[384,128]{1,0:T(8,128)(2,1)S(1)}, bf16[384,128]{1,0:T(8,128)(2,1)S(1)}, u32[]{:S(2)}, u32[]{:S(2)}) collective-permute-start(bf16[384,128]{1,0:T(8,128)(2,1)S(1)} %get-tuple-element.70), channel_id=1, source_target_pairs={{0,6},{2,4},{4,2},{6,0},{8,14},{10,12},{12,10},{14,8},{16,22},{18,... | collective-permute-start | bytes 294920 | tf_op jit(solution)/shard_map/ppermute | solution.py:271
  43.5 4.1 %copy-start.4 = (bf16[512,1024]{1,0:T(8,128)(2,1)S(1)}, bf16[512,1024]{1,0:T(8,128)(2,1)}, u32[]{:S(2)}) copy-start(bf16[512,1024]{1,0:T(8,128)(2,1)} %refs_3_.1) | copy-start | bytes 3145732
  48.7 14.3 %collective-permute-start.15 = (bf16[192,1024]{1,0:T(8,128)(2,1)S(1)}, bf16[192,1024]{1,0:T(8,128)(2,1)S(1)}, u32[]{:S(2)}, u32[]{:S(2)}) collective-permute-start(bf16[192,1024]{1,0:T(8,128)(2,1)S(1)} %get-tuple-element.96), channel_id=1, source_target_pairs={{0,30},{2,0},{4,2},{6,4},{8,6},{10,8},{12,10},{14,12},{16,14},{18,... | collective-permute-start | bytes 1179656 | tf_op jit(solution)/shard_map/ppermute | solution.py:276
  49.6 1.2 %collective-permute-start.11 = (f32[8,512]{1,0:T(8,128)S(1)}, f32[8,512]{1,0:T(8,128)S(1)}, u32[]{:S(2)}, u32[]{:S(2)}) collective-permute-start(f32[8,512]{1,0:T(8,128)S(1)} %get-tuple-element.75), channel_id=1, source_target_pairs={{0,1},{1,0},{2,3},{3,2},{4,5},{5,4},{6,7},{7,6},{8,9},{9,8},{10,11... | collective-permute-start | bytes 49160 | tf_op jit(solution)/shard_map/ppermute | solution.py:702
  53.0 10.0 %collective-permute-start.12 = (bf16[384,128]{1,0:T(8,128)(2,1)S(1)}, bf16[384,128]{1,0:T(8,128)(2,1)S(1)}, u32[]{:S(2)}, u32[]{:S(2)}) collective-permute-start(bf16[384,128]{1,0:T(8,128)(2,1)S(1)} %get-tuple-element.92), channel_id=1, source_target_pairs={{0,2},{2,0},{4,6},{6,4},{8,10},{10,8},{12,14},{14,12},{16,18},{18,... | collective-permute-start | bytes 294920 | tf_op jit(solution)/shard_map/ppermute | solution.py:271
  54.5 8.5 %collective-permute-start.13 = (bf16[384,128]{1,0:T(8,128)(2,1)S(1)}, bf16[384,128]{1,0:T(8,128)(2,1)S(1)}, u32[]{:S(2)}, u32[]{:S(2)}) collective-permute-start(bf16[384,128]{1,0:T(8,128)(2,1)S(1)} %get-tuple-element.93), channel_id=1, source_target_pairs={{0,4},{2,6},{4,0},{6,2},{8,12},{10,14},{12,8},{14,10},{16,20},{18,... | collective-permute-start | bytes 294920 | tf_op jit(solution)/shard_map/ppermute | solution.py:271
  54.5 8.5 %collective-permute-start.14 = (bf16[384,128]{1,0:T(8,128)(2,1)S(1)}, bf16[384,128]{1,0:T(8,128)(2,1)S(1)}, u32[]{:S(2)}, u32[]{:S(2)}) collective-permute-start(bf16[384,128]{1,0:T(8,128)(2,1)S(1)} %get-tuple-element.94), channel_id=1, source_target_pairs={{0,6},{2,4},{4,2},{6,0},{8,14},{10,12},{12,10},{14,8},{16,22},{18,... | collective-permute-start | bytes 294920 | tf_op jit(solution)/shard_map/ppermute | solution.py:271
  63.1 20.3 %collective-permute-start.16 = (bf16[336,1024]{1,0:T(8,128)(2,1)S(1)}, bf16[336,1024]{1,0:T(8,128)(2,1)S(1)}, u32[]{:S(2)}, u32[]{:S(2)}) collective-permute-start(bf16[336,1024]{1,0:T(8,128)(2,1)S(1)} %get-tuple-element.100), channel_id=1, source_target_pairs={{0,30},{2,0},{4,2},{6,4},{8,6},{10,8},{12,10},{14,12},{16,14},{18,... | collective-permute-start | bytes 2064392 | tf_op jit(solution)/shard_map/ppermute | solution.py:276
  68.5 6.3 %collective-permute-start.19 = (bf16[384,128]{1,0:T(8,128)(2,1)S(1)}, bf16[384,128]{1,0:T(8,128)(2,1)S(1)}, u32[]{:S(2)}, u32[]{:S(2)}) collective-permute-start(bf16[384,128]{1,0:T(8,128)(2,1)S(1)} %get-tuple-element.98.refs_17_), channel_id=1, source_target_pairs={{26,2},{28,4},{30,6},{27,3},{29,5},{31,7}} | collective-permute-start | bytes 294920 | tf_op jit(solution)/shard_map/ppermute | solution.py:281
  69.2 5.7 %collective-permute-start.18 = (bf16[384,128]{1,0:T(8,128)(2,1)S(1)}, bf16[384,128]{1,0:T(8,128)(2,1)S(1)}, u32[]{:S(2)}, u32[]{:S(2)}) collective-permute-start(bf16[384,128]{1,0:T(8,128)(2,1)S(1)} %get-tuple-element.98.refs_17_), channel_id=1, source_target_pairs={{18,2},{20,4},{22,6},{26,10},{28,12},{30,14},{19,3},{21,5},{23,7},... | collective-permute-start | bytes 294920 | tf_op jit(solution)/shard_map/ppermute | solution.py:281
  69.9 5.0 %collective-permute-start.17 = (bf16[384,128]{1,0:T(8,128)(2,1)S(1)}, bf16[384,128]{1,0:T(8,128)(2,1)S(1)}, u32[]{:S(2)}, u32[]{:S(2)}) collective-permute-start(bf16[384,128]{1,0:T(8,128)(2,1)S(1)} %get-tuple-element.98.refs_17_), channel_id=1, source_target_pairs={{10,2},{12,4},{14,6},{18,10},{20,12},{22,14},{26,18},{28,20},{30,2... | collective-permute-start | bytes 294920 | tf_op jit(solution)/shard_map/ppermute | solution.py:281
  75.2 10.2 %collective-permute-start.20 = (bf16[384,128]{1,0:T(8,128)(2,1)S(1)}, bf16[384,128]{1,0:T(8,128)(2,1)S(1)}, u32[]{:S(2)}, u32[]{:S(2)}) collective-permute-start(bf16[384,128]{1,0:T(8,128)(2,1)S(1)} %get-tuple-element.105), channel_id=1, source_target_pairs={{0,2},{2,0},{4,6},{6,4},{8,10},{10,8},{12,14},{14,12},{16,18},{18,... | collective-permute-start | bytes 294920 | tf_op jit(solution)/shard_map/ppermute | solution.py:271
  77.2 8.2 %collective-permute-start.21 = (bf16[384,128]{1,0:T(8,128)(2,1)S(1)}, bf16[384,128]{1,0:T(8,128)(2,1)S(1)}, u32[]{:S(2)}, u32[]{:S(2)}) collective-permute-start(bf16[384,128]{1,0:T(8,128)(2,1)S(1)} %get-tuple-element.106), channel_id=1, source_target_pairs={{0,4},{2,6},{4,0},{6,2},{8,12},{10,14},{12,8},{14,10},{16,20},{18,... | collective-permute-start | bytes 294920 | tf_op jit(solution)/shard_map/ppermute | solution.py:271
  79.7 6.0 %collective-permute-start.22 = (bf16[384,128]{1,0:T(8,128)(2,1)S(1)}, bf16[384,128]{1,0:T(8,128)(2,1)S(1)}, u32[]{:S(2)}, u32[]{:S(2)}) collective-permute-start(bf16[384,128]{1,0:T(8,128)(2,1)S(1)} %get-tuple-element.107), channel_id=1, source_target_pairs={{0,6},{2,4},{4,2},{6,0},{8,14},{10,12},{12,10},{14,8},{16,22},{18,... | collective-permute-start | bytes 294920 | tf_op jit(solution)/shard_map/ppermute | solution.py:271

commit v4 on v3

--- a/solution.py
+++ b/solution.py
@@ -57,7 +57,17 @@
 
 
 def sent_chunks(heads):
-    return [(0, 2), (2, heads - 2)] if heads > 2 else [(0, heads)]
+    return [(0, heads - 2), (heads - 2, 2)] if heads > 4 else [(0, heads)]
+
+
+def tails_apart(tails):
+    return [tuple(tails[:2])] + [(tail, tail) for tail in tails[2:]]
+
+
+def tail_columns(tail, place):
+    keys, values = tail
+    below = WINDOW if keys is values else 0
+    return keys[:WINDOW, columns_of(place)], values[below : below + WINDOW, columns_of(place)]
 
 
 def even_chunks(heads):
@@ -171,53 +181,47 @@
         held[lax.bitwise_xor(place, jnp.int32(other))] = ins[other][...]
 
 
-def state_body(steps, k_ref, v_ref, *rest):
+def state_body(k_ref, v_ref, *rest):
     outs, tails = rest[:GROUP], rest[GROUP:-4]
     k_held, v_held, held, done = rest[-4:]
     rows, width = k_held.shape
-    wide = width // steps
-    chunks = sent_chunks(width // HEAD_DIM)
-    loads, sends = [], {}
-    for step in range(steps):
-        cols = pl.ds(step * wide, wide)
-        for at, (source, target) in enumerate(((k_ref, k_held), (v_ref, v_held))):
-            loads.append(pltpu.make_async_copy(source.at[:, cols], target.at[:, cols], done.at[2 * step + at]))
-    for step in range(steps):
-        cols = pl.ds(step * wide, wide)
-        tail, place = picked(chunks, tails, step * wide // HEAD_DIM)
-        sends[step] = [
-            pltpu.make_async_copy(
-                source.at[pl.ds(rows - WINDOW, WINDOW), cols],
-                tail.at[pl.ds(at * WINDOW, WINDOW), pl.ds(place * HEAD_DIM, wide)],
-                done.at[2 * (steps + step) + at],
+    held[...] = jnp.zeros_like(held)
+    loads = []
+    for first in (rows - WINDOW, 0):
+        part = pl.ds(first, rows - WINDOW if first == 0 else WINDOW)
+        for source, target in ((k_ref, k_held), (v_ref, v_held)):
+            loads.append(pltpu.make_async_copy(source.at[part, :], target.at[part, :], done.at[len(loads)]))
+            loads[-1].start()
+    for copy in loads[:2]:
+        copy.wait()
+    sends = []
+    for (first, count), tail in zip(sent_chunks(width // HEAD_DIM), tails):
+        for at, source in enumerate((v_held,) if first == 0 else (k_held, v_held)):
+            sends.append(
+                pltpu.make_async_copy(
+                    source.at[pl.ds(rows - WINDOW, WINDOW), pl.ds(first * HEAD_DIM, count * HEAD_DIM)],
+                    tail.at[pl.ds(at * WINDOW, WINDOW), :],
+                    done.at[4 + len(sends)],
+                )
             )
-            for at, source in enumerate((k_held, v_held))
-        ]
-    held[...] = jnp.zeros_like(held)
-    for copy in loads:
-        copy.start()
-    for step in range(steps):
-        loads[2 * step].wait()
-        loads[2 * step + 1].wait()
-        for copy in sends[step]:
-            copy.start()
-        for head in range(step * wide // HEAD_DIM, (step + 1) * wide // HEAD_DIM):
-            cols = slice(head * HEAD_DIM, (head + 1) * HEAD_DIM)
-            store_state(held, head, dot_tn(k_held[:, cols], v_held[:, cols]).astype(BF16), False)
+            sends[-1].start()
+    for copy in loads[2:]:
+        copy.wait()
+    for head in range(width // HEAD_DIM):
+        cols = columns_of(head)
+        store_state(held, head, dot_tn(k_held[:, cols], v_held[:, cols]).astype(BF16), False)
     spread(held, outs)
-    for step in range(steps):
-        for copy in sends[step]:
-            copy.wait()
+    for copy in sends:
+        copy.wait()
 
 
 def local_states(keys, values):
     rows, width = keys.shape
     heads = width // HEAD_DIM
-    tails = [(2 * WINDOW, count * HEAD_DIM) for _, count in sent_chunks(heads)]
-    steps = heads // heads_a_step(heads)
+    tails = [(2 * WINDOW if first else WINDOW, count * HEAD_DIM) for first, count in sent_chunks(heads)]
     piece = part_shape(heads)
     results, _ = call(
-        lambda *refs: state_body(steps, *refs),
+        state_body,
         (1,),
         [HBM] * 2,
         [whole(piece)] * GROUP + [ANY] * len(tails),
@@ -226,7 +230,7 @@
             pltpu.VMEM((rows, width), BF16),
             pltpu.VMEM((rows, width), BF16),
             pltpu.VMEM((GROUP,) + piece, BF16),
-            pltpu.SemaphoreType.DMA((4 * steps,)),
+            pltpu.SemaphoreType.DMA((4 + 2 * len(tails),)),
         ],
         2 * rows * width * HEAD_DIM,
         2 * 2 * rows * width,
@@ -281,6 +285,10 @@
     return lax.ppermute(
         value, "ctx", [(at, at + steps) for at in range(count) if at % GROUP in places and 0 <= at + steps < count]
     )
+
+
+def onward(value, steps):
+    return shift(value, steps, range(GROUP))
 
 
 def scan(pieces, reverse, first, second):
@@ -371,7 +379,8 @@
     )[0]
 
 
-def early_body(first, count, q_ref, k_ref, v_ref, tail_ref, *rest):
+def early_body(first, count, sent, q_ref, k_ref, v_ref, *rest):
+    tail, rest = (rest[0], rest[sent - 1]), rest[sent:]
     prob_ref, sum_ref, inside_ref, window_ref, lse_ref = rest[-5:]
     rows = k_ref.shape[0]
     block = lax.axis_index("ctx")
@@ -383,14 +392,15 @@
     for at in range(count):
         cols, own = columns_of(first + at), columns_of(at)
         query = q_ref[:WINDOW, cols]
-        scores = [dot_nt(tail_ref[:WINDOW, own], query), dot_nt(k_ref[:WINDOW, cols], query)]
+        key_before, value_before = tail_columns(tail, at)
+        scores = [dot_nt(key_before, query), dot_nt(k_ref[:WINDOW, cols], query)]
         probs, sums, lse = attend(scores, masks, coef, ["none", "masked"])
         prob_ref[at, 0] = probs[0]
         prob_ref[at, 1] = probs[1]
         sum_ref[at] = sums[1]
         lse_ref[first + at : first + at + 1, :] = lse
         value = v_ref[:WINDOW, cols]
-        before = dot_tn(tail_ref[WINDOW:, own], probs[0])
+        before = dot_tn(value_before, probs[0])
         window_ref[:, own] = (before + dot_tn(value, probs[1])).T
         inside_ref[:, own] = (before + dot_tn(value, sums[1])).T
 
@@ -398,8 +408,8 @@
 def early_rows(first, count, queries, keys, values, before, done, after):
     wide = count * HEAD_DIM
     return run_once(
-        lambda *refs: early_body(first, count, *refs),
-        [queries, keys, values, before, *done],
+        lambda *refs: early_body(first, count, len(before), *refs),
+        [queries, keys, values, *before, *done],
         [
             ((count, 2, WINDOW, WINDOW), BF16),
             ((count, WINDOW, WINDOW), BF16),
@@ -538,7 +548,7 @@
     rows = q_ref.shape[0]
     last = first + count == heads
     ins, rest = rest[:GROUP], rest[GROUP:]
-    tails, rest = rest[: len(sent)], rest[len(sent) :]
+    tails, rest = tails_apart(rest[: len(sent) + 1]), rest[len(sent) + 1 :]
     probs0, rest = rest[: len(sent)], rest[len(sent) :]
     sums0, rest = rest[: len(sent)], rest[len(sent) :]
     probs1, sums1 = rest[0], rest[1]
@@ -563,13 +573,14 @@
     for at in range(count):
         head = first + at
         cols, own = columns_of(head), columns_of(at)
-        before_ref, place = picked(sent, tails, head)
+        tail, place = picked(sent, tails, head)
+        key_before, value_before = tail_columns(tail, place)
         prob0 = picked(sent, probs0, head)[0]
         sum0 = picked(sent, sums0, head)[0]
         grads = g_ref[early, cols], g_ref[late, cols]
         queries = q_ref[early, cols], q_ref[late, cols]
-        keys = before_ref[:WINDOW, columns_of(place)], k_ref[early, cols], k_ref[late, cols]
-        values = before_ref[WINDOW:, columns_of(place)], v_ref[early, cols], v_ref[late, cols]
+        keys = key_before, k_ref[early, cols], k_ref[late, cols]
+        values = value_before, v_ref[early, cols], v_ref[late, cols]
         probs = (
             (prob0[place, 0].astype(F32), prob0[place, 1].astype(F32)),
             (probs1[at, 0].astype(F32), probs1[at, 1].astype(F32)),
@@ -712,21 +723,21 @@
     gain = gain.reshape(1, width)
     late, own, grads_after = [], [], []
 
+    before = [turn(keys[rows - WINDOW :, : sent[0][1] * HEAD_DIM], 1)]
     pieces, tails = local_states(keys, values)
-    before = [turn(tails[0], 1)]
 
     def first_round():
         late.append(late_rows(*even[0], queries, keys, values, pieces[:1]))
-        return tails[1:], [before[0], late[0][2]]
+        return tails, [before[0], late[0][2]]
 
     def second_round(total, held):
-        before.extend(turn(tail, 1) for tail in held)
+        before.extend(onward(tail, 1) if at else turn(tail, 1) for at, tail in enumerate(held))
         late.extend(late_rows(*chunk, queries, keys, values, [total]) for chunk in even[1:])
         return [], [late[-1][2]]
 
     prefix, merged, _ = scan(pieces, False, first_round, second_round)
     early = []
-    for chunk, tail in zip(sent, before):
+    for chunk, tail in zip(sent, [before[:2]] + [[tail] for tail in before[2:]]):
         done = [early[-1][4]] if early else []
         early.append(early_rows(*chunk, queries, keys, values, tail, done, merged[:1]))
     probs0, sums0, insides, windows, lses = zip(*early)

time: 89.4 us -> 86.8 us (0.971)
  the two profiles are of different devices: /device:TPU:0 before, /device:TPU:31 now
where the time goes in v4:
time: 86.8 us; the launch traced here: 86.5 us
  starting transfers between devices  30.7 us (35%)
  Pallas kernels  26.4 us (30%)
  waiting for transfers between devices  24.8 us (29%)
  local copies, waits for them, and re-layouts  3.36 us (4%)
  between operations  1.15 us (1%)
    pallas_call x15, Pallas kernels, call(): pl.pallas_call(run, grid=grid, input_output_aliases={**(aliases or {}), *...  26.4 us
    ppermute x12, waiting for transfers between devices, swap(): return lax.ppermute(value, 'ctx', [(at, at ^ mask) for at in range(count)])  16.6 us
    ppermute x12, starting transfers between devices, swap(): return lax.ppermute(value, 'ctx', [(at, at ^ mask) for at in range(count)])  15.5 us
    ppermute x7, starting transfers between devices, shift(): lax.ppermute(value, 'ctx', [(at, at + steps) for at in range(count) if at...  8.91 us
    ppermute x4, waiting for transfers between devices, turn(): lax.ppermute(value, 'ctx', [(at, (at + steps) % count) for at in range(co...  7.33 us
    ppermute x4, starting transfers between devices, turn(): lax.ppermute(value, 'ctx', [(at, (at + steps) % count) for at in range(co...  5.07 us
    unnamed x18, local copies, waits for them, and re-layouts  2.16 us
  transfers between devices with their start and end apart: 24, of which 10 were waited for; matrix products, arithmetic and copies ran while one was open for 0% of the time, Pallas kernels for 27%

profile of v4, /device:TPU:31, one launch (start us, length us, event | category | flops | bytes accessed | tf_op | source)
XLA Modules:
  0.0 86.5 jit_solution(15217027725881168795)
XLA Ops:
  0.7 1.2 %slice.6 = bf16[256,768]{1,0:T(8,128)(2,1)S(1)} slice(bf16[512,1024]{1,0:T(8,128)(2,1)} %refs_0_.19), slice={[256:512], [0:768]} | slice | bytes 786432 | tf_op jit(solution)/shard_map/slice | solution.py:726
  1.9 2.9 %shard_map.84 = (bf16[384,128]{1,0:T(8,128)(2,1)}, bf16[384,128]{1,0:T(8,128)(2,1)}, bf16[384,128]{1,0:T(8,128)(2,1)}, bf16[384,128]{1,0:T(8,128)(2,1)}, bf16[25...) custom-call(bf16[512,1024]{1,0:T(8,128)(2,1)} %refs_0_.19, bf16[512,1024]{1,0:T(8,128)(2,1)} %refs_1_.17), custom_call_target="tpu_custom_call" | custom-call | flops 134217728 | bytes 2097152 | tf_op jit(solution)/shard_map/pallas_call | solution.py:95
  4.8 1.5 %collective-permute-start = (bf16[384,128]{1,0:T(8,128)(2,1)}, bf16[384,128]{1,0:T(8,128)(2,1)S(1)}, u32[]{:S(2)}, u32[]{:S(2)}) collective-permute-start(bf16[384,128]{1,0:T(8,128)(2,1)} %get-tuple-element.60), channel_id=1, source_target_pairs={{0,2},{2,0},{4,6},{6,4},{8,10},{10,8},{12,14},{14,12},{16,18},{18,... | collective-permute-start | bytes 294920 | tf_op jit(solution)/shard_map/ppermute | solution.py:275
  7.6 1.2 %copy-done.2 = bf16[512,1024]{1,0:T(8,128)(2,1)S(1)} copy-done((bf16[512,1024]{1,0:T(8,128)(2,1)S(1)}, bf16[512,1024]{1,0:T(8,128)(2,1)}, u32[]{:S(2)}) %copy-start.2) | copy-done | bytes 1048600
  9.7 2.1 %shard_map.85 = (bf16[4,2,256,256]{3,2,1,0:T(8,128)(2,1)S(1)}, bf16[4,2,256,256]{3,2,1,0:T(8,128)(2,1)S(1)}, f32[256,512]{1,0:T(8,128)S(1)}) custom-call(bf16[512,1024]{1,0:T(8,128)(2,1)S(1)} %copy-done.2, bf16[512,1024]{1,0:T(8,128)(2,1)S(1)} %copy-done, bf16[512,1024]{1,0:T(8,128)(2,1)S(1)} %copy-done.1, bf16[384,128]{1,0:T(8,128)(2,1)S(1)} %copy-done.6), custom_call_target="tpu_custom_call" | custom-call | flops 1073741824 | bytes 3145728 | tf_op jit(solution)/shard_map/pallas_call | solution.py:95
  11.8 2.2 %collective-permute-done.refs_1_.refs_4_ = bf16[384,128]{1,0:T(8,128)(2,1)S(1)} collective-permute-done((bf16[384,128]{1,0:T(8,128)(2,1)}, bf16[384,128]{1,0:T(8,128)(2,1)S(1)}, u32[]{:S(2)}, u32[]{:S(2)}) %collective-permute-start) | collective-permute-done | bytes 98336 | tf_op jit(solution)/shard_map/ppermute | solution.py:275
  14.0 2.1 %collective-permute-done.2.refs_3_.refs_6_ = bf16[384,128]{1,0:T(8,128)(2,1)S(1)} collective-permute-done((bf16[384,128]{1,0:T(8,128)(2,1)}, bf16[384,128]{1,0:T(8,128)(2,1)S(1)}, u32[]{:S(2)}, u32[]{:S(2)}) %collective-permute-start.2) | collective-permute-done | bytes 98336 | tf_op jit(solution)/shard_map/ppermute | solution.py:275
  16.2 4.7 %collective-permute-start.10 = (bf16[256,768]{1,0:T(8,128)(2,1)S(1)}, bf16[256,768]{1,0:T(8,128)(2,1)S(1)}, u32[]{:S(2)}, u32[]{:S(2)}) collective-permute-start(bf16[256,768]{1,0:T(8,128)(2,1)S(1)} %get-tuple-element.72), channel_id=1, source_target_pairs={{0,2},{2,4},{4,6},{6,8},{8,10},{10,12},{12,14},{14,16},{16,18},{18... | collective-permute-start | bytes 1179656 | tf_op jit(solution)/shard_map/ppermute | solution.py:280
  22.9 1.3 %collective-permute-start.11 = (bf16[512,256]{1,0:T(8,128)(2,1)S(1)}, bf16[512,256]{1,0:T(8,128)(2,1)S(1)}, u32[]{:S(2)}, u32[]{:S(2)}) collective-permute-start(bf16[512,256]{1,0:T(8,128)(2,1)S(1)} %get-tuple-element.74), channel_id=1, source_target_pairs={{0,2},{2,4},{4,6},{6,8},{8,10},{10,12},{12,14},{14,16},{16,18},{18... | collective-permute-start | bytes 786440 | tf_op jit(solution)/shard_map/ppermute | solution.py:285
  24.2 2.1 %shard_map.87 = (bf16[4,2,256,256]{3,2,1,0:T(8,128)(2,1)S(1)}, bf16[4,2,256,256]{3,2,1,0:T(8,128)(2,1)S(1)}, f32[256,512]{1,0:T(8,128)S(1)}) custom-call(bf16[512,1024]{1,0:T(8,128)(2,1)S(1)} %copy-done.3, bf16[512,1024]{1,0:T(8,128)(2,1)S(1)} %copy-done, bf16[512,1024]{1,0:T(8,128)(2,1)S(1)} %copy-done.1, bf16[384,128]{1,0:T(8,128)(2,1)S(1)} %get-tuple-element.66.refs_3_), custom_call_target="tpu_custom_call" | custom-call | flops 1073741824 | bytes 3145728 | tf_op jit(solution)/shard_map/pallas_call | solution.py:95
  26.7 3.9 %collective-permute-start.7 = (bf16[384,128]{1,0:T(8,128)(2,1)S(1)}, bf16[384,128]{1,0:T(8,128)(2,1)S(1)}, u32[]{:S(2)}, u32[]{:S(2)}) collective-permute-start(bf16[384,128]{1,0:T(8,128)(2,1)S(1)} %get-tuple-element.69), channel_id=1, source_target_pairs={{0,2},{2,0},{4,6},{6,4},{8,10},{10,8},{12,14},{14,12},{16,18},{18,... | collective-permute-start | bytes 294920 | tf_op jit(solution)/shard_map/ppermute | solution.py:275
  30.6 1.8 %collective-permute-start.8 = (bf16[384,128]{1,0:T(8,128)(2,1)S(1)}, bf16[384,128]{1,0:T(8,128)(2,1)S(1)}, u32[]{:S(2)}, u32[]{:S(2)}) collective-permute-start(bf16[384,128]{1,0:T(8,128)(2,1)S(1)} %get-tuple-element.70), channel_id=1, source_target_pairs={{0,4},{2,6},{4,0},{6,2},{8,12},{10,14},{12,8},{14,10},{16,20},{18,... | collective-permute-start | bytes 294920 | tf_op jit(solution)/shard_map/ppermute | solution.py:275
  32.6 2.9 %shard_map.89 = (bf16[6,2,256,256]{3,2,1,0:T(8,128)(2,1)S(1)}, bf16[6,256,256]{2,1,0:T(8,128)(2,1)S(1)}, f32[256,768]{1,0:T(8,128)S(1)}, f32[256,768]{1,0:T(8,128)S(1)}, f32[8,256]{1,0:T(8,128)S(1)}) custom-call(bf16[512,1024]{1,0:T(8,128)(2,1)S(1)} %copy-done.3, bf16[512,1024]{1,0:T(8,128)(2,1)S(1)} %copy-done, bf16[512,1024]{1,0:T(8,128)(2,1)S(1)} %copy-done.1, ...), custom_call_target="tpu_custom_call" | custom-call | flops 2013265920 | bytes 4718592 | tf_op jit(solution)/shard_map/pallas_call | solution.py:95
  35.5 1.2 %shard_map.90 = (bf16[2,2,256,256]{3,2,1,0:T(8,128)(2,1)S(1)}, bf16[2,256,256]{2,1,0:T(8,128)(2,1)S(1)}, f32[256,256]{1,0:T(8,128)S(1)}, f32[256,256]{1,0:T(8,128)S(1)}, f32[8,256]{1,0:T(8,128)S(1)}) custom-call(bf16[512,1024]{1,0:T(8,128)(2,1)S(1)} %copy-done.3, bf16[512,1024]{1,0:T(8,128)(2,1)S(1)} %copy-done, bf16[512,1024]{1,0:T(8,128)(2,1)S(1)} %copy-done.1, ...), custom_call_target="tpu_custom_call" | custom-call | flops 671088640 | bytes 1572864 | tf_op jit(solution)/shard_map/pallas_call | solution.py:95
  36.7 2.1 %collective-permute-done.9.refs_6_.refs_7_ = bf16[384,128]{1,0:T(8,128)(2,1)S(1)} collective-permute-done((bf16[384,128]{1,0:T(8,128)(2,1)S(1)}, bf16[384,128]{1,0:T(8,128)(2,1)S(1)}, u32[]{:S(2)}, u32[]{:S(2)}) %collective-permute-start.9) | collective-permute-done | bytes 98336 | tf_op jit(solution)/shard_map/ppermute | solution.py:275
  40.2 1.2 %collective-permute-start.12 = (f32[8,512]{1,0:T(8,128)S(1)}, f32[8,512]{1,0:T(8,128)S(1)}, u32[]{:S(2)}, u32[]{:S(2)}) collective-permute-start(f32[8,512]{1,0:T(8,128)S(1)} %get-tuple-element.77), channel_id=1, source_target_pairs={{0,1},{1,0},{2,3},{3,2},{4,5},{5,4},{6,7},{7,6},{8,9},{9,8},{10,11... | collective-permute-start | bytes 49160 | tf_op jit(solution)/shard_map/ppermute | solution.py:713
  42.3 2.3 %shard_map.92 = (bf16[512,1024]{1,0:T(8,128)(2,1)}, bf16[512,1024]{1,0:T(8,128)(2,1)S(1)}, bf16[336,1024]{1,0:T(8,128)(2,1)S(1)}, bf16[384,128]{1,0:T(8,128)(2,1...) custom-call(f32[8,512]{1,0:T(8,128)S(1)} %add.3.refs_0_, ...), custom_call_target="tpu_custom_call" | custom-call | flops 134217728 | bytes 7340032 | tf_op jit(solution)/shard_map/pallas_call | solution.py:95
  44.6 1.4 %collective-permute-start.13 = (bf16[384,128]{1,0:T(8,128)(2,1)S(1)}, bf16[384,128]{1,0:T(8,128)(2,1)S(1)}, u32[]{:S(2)}, u32[]{:S(2)}) collective-permute-start(bf16[384,128]{1,0:T(8,128)(2,1)S(1)} %get-tuple-element.94), channel_id=1, source_target_pairs={{0,2},{2,0},{4,6},{6,4},{8,10},{10,8},{12,14},{14,12},{16,18},{18,... | collective-permute-start | bytes 294920 | tf_op jit(solution)/shard_map/ppermute | solution.py:275
  46.0 2.7 %collective-permute-start.14 = (bf16[384,128]{1,0:T(8,128)(2,1)S(1)}, bf16[384,128]{1,0:T(8,128)(2,1)S(1)}, u32[]{:S(2)}, u32[]{:S(2)}) collective-permute-start(bf16[384,128]{1,0:T(8,128)(2,1)S(1)} %get-tuple-element.95), channel_id=1, source_target_pairs={{0,4},{2,6},{4,0},{6,2},{8,12},{10,14},{12,8},{14,10},{16,20},{18,... | collective-permute-start | bytes 294920 | tf_op jit(solution)/shard_map/ppermute | solution.py:275
  48.8 3.2 %shard_map.93 = (bf16[512,512]{1,0:T(8,128)(2,1)S(1)}, f32[512,512]{1,0:T(8,128)S(1)}, f32[512,512]{1,0:T(8,128)S(1)}) custom-call(bf16[512,1024]{1,0:T(8,128)(2,1)S(1)} %copy-done.3, bf16[512,1024]{1,0:T(8,128)(2,1)S(1)} %copy-done, bf16[512,1024]{1,0:T(8,128)(2,1)S(1)} %copy-done.1, bf16[512,1024]{1,0:T(8,128)(2,1)S(1)} %get-tuple-element.83.refs_3_, ...), custom_call_target="tpu_custom_call" | custom-call | flops 2147483648 | bytes 10485760 | tf_op jit(solution)/shard_map/pallas_call | solution.py:95
  52.0 4.9 %collective-permute-done.14.refs_2_.refs_5_ = bf16[384,128]{1,0:T(8,128)(2,1)S(1)} collective-permute-done((bf16[384,128]{1,0:T(8,128)(2,1)S(1)}, bf16[384,128]{1,0:T(8,128)(2,1)S(1)}, u32[]{:S(2)}, u32[]{:S(2)}) %collective-permute-start.14) | collective-permute-done | bytes 98336 | tf_op jit(solution)/shard_map/ppermute | solution.py:275
  56.9 2.1 %collective-permute-done.15.refs_3_.refs_6_ = bf16[384,128]{1,0:T(8,128)(2,1)S(1)} collective-permute-done((bf16[384,128]{1,0:T(8,128)(2,1)S(1)}, bf16[384,128]{1,0:T(8,128)(2,1)S(1)}, u32[]{:S(2)}, u32[]{:S(2)}) %collective-permute-start.15) | collective-permute-done | bytes 98336 | tf_op jit(solution)/shard_map/ppermute | solution.py:275
  59.2 1.9 %collective-permute-start.20 = (bf16[384,128]{1,0:T(8,128)(2,1)S(1)}, bf16[384,128]{1,0:T(8,128)(2,1)S(1)}, u32[]{:S(2)}, u32[]{:S(2)}) collective-permute-start(bf16[384,128]{1,0:T(8,128)(2,1)S(1)} %get-tuple-element.100.refs_18_), channel_id=1, source_target_pairs={{26,2},{28,4},{30,6},{27,3},{29,5},{31,7}} | collective-permute-start | bytes 294920 | tf_op jit(solution)/shard_map/ppermute | solution.py:285
  61.1 1.3 %collective-permute-start.19 = (bf16[384,128]{1,0:T(8,128)(2,1)S(1)}, bf16[384,128]{1,0:T(8,128)(2,1)S(1)}, u32[]{:S(2)}, u32[]{:S(2)}) collective-permute-start(bf16[384,128]{1,0:T(8,128)(2,1)S(1)} %get-tuple-element.100.refs_18_), channel_id=1, source_target_pairs={{18,2},{20,4},{22,6},{26,10},{28,12},{30,14},{19,3},{21,5},{23,7},... | collective-permute-start | bytes 294920 | tf_op jit(solution)/shard_map/ppermute | solution.py:285
  62.4 2.4 %collective-permute-start.18 = (bf16[384,128]{1,0:T(8,128)(2,1)S(1)}, bf16[384,128]{1,0:T(8,128)(2,1)S(1)}, u32[]{:S(2)}, u32[]{:S(2)}) collective-permute-start(bf16[384,128]{1,0:T(8,128)(2,1)S(1)} %get-tuple-element.100.refs_18_), channel_id=1, source_target_pairs={{10,2},{12,4},{14,6},{18,10},{20,12},{22,14},{26,18},{28,20},{30,2... | collective-permute-start | bytes 294920 | tf_op jit(solution)/shard_map/ppermute | solution.py:285
  64.8 4.1 %shard_map.95 = (bf16[512,1024]{1,0:T(8,128)(2,1)}, f32[512,512]{1,0:T(8,128)S(1)}, f32[512,512]{1,0:T(8,128)S(1)}) custom-call(bf16[512,1024]{1,0:T(8,128)(2,1)S(1)} %copy-done.3, bf16[512,1024]{1,0:T(8,128)(2,1)S(1)} %copy-done, bf16[512,1024]{1,0:T(8,128)(2,1)S(1)} %copy-done.1, bf16[512,1024]{1,0:T(8,128)(2,1)S(1)} %get-tuple-element.83.refs_3_, ...), custom_call_target="tpu_custom_call" | custom-call | flops 2147483648 | bytes 10485760 | tf_op jit(solution)/shard_map/pallas_call | solution.py:95
  69.4 2.6 %collective-permute-start.23 = (bf16[384,128]{1,0:T(8,128)(2,1)S(1)}, bf16[384,128]{1,0:T(8,128)(2,1)S(1)}, u32[]{:S(2)}, u32[]{:S(2)}) collective-permute-start(bf16[384,128]{1,0:T(8,128)(2,1)S(1)} %get-tuple-element.109), channel_id=1, source_target_pairs={{0,6},{2,4},{4,2},{6,0},{8,14},{10,12},{12,10},{14,8},{16,22},{18,... | collective-permute-start | bytes 294920 | tf_op jit(solution)/shard_map/ppermute | solution.py:275
  72.0 7.3 %collective-permute-done.17.refs_3_ = bf16[336,1024]{1,0:T(8,128)(2,1)S(1)} collective-permute-done((bf16[336,1024]{1,0:T(8,128)(2,1)S(1)}, bf16[336,1024]{1,0:T(8,128)(2,1)S(1)}, u32[]{:S(2)}, u32[]{:S(2)}) %collective-permute-start.17) | collective-permute-done | bytes 688160 | tf_op jit(solution)/shard_map/ppermute | solution.py:280
  79.3 2.0 %shard_map.97 = (f32[256,1024]{1,0:T(8,128)S(1)}, f32[256,1024]{1,0:T(8,128)S(1)}) custom-call(bf16[512,1024]{1,0:T(8,128)(2,1)S(1)} %copy-done, bf16[512,1024]{1,0:T(8,128)(2,1)S(1)} %copy-done.1, bf16[192,1024]{1,0:T(8,128)(2,1)S(1)} %collective-permute-done.16.refs_5_.refs_2_, bf16[336,1024]{1,0:T(8,128)(2,1)S(1)} %collective-permute-done.17.refs_3_, ...), custom_call_target="tpu_custom_call" | custom-call | flops 536870912 | bytes 3145728 | tf_op jit(solution)/shard_map/pallas_call | solution.py:95
  81.3 1.1 %collective-permute-done.22.refs_6_ = bf16[384,128]{1,0:T(8,128)(2,1)S(1)} collective-permute-done((bf16[384,128]{1,0:T(8,128)(2,1)S(1)}, bf16[384,128]{1,0:T(8,128)(2,1)S(1)}, u32[]{:S(2)}, u32[]{:S(2)}) %collective-permute-start.22) | collective-permute-done | bytes 98336 | tf_op jit(solution)/shard_map/ppermute | solution.py:275
  82.4 2.0 %collective-permute-done.23.refs_7_ = bf16[384,128]{1,0:T(8,128)(2,1)S(1)} collective-permute-done((bf16[384,128]{1,0:T(8,128)(2,1)S(1)}, bf16[384,128]{1,0:T(8,128)(2,1)S(1)}, u32[]{:S(2)}, u32[]{:S(2)}) %collective-permute-start.23) | collective-permute-done | bytes 98336 | tf_op jit(solution)/shard_map/ppermute | solution.py:275
  84.3 1.9 %shard_map.98 = (bf16[512,1024]{1,0:T(8,128)(2,1)}, bf16[512,1024]{1,0:T(8,128)(2,1)}) custom-call(bf16[512,1024]{1,0:T(8,128)(2,1)S(1)} %copy-done, bf16[512,1024]{1,0:T(8,128)(2,1)S(1)} %copy-done.1, f32[256,1024]{1,0:T(8,128)S(1)} %get-tuple-element.105.refs_2_, f32[256,1024]{1,0:T(8,128)S(1)} %get-tuple-element.106.refs_3_, ...), custom_call_target="tpu_custom_call" | custom-call | flops 268435456 | bytes 9437184 | tf_op jit(solution)/shard_map/pallas_call | solution.py:95
  (53 shorter events, 7.7 us)
Async XLA Ops:
  0.6 6.9 %copy-start = (bf16[512,1024]{1,0:T(8,128)(2,1)S(1)}, bf16[512,1024]{1,0:T(8,128)(2,1)}, u32[]{:S(2)}) copy-start(bf16[512,1024]{1,0:T(8,128)(2,1)} %refs_0_.19) | copy-start | bytes 3145732
  0.6 6.9 %copy-start.1 = (bf16[512,1024]{1,0:T(8,128)(2,1)S(1)}, bf16[512,1024]{1,0:T(8,128)(2,1)}, u32[]{:S(2)}) copy-start(bf16[512,1024]{1,0:T(8,128)(2,1)} %refs_1_.17) | copy-start | bytes 3145732
  1.8 14.3 %collective-permute-start.3 = (bf16[256,768]{1,0:T(8,128)(2,1)S(1)}, bf16[256,768]{1,0:T(8,128)(2,1)S(1)}, u32[]{:S(2)}, u32[]{:S(2)}) collective-permute-start(bf16[256,768]{1,0:T(8,128)(2,1)S(1)} %slice.6), channel_id=1, source_target_pairs={{0,2},{2,4},{4,6},{6,8},{8,10},{10,12},{12,14},{14,16},{16,18},{18... | collective-permute-start | bytes 1179656 | tf_op jit(solution)/shard_map/ppermute | solution.py:280
  4.8 9.3 %collective-permute-start = (bf16[384,128]{1,0:T(8,128)(2,1)}, bf16[384,128]{1,0:T(8,128)(2,1)S(1)}, u32[]{:S(2)}, u32[]{:S(2)}) collective-permute-start(bf16[384,128]{1,0:T(8,128)(2,1)} %get-tuple-element.60), channel_id=1, source_target_pairs={{0,2},{2,0},{4,6},{6,4},{8,10},{10,8},{12,14},{14,12},{16,18},{18,... | collective-permute-start | bytes 294920 | tf_op jit(solution)/shard_map/ppermute | solution.py:275
  6.3 7.7 %collective-permute-start.1 = (bf16[384,128]{1,0:T(8,128)(2,1)}, bf16[384,128]{1,0:T(8,128)(2,1)S(1)}, u32[]{:S(2)}, u32[]{:S(2)}) collective-permute-start(bf16[384,128]{1,0:T(8,128)(2,1)} %get-tuple-element.61), channel_id=1, source_target_pairs={{0,4},{2,6},{4,0},{6,2},{8,12},{10,14},{12,8},{14,10},{16,20},{18,... | collective-permute-start | bytes 294920 | tf_op jit(solution)/shard_map/ppermute | solution.py:275
  6.5 9.6 %collective-permute-start.2 = (bf16[384,128]{1,0:T(8,128)(2,1)}, bf16[384,128]{1,0:T(8,128)(2,1)S(1)}, u32[]{:S(2)}, u32[]{:S(2)}) collective-permute-start(bf16[384,128]{1,0:T(8,128)(2,1)} %get-tuple-element.62), channel_id=1, source_target_pairs={{0,6},{2,4},{4,2},{6,0},{8,14},{10,12},{12,10},{14,8},{16,22},{18,... | collective-permute-start | bytes 294920 | tf_op jit(solution)/shard_map/ppermute | solution.py:275
  7.6 1.2 %copy-start.2 = (bf16[512,1024]{1,0:T(8,128)(2,1)S(1)}, bf16[512,1024]{1,0:T(8,128)(2,1)}, u32[]{:S(2)}) copy-start(bf16[512,1024]{1,0:T(8,128)(2,1)} %refs_0_.17) | copy-start | bytes 3145732
  9.7 6.5 %copy-start.5 = (bf16[256,768]{1,0:T(8,128)(2,1)S(1)}, bf16[256,768]{1,0:T(8,128)(2,1)}, u32[]{:S(2)}) copy-start(bf16[256,768]{1,0:T(8,128)(2,1)} %get-tuple-element.63.refs_4_) | copy-start | bytes 1179652
  9.7 6.5 %copy-start.7 = (bf16[512,256]{1,0:T(8,128)(2,1)S(1)}, bf16[512,256]{1,0:T(8,128)(2,1)}, u32[]{:S(2)}) copy-start(bf16[512,256]{1,0:T(8,128)(2,1)} %get-tuple-element.64.refs_5_) | copy-start | bytes 786436
  11.8 9.1 %copy-start.8 = (bf16[1024]{0:T(1024)(128)(2,1)S(1)}, bf16[1024]{0:T(1024)(128)(2,1)}, u32[]{:S(2)}) copy-start(bf16[1024]{0:T(1024)(128)(2,1)} %param.8) | copy-start | bytes 6148
  11.8 12.4 %copy-start.3 = (bf16[512,1024]{1,0:T(8,128)(2,1)S(1)}, bf16[512,1024]{1,0:T(8,128)(2,1)}, u32[]{:S(2)}) copy-start(bf16[512,1024]{1,0:T(8,128)(2,1)} %refs_0_.17) | copy-start | bytes 3145732
  16.2 16.4 %collective-permute-start.10 = (bf16[256,768]{1,0:T(8,128)(2,1)S(1)}, bf16[256,768]{1,0:T(8,128)(2,1)S(1)}, u32[]{:S(2)}, u32[]{:S(2)}) collective-permute-start(bf16[256,768]{1,0:T(8,128)(2,1)S(1)} %get-tuple-element.72), channel_id=1, source_target_pairs={{0,2},{2,4},{4,6},{6,8},{8,10},{10,12},{12,14},{14,16},{16,18},{18... | collective-permute-start | bytes 1179656 | tf_op jit(solution)/shard_map/ppermute | solution.py:280
  20.9 5.5 %collective-permute-start.6 = (bf16[384,128]{1,0:T(8,128)(2,1)S(1)}, bf16[384,128]{1,0:T(8,128)(2,1)S(1)}, u32[]{:S(2)}, u32[]{:S(2)}) collective-permute-start(bf16[384,128]{1,0:T(8,128)(2,1)S(1)} %get-tuple-element.66.refs_3_), channel_id=1, source_target_pairs={{0,24},{2,26},{4,28},{1,25},{3,27},{5,29}} | collective-permute-start | bytes 294920 | tf_op jit(solution)/shard_map/ppermute | solution.py:285
  21.6 4.8 %collective-permute-start.5 = (bf16[384,128]{1,0:T(8,128)(2,1)S(1)}, bf16[384,128]{1,0:T(8,128)(2,1)S(1)}, u32[]{:S(2)}, u32[]{:S(2)}) collective-permute-start(bf16[384,128]{1,0:T(8,128)(2,1)S(1)} %get-tuple-element.66.refs_3_), channel_id=1, source_target_pairs={{0,16},{2,18},{4,20},{8,24},{10,26},{12,28},{1,17},{3,19},{5,21},{... | collective-permute-start | bytes 294920 | tf_op jit(solution)/shard_map/ppermute | solution.py:285
  22.3 4.1 %collective-permute-start.4 = (bf16[384,128]{1,0:T(8,128)(2,1)S(1)}, bf16[384,128]{1,0:T(8,128)(2,1)S(1)}, u32[]{:S(2)}, u32[]{:S(2)}) collective-permute-start(bf16[384,128]{1,0:T(8,128)(2,1)S(1)} %get-tuple-element.66.refs_3_), channel_id=1, source_target_pairs={{0,8},{2,10},{4,12},{8,16},{10,18},{12,20},{16,24},{18,26},{20,28}... | collective-permute-start | bytes 294920 | tf_op jit(solution)/shard_map/ppermute | solution.py:285
  22.9 12.5 %collective-permute-start.11 = (bf16[512,256]{1,0:T(8,128)(2,1)S(1)}, bf16[512,256]{1,0:T(8,128)(2,1)S(1)}, u32[]{:S(2)}, u32[]{:S(2)}) collective-permute-start(bf16[512,256]{1,0:T(8,128)(2,1)S(1)} %get-tuple-element.74), channel_id=1, source_target_pairs={{0,2},{2,4},{4,6},{6,8},{8,10},{10,12},{12,14},{14,16},{16,18},{18... | collective-permute-start | bytes 786440 | tf_op jit(solution)/shard_map/ppermute | solution.py:285
  26.7 10.0 %collective-permute-start.7 = (bf16[384,128]{1,0:T(8,128)(2,1)S(1)}, bf16[384,128]{1,0:T(8,128)(2,1)S(1)}, u32[]{:S(2)}, u32[]{:S(2)}) collective-permute-start(bf16[384,128]{1,0:T(8,128)(2,1)S(1)} %get-tuple-element.69), channel_id=1, source_target_pairs={{0,2},{2,0},{4,6},{6,4},{8,10},{10,8},{12,14},{14,12},{16,18},{18,... | collective-permute-start | bytes 294920 | tf_op jit(solution)/shard_map/ppermute | solution.py:275
  30.6 6.1 %collective-permute-start.8 = (bf16[384,128]{1,0:T(8,128)(2,1)S(1)}, bf16[384,128]{1,0:T(8,128)(2,1)S(1)}, u32[]{:S(2)}, u32[]{:S(2)}) collective-permute-start(bf16[384,128]{1,0:T(8,128)(2,1)S(1)} %get-tuple-element.70), channel_id=1, source_target_pairs={{0,4},{2,6},{4,0},{6,2},{8,12},{10,14},{12,8},{14,10},{16,20},{18,... | collective-permute-start | bytes 294920 | tf_op jit(solution)/shard_map/ppermute | solution.py:275
  32.5 6.4 %collective-permute-start.9 = (bf16[384,128]{1,0:T(8,128)(2,1)S(1)}, bf16[384,128]{1,0:T(8,128)(2,1)S(1)}, u32[]{:S(2)}, u32[]{:S(2)}) collective-permute-start(bf16[384,128]{1,0:T(8,128)(2,1)S(1)} %get-tuple-element.71), channel_id=1, source_target_pairs={{0,6},{2,4},{4,2},{6,0},{8,14},{10,12},{12,10},{14,8},{16,22},{18,... | collective-permute-start | bytes 294920 | tf_op jit(solution)/shard_map/ppermute | solution.py:275
  35.5 3.4 %copy-start.4 = (bf16[512,1024]{1,0:T(8,128)(2,1)S(1)}, bf16[512,1024]{1,0:T(8,128)(2,1)}, u32[]{:S(2)}) copy-start(bf16[512,1024]{1,0:T(8,128)(2,1)} %refs_3_.1) | copy-start | bytes 3145732
  39.9 19.1 %collective-permute-start.16 = (bf16[192,1024]{1,0:T(8,128)(2,1)S(1)}, bf16[192,1024]{1,0:T(8,128)(2,1)S(1)}, u32[]{:S(2)}, u32[]{:S(2)}) collective-permute-start(bf16[192,1024]{1,0:T(8,128)(2,1)S(1)} %get-tuple-element.98), channel_id=1, source_target_pairs={{0,30},{2,0},{4,2},{6,4},{8,6},{10,8},{12,10},{14,12},{16,14},{18,... | collective-permute-start | bytes 1179656 | tf_op jit(solution)/shard_map/ppermute | solution.py:280
  40.2 2.0 %collective-permute-start.12 = (f32[8,512]{1,0:T(8,128)S(1)}, f32[8,512]{1,0:T(8,128)S(1)}, u32[]{:S(2)}, u32[]{:S(2)}) collective-permute-start(f32[8,512]{1,0:T(8,128)S(1)} %get-tuple-element.77), channel_id=1, source_target_pairs={{0,1},{1,0},{2,3},{3,2},{4,5},{5,4},{6,7},{7,6},{8,9},{9,8},{10,11... | collective-permute-start | bytes 49160 | tf_op jit(solution)/shard_map/ppermute | solution.py:713
  44.6 7.4 %collective-permute-start.13 = (bf16[384,128]{1,0:T(8,128)(2,1)S(1)}, bf16[384,128]{1,0:T(8,128)(2,1)S(1)}, u32[]{:S(2)}, u32[]{:S(2)}) collective-permute-start(bf16[384,128]{1,0:T(8,128)(2,1)S(1)} %get-tuple-element.94), channel_id=1, source_target_pairs={{0,2},{2,0},{4,6},{6,4},{8,10},{10,8},{12,14},{14,12},{16,18},{18,... | collective-permute-start | bytes 294920 | tf_op jit(solution)/shard_map/ppermute | solution.py:275
  46.0 10.9 %collective-permute-start.14 = (bf16[384,128]{1,0:T(8,128)(2,1)S(1)}, bf16[384,128]{1,0:T(8,128)(2,1)S(1)}, u32[]{:S(2)}, u32[]{:S(2)}) collective-permute-start(bf16[384,128]{1,0:T(8,128)(2,1)S(1)} %get-tuple-element.95), channel_id=1, source_target_pairs={{0,4},{2,6},{4,0},{6,2},{8,12},{10,14},{12,8},{14,10},{16,20},{18,... | collective-permute-start | bytes 294920 | tf_op jit(solution)/shard_map/ppermute | solution.py:275
  48.8 10.3 %collective-permute-start.15 = (bf16[384,128]{1,0:T(8,128)(2,1)S(1)}, bf16[384,128]{1,0:T(8,128)(2,1)S(1)}, u32[]{:S(2)}, u32[]{:S(2)}) collective-permute-start(bf16[384,128]{1,0:T(8,128)(2,1)S(1)} %get-tuple-element.96), channel_id=1, source_target_pairs={{0,6},{2,4},{4,2},{6,0},{8,14},{10,12},{12,10},{14,8},{16,22},{18,... | collective-permute-start | bytes 294920 | tf_op jit(solution)/shard_map/ppermute | solution.py:275
  59.1 20.2 %collective-permute-start.17 = (bf16[336,1024]{1,0:T(8,128)(2,1)S(1)}, bf16[336,1024]{1,0:T(8,128)(2,1)S(1)}, u32[]{:S(2)}, u32[]{:S(2)}) collective-permute-start(bf16[336,1024]{1,0:T(8,128)(2,1)S(1)} %get-tuple-element.102), channel_id=1, source_target_pairs={{0,30},{2,0},{4,2},{6,4},{8,6},{10,8},{12,10},{14,12},{16,14},{18,... | collective-permute-start | bytes 2064392 | tf_op jit(solution)/shard_map/ppermute | solution.py:280
  59.2 9.7 %collective-permute-start.20 = (bf16[384,128]{1,0:T(8,128)(2,1)S(1)}, bf16[384,128]{1,0:T(8,128)(2,1)S(1)}, u32[]{:S(2)}, u32[]{:S(2)}) collective-permute-start(bf16[384,128]{1,0:T(8,128)(2,1)S(1)} %get-tuple-element.100.refs_18_), channel_id=1, source_target_pairs={{26,2},{28,4},{30,6},{27,3},{29,5},{31,7}} | collective-permute-start | bytes 294920 | tf_op jit(solution)/shard_map/ppermute | solution.py:285
  61.1 7.8 %collective-permute-start.19 = (bf16[384,128]{1,0:T(8,128)(2,1)S(1)}, bf16[384,128]{1,0:T(8,128)(2,1)S(1)}, u32[]{:S(2)}, u32[]{:S(2)}) collective-permute-start(bf16[384,128]{1,0:T(8,128)(2,1)S(1)} %get-tuple-element.100.refs_18_), channel_id=1, source_target_pairs={{18,2},{20,4},{22,6},{26,10},{28,12},{30,14},{19,3},{21,5},{23,7},... | collective-permute-start | bytes 294920 | tf_op jit(solution)/shard_map/ppermute | solution.py:285
  62.4 6.5 %collective-permute-start.18 = (bf16[384,128]{1,0:T(8,128)(2,1)S(1)}, bf16[384,128]{1,0:T(8,128)(2,1)S(1)}, u32[]{:S(2)}, u32[]{:S(2)}) collective-permute-start(bf16[384,128]{1,0:T(8,128)(2,1)S(1)} %get-tuple-element.100.refs_18_), channel_id=1, source_target_pairs={{10,2},{12,4},{14,6},{18,10},{20,12},{22,14},{26,18},{28,20},{30,2... | collective-permute-start | bytes 294920 | tf_op jit(solution)/shard_map/ppermute | solution.py:285
  69.2 12.0 %collective-permute-start.21 = (bf16[384,128]{1,0:T(8,128)(2,1)S(1)}, bf16[384,128]{1,0:T(8,128)(2,1)S(1)}, u32[]{:S(2)}, u32[]{:S(2)}) collective-permute-start(bf16[384,128]{1,0:T(8,128)(2,1)S(1)} %get-tuple-element.107), channel_id=1, source_target_pairs={{0,2},{2,0},{4,6},{6,4},{8,10},{10,8},{12,14},{14,12},{16,18},{18,... | collective-permute-start | bytes 294920 | tf_op jit(solution)/shard_map/ppermute | solution.py:275
  69.3 13.0 %collective-permute-start.22 = (bf16[384,128]{1,0:T(8,128)(2,1)S(1)}, bf16[384,128]{1,0:T(8,128)(2,1)S(1)}, u32[]{:S(2)}, u32[]{:S(2)}) collective-permute-start(bf16[384,128]{1,0:T(8,128)(2,1)S(1)} %get-tuple-element.108), channel_id=1, source_target_pairs={{0,4},{2,6},{4,0},{6,2},{8,12},{10,14},{12,8},{14,10},{16,20},{18,... | collective-permute-start | bytes 294920 | tf_op jit(solution)/shard_map/ppermute | solution.py:275
  69.4 14.9 %collective-permute-start.23 = (bf16[384,128]{1,0:T(8,128)(2,1)S(1)}, bf16[384,128]{1,0:T(8,128)(2,1)S(1)}, u32[]{:S(2)}, u32[]{:S(2)}) collective-permute-start(bf16[384,128]{1,0:T(8,128)(2,1)S(1)} %get-tuple-element.109), channel_id=1, source_target_pairs={{0,6},{2,4},{4,2},{6,0},{8,14},{10,12},{12,10},{14,8},{16,22},{18,... | collective-permute-start | bytes 294920 | tf_op jit(solution)/shard_map/ppermute | solution.py:275
  (1 other events, 0.9 us)

commit v5 on v4

--- a/solution.py
+++ b/solution.py
@@ -143,30 +143,28 @@
     return pl.BlockSpec(shape, lambda *_: (0,) * len(shape))
 
 
-def heads_a_part(heads):
-    return -(-heads // HOLDERS)
-
-
 def part_shape(heads):
-    return (heads_a_part(heads) * HEAD_DIM, HEAD_DIM)
-
-
-def part_at(held, head, reverse):
-    each = held.shape[1] // HEAD_DIM
-    at = lax.rem(head, each) * HEAD_DIM
-    if not isinstance(at, int):
-        at = pl.multiple_of(at, HEAD_DIM)
-    return head // each + (GROUP - HOLDERS if reverse else 0), pl.ds(at, HEAD_DIM)
+    return (-(-heads * HEAD_DIM // (HOLDERS * 16)) * 16, HEAD_DIM)
+
+
+def spans(held, head, reverse):
+    rows = held.shape[1]
+    first, last = head * HEAD_DIM, (head + 1) * HEAD_DIM
+    at = first
+    while at < last:
+        count = min(last, (at // rows + 1) * rows) - at
+        yield at // rows + (GROUP - HOLDERS if reverse else 0), at % rows, at - first, count
+        at += count
 
 
 def store_state(held, head, state, reverse):
-    slot, rows = part_at(held, head, reverse)
-    held[slot, rows, :] = state
+    for slot, at, start, count in spans(held, head, reverse):
+        held[slot, at : at + count, :] = state[start : start + count]
 
 
 def held_state(held, head, reverse):
-    slot, rows = part_at(held, head, reverse)
-    return held[slot, rows, :]
+    pieces = [held[slot, at : at + count, :] for slot, at, _, count in spans(held, head, reverse)]
+    return pieces[0] if len(pieces) == 1 else jnp.concatenate(pieces, 0)
 
 
 def spread(held, outs):

time: 86.8 us -> 85.5 us (0.985)
  the two profiles are of different devices: /device:TPU:31 before, /device:TPU:0 now
where the time goes in v5:
time: 85.5 us; the launch traced here: 83.9 us
  starting transfers between devices  38.8 us (45%)
  Pallas kernels  26.6 us (31%)
  waiting for transfers between devices  14 us (16%)
  local copies, waits for them, and re-layouts  3.37 us (4%)
  between operations  1.19 us (1%)
    pallas_call x15, Pallas kernels, call(): pl.pallas_call(run, grid=grid, input_output_aliases={**(aliases or {}), *...  26.6 us
    ppermute x12, starting transfers between devices, swap(): return lax.ppermute(value, 'ctx', [(at, at ^ mask) for at in range(count)])  14.2 us
    ppermute x7, starting transfers between devices, shift(): lax.ppermute(value, 'ctx', [(at, at + steps) for at in range(count) if at...  13.5 us
    ppermute x4, starting transfers between devices, turn(): lax.ppermute(value, 'ctx', [(at, (at + steps) % count) for at in range(co...  11.1 us
    ppermute x12, waiting for transfers between devices, swap(): return lax.ppermute(value, 'ctx', [(at, at ^ mask) for at in range(count)])  8.12 us
    ppermute x4, waiting for transfers between devices, turn(): lax.ppermute(value, 'ctx', [(at, (at + steps) % count) for at in range(co...  4.65 us
    unnamed x20, local copies, waits for them, and re-layouts  2.17 us
  transfers between devices with their start and end apart: 24, of which 6 were waited for; matrix products, arithmetic and copies ran while one was open for 0% of the time, Pallas kernels for 28%

profile of v5, /device:TPU:0, one launch (start us, length us, event | category | flops | bytes accessed | tf_op | source)
XLA Modules:
  0.0 83.9 jit_solution(14782490678815546135)
XLA Ops:
  0.7 1.2 %slice.6 = bf16[256,768]{1,0:T(8,128)(2,1)S(1)} slice(bf16[512,1024]{1,0:T(8,128)(2,1)} %refs_0_.19), slice={[256:512], [0:768]} | slice | bytes 786432 | tf_op jit(solution)/shard_map/slice | solution.py:724
  1.8 3.0 %collective-permute-start.3 = (bf16[256,768]{1,0:T(8,128)(2,1)S(1)}, bf16[256,768]{1,0:T(8,128)(2,1)S(1)}, u32[]{:S(2)}, u32[]{:S(2)}) collective-permute-start(bf16[256,768]{1,0:T(8,128)(2,1)S(1)} %slice.6), channel_id=1, source_target_pairs={{0,2},{2,4},{4,6},{6,8},{8,10},{10,12},{12,14},{14,16},{16,18},{18... | collective-permute-start | bytes 1179656 | tf_op jit(solution)/shard_map/ppermute | solution.py:278
  4.8 2.8 %shard_map.84 = (bf16[352,128]{1,0:T(8,128)(2,1)}, bf16[352,128]{1,0:T(8,128)(2,1)}, bf16[352,128]{1,0:T(8,128)(2,1)}, bf16[352,128]{1,0:T(8,128)(2,1)}, bf16[25...) custom-call(bf16[512,1024]{1,0:T(8,128)(2,1)} %refs_0_.19, bf16[512,1024]{1,0:T(8,128)(2,1)} %refs_1_.17), custom_call_target="tpu_custom_call" | custom-call | flops 134217728 | bytes 2097152 | tf_op jit(solution)/shard_map/pallas_call | solution.py:95
  7.7 1.6 %collective-permute-start = (bf16[352,128]{1,0:T(8,128)(2,1)}, bf16[352,128]{1,0:T(8,128)(2,1)S(1)}, u32[]{:S(2)}, u32[]{:S(2)}) collective-permute-start(bf16[352,128]{1,0:T(8,128)(2,1)} %get-tuple-element.60), channel_id=1, source_target_pairs={{0,2},{2,0},{4,6},{6,4},{8,10},{10,8},{12,14},{14,12},{16,18},{18,... | collective-permute-start | bytes 270344 | tf_op jit(solution)/shard_map/ppermute | solution.py:273
  9.2 1.5 %collective-permute-start.1 = (bf16[352,128]{1,0:T(8,128)(2,1)}, bf16[352,128]{1,0:T(8,128)(2,1)S(1)}, u32[]{:S(2)}, u32[]{:S(2)}) collective-permute-start(bf16[352,128]{1,0:T(8,128)(2,1)} %get-tuple-element.61), channel_id=1, source_target_pairs={{0,4},{2,6},{4,0},{6,2},{8,12},{10,14},{12,8},{14,10},{16,20},{18,... | collective-permute-start | bytes 270344 | tf_op jit(solution)/shard_map/ppermute | solution.py:273
  11.2 1.2 %copy-done.2 = bf16[512,1024]{1,0:T(8,128)(2,1)S(1)} copy-done((bf16[512,1024]{1,0:T(8,128)(2,1)S(1)}, bf16[512,1024]{1,0:T(8,128)(2,1)}, u32[]{:S(2)}) %copy-start.2) | copy-done | bytes 1048600
  13.4 2.1 %shard_map.85 = (bf16[4,2,256,256]{3,2,1,0:T(8,128)(2,1)S(1)}, bf16[4,2,256,256]{3,2,1,0:T(8,128)(2,1)S(1)}, f32[256,512]{1,0:T(8,128)S(1)}) custom-call(bf16[512,1024]{1,0:T(8,128)(2,1)S(1)} %copy-done.2, bf16[512,1024]{1,0:T(8,128)(2,1)S(1)} %copy-done, bf16[512,1024]{1,0:T(8,128)(2,1)S(1)} %copy-done.1, bf16[352,128]{1,0:T(8,128)(2,1)S(1)} %copy-done.6), custom_call_target="tpu_custom_call" | custom-call | flops 1073741824 | bytes 3145728 | tf_op jit(solution)/shard_map/pallas_call | solution.py:95
  15.5 2.6 %collective-permute-done.refs_1_.refs_4_ = bf16[352,128]{1,0:T(8,128)(2,1)S(1)} collective-permute-done((bf16[352,128]{1,0:T(8,128)(2,1)}, bf16[352,128]{1,0:T(8,128)(2,1)S(1)}, u32[]{:S(2)}, u32[]{:S(2)}) %collective-permute-start) | collective-permute-done | bytes 90144 | tf_op jit(solution)/shard_map/ppermute | solution.py:273
  18.1 1.9 %collective-permute-done.1.refs_2_.refs_5_ = bf16[352,128]{1,0:T(8,128)(2,1)S(1)} collective-permute-done((bf16[352,128]{1,0:T(8,128)(2,1)}, bf16[352,128]{1,0:T(8,128)(2,1)S(1)}, u32[]{:S(2)}, u32[]{:S(2)}) %collective-permute-start.1) | collective-permute-done | bytes 90144 | tf_op jit(solution)/shard_map/ppermute | solution.py:273
  20.0 1.8 %collective-permute-done.2.refs_3_.refs_6_ = bf16[352,128]{1,0:T(8,128)(2,1)S(1)} collective-permute-done((bf16[352,128]{1,0:T(8,128)(2,1)}, bf16[352,128]{1,0:T(8,128)(2,1)S(1)}, u32[]{:S(2)}, u32[]{:S(2)}) %collective-permute-start.2) | collective-permute-done | bytes 90144 | tf_op jit(solution)/shard_map/ppermute | solution.py:273
  22.0 4.2 %collective-permute-start.6 = (bf16[352,128]{1,0:T(8,128)(2,1)S(1)}, bf16[352,128]{1,0:T(8,128)(2,1)S(1)}, u32[]{:S(2)}, u32[]{:S(2)}) collective-permute-start(bf16[352,128]{1,0:T(8,128)(2,1)S(1)} %get-tuple-element.66.refs_3_), channel_id=1, source_target_pairs={{0,24},{2,26},{4,28},{1,25},{3,27},{5,29}} | collective-permute-start | bytes 270344 | tf_op jit(solution)/shard_map/ppermute | solution.py:283
  26.2 1.3 %collective-permute-start.5 = (bf16[352,128]{1,0:T(8,128)(2,1)S(1)}, bf16[352,128]{1,0:T(8,128)(2,1)S(1)}, u32[]{:S(2)}, u32[]{:S(2)}) collective-permute-start(bf16[352,128]{1,0:T(8,128)(2,1)S(1)} %get-tuple-element.66.refs_3_), channel_id=1, source_target_pairs={{0,16},{2,18},{4,20},{8,24},{10,26},{12,28},{1,17},{3,19},{5,21},{... | collective-permute-start | bytes 270344 | tf_op jit(solution)/shard_map/ppermute | solution.py:283
  27.5 2.5 %collective-permute-start.4 = (bf16[352,128]{1,0:T(8,128)(2,1)S(1)}, bf16[352,128]{1,0:T(8,128)(2,1)S(1)}, u32[]{:S(2)}, u32[]{:S(2)}) collective-permute-start(bf16[352,128]{1,0:T(8,128)(2,1)S(1)} %get-tuple-element.66.refs_3_), channel_id=1, source_target_pairs={{0,8},{2,10},{4,12},{8,16},{10,18},{12,20},{16,24},{18,26},{20,28}... | collective-permute-start | bytes 270344 | tf_op jit(solution)/shard_map/ppermute | solution.py:283
  30.0 3.4 %collective-permute-start.11 = (bf16[512,256]{1,0:T(8,128)(2,1)S(1)}, bf16[512,256]{1,0:T(8,128)(2,1)S(1)}, u32[]{:S(2)}, u32[]{:S(2)}) collective-permute-start(bf16[512,256]{1,0:T(8,128)(2,1)S(1)} %get-tuple-element.74), channel_id=1, source_target_pairs={{0,2},{2,4},{4,6},{6,8},{8,10},{10,12},{12,14},{14,16},{16,18},{18... | collective-permute-start | bytes 786440 | tf_op jit(solution)/shard_map/ppermute | solution.py:283
  33.4 2.1 %shard_map.87 = (bf16[4,2,256,256]{3,2,1,0:T(8,128)(2,1)S(1)}, bf16[4,2,256,256]{3,2,1,0:T(8,128)(2,1)S(1)}, f32[256,512]{1,0:T(8,128)S(1)}) custom-call(bf16[512,1024]{1,0:T(8,128)(2,1)S(1)} %copy-done.3, bf16[512,1024]{1,0:T(8,128)(2,1)S(1)} %copy-done, bf16[512,1024]{1,0:T(8,128)(2,1)S(1)} %copy-done.1, bf16[352,128]{1,0:T(8,128)(2,1)S(1)} %get-tuple-element.66.refs_3_), custom_call_target="tpu_custom_call" | custom-call | flops 1073741824 | bytes 3145728 | tf_op jit(solution)/shard_map/pallas_call | solution.py:95
  37.4 2.0 %collective-permute-start.9 = (bf16[352,128]{1,0:T(8,128)(2,1)S(1)}, bf16[352,128]{1,0:T(8,128)(2,1)S(1)}, u32[]{:S(2)}, u32[]{:S(2)}) collective-permute-start(bf16[352,128]{1,0:T(8,128)(2,1)S(1)} %get-tuple-element.71), channel_id=1, source_target_pairs={{0,6},{2,4},{4,2},{6,0},{8,14},{10,12},{12,10},{14,8},{16,22},{18,... | collective-permute-start | bytes 270344 | tf_op jit(solution)/shard_map/ppermute | solution.py:273
  39.4 2.9 %shard_map.89 = (bf16[6,2,256,256]{3,2,1,0:T(8,128)(2,1)S(1)}, bf16[6,256,256]{2,1,0:T(8,128)(2,1)S(1)}, f32[256,768]{1,0:T(8,128)S(1)}, f32[256,768]{1,0:T(8,128)S(1)}, f32[8,256]{1,0:T(8,128)S(1)}) custom-call(bf16[512,1024]{1,0:T(8,128)(2,1)S(1)} %copy-done.3, bf16[512,1024]{1,0:T(8,128)(2,1)S(1)} %copy-done, bf16[512,1024]{1,0:T(8,128)(2,1)S(1)} %copy-done.1, ...), custom_call_target="tpu_custom_call" | custom-call | flops 2013265920 | bytes 4718592 | tf_op jit(solution)/shard_map/pallas_call | solution.py:95
  42.3 1.1 %shard_map.90 = (bf16[2,2,256,256]{3,2,1,0:T(8,128)(2,1)S(1)}, bf16[2,256,256]{2,1,0:T(8,128)(2,1)S(1)}, f32[256,256]{1,0:T(8,128)S(1)}, f32[256,256]{1,0:T(8,128)S(1)}, f32[8,256]{1,0:T(8,128)S(1)}) custom-call(bf16[512,1024]{1,0:T(8,128)(2,1)S(1)} %copy-done.3, bf16[512,1024]{1,0:T(8,128)(2,1)S(1)} %copy-done, bf16[512,1024]{1,0:T(8,128)(2,1)S(1)} %copy-done.1, ...), custom_call_target="tpu_custom_call" | custom-call | flops 671088640 | bytes 1572864 | tf_op jit(solution)/shard_map/pallas_call | solution.py:95
  43.5 1.1 %shard_map.91 = (f32[512,1024]{1,0:T(8,128)S(1)}, f32[8,512]{1,0:T(8,128)S(1)}, bf16[192,1024]{1,0:T(8,128)(2,1)S(1)}) custom-call(bf16[512,1024]{1,0:T(8,128)(2,1)S(1)} %copy-done.3, bf16[1,1024]{1,0:T(2,128)(2,1)S(1)} %reshape.11.refs_1_.refs_2_, bf16[512,1024]{1,0:T(8,128)(2,1)S(1)} %copy-done.4, ...), custom_call_target="tpu_custom_call", output_to_operand_aliasing={{2}: (11, {})} | custom-call | flops 134217728 | bytes 6291456 | tf_op jit(solution)/shard_map/pallas_call | solution.py:95
  44.7 1.6 %collective-permute-start.16 = (bf16[192,1024]{1,0:T(8,128)(2,1)S(1)}, bf16[192,1024]{1,0:T(8,128)(2,1)S(1)}, u32[]{:S(2)}, u32[]{:S(2)}) collective-permute-start(bf16[192,1024]{1,0:T(8,128)(2,1)S(1)} %get-tuple-element.98), channel_id=1, source_target_pairs={{0,30},{2,0},{4,2},{6,4},{8,6},{10,8},{12,10},{14,12},{16,14},{18,... | collective-permute-start | bytes 1179656 | tf_op jit(solution)/shard_map/ppermute | solution.py:278
  46.3 1.2 %collective-permute-done.12 = f32[8,512]{1,0:T(8,128)S(1)} collective-permute-done((f32[8,512]{1,0:T(8,128)S(1)}, f32[8,512]{1,0:T(8,128)S(1)}, u32[]{:S(2)}, u32[]{:S(2)}) %collective-permute-start.12) | collective-permute-done | bytes 16416 | tf_op jit(solution)/shard_map/ppermute | solution.py:711
  47.4 2.3 %shard_map.92 = (bf16[512,1024]{1,0:T(8,128)(2,1)}, bf16[512,1024]{1,0:T(8,128)(2,1)S(1)}, bf16[336,1024]{1,0:T(8,128)(2,1)S(1)}, bf16[352,128]{1,0:T(8,128)(2,1...) custom-call(f32[8,512]{1,0:T(8,128)S(1)} %add.3.refs_0_, ...), custom_call_target="tpu_custom_call" | custom-call | flops 134217728 | bytes 7340032 | tf_op jit(solution)/shard_map/pallas_call | solution.py:95
  50.8 2.5 %collective-permute-start.15 = (bf16[352,128]{1,0:T(8,128)(2,1)S(1)}, bf16[352,128]{1,0:T(8,128)(2,1)S(1)}, u32[]{:S(2)}, u32[]{:S(2)}) collective-permute-start(bf16[352,128]{1,0:T(8,128)(2,1)S(1)} %get-tuple-element.96), channel_id=1, source_target_pairs={{0,6},{2,4},{4,2},{6,0},{8,14},{10,12},{12,10},{14,8},{16,22},{18,... | collective-permute-start | bytes 270344 | tf_op jit(solution)/shard_map/ppermute | solution.py:273
  53.3 3.3 %shard_map.93 = (bf16[512,512]{1,0:T(8,128)(2,1)S(1)}, f32[512,512]{1,0:T(8,128)S(1)}, f32[512,512]{1,0:T(8,128)S(1)}) custom-call(bf16[512,1024]{1,0:T(8,128)(2,1)S(1)} %copy-done.3, bf16[512,1024]{1,0:T(8,128)(2,1)S(1)} %copy-done, bf16[512,1024]{1,0:T(8,128)(2,1)S(1)} %copy-done.1, bf16[512,1024]{1,0:T(8,128)(2,1)S(1)} %get-tuple-element.83.refs_3_, ...), custom_call_target="tpu_custom_call" | custom-call | flops 2147483648 | bytes 10485760 | tf_op jit(solution)/shard_map/pallas_call | solution.py:95
  56.6 1.8 %collective-permute-done.15.refs_3_.refs_6_ = bf16[352,128]{1,0:T(8,128)(2,1)S(1)} collective-permute-done((bf16[352,128]{1,0:T(8,128)(2,1)S(1)}, bf16[352,128]{1,0:T(8,128)(2,1)S(1)}, u32[]{:S(2)}, u32[]{:S(2)}) %collective-permute-start.15) | collective-permute-done | bytes 90144 | tf_op jit(solution)/shard_map/ppermute | solution.py:273
  58.5 6.4 %collective-permute-start.17 = (bf16[336,1024]{1,0:T(8,128)(2,1)S(1)}, bf16[336,1024]{1,0:T(8,128)(2,1)S(1)}, u32[]{:S(2)}, u32[]{:S(2)}) collective-permute-start(bf16[336,1024]{1,0:T(8,128)(2,1)S(1)} %get-tuple-element.102), channel_id=1, source_target_pairs={{0,30},{2,0},{4,2},{6,4},{8,6},{10,8},{12,10},{14,12},{16,14},{18,... | collective-permute-start | bytes 2064392 | tf_op jit(solution)/shard_map/ppermute | solution.py:278
  67.1 4.1 %shard_map.95 = (bf16[512,1024]{1,0:T(8,128)(2,1)}, f32[512,512]{1,0:T(8,128)S(1)}, f32[512,512]{1,0:T(8,128)S(1)}) custom-call(bf16[512,1024]{1,0:T(8,128)(2,1)S(1)} %copy-done.3, bf16[512,1024]{1,0:T(8,128)(2,1)S(1)} %copy-done, bf16[512,1024]{1,0:T(8,128)(2,1)S(1)} %copy-done.1, bf16[512,1024]{1,0:T(8,128)(2,1)S(1)} %get-tuple-element.83.refs_3_, ...), custom_call_target="tpu_custom_call" | custom-call | flops 2147483648 | bytes 10485760 | tf_op jit(solution)/shard_map/pallas_call | solution.py:95
  71.6 1.4 %collective-permute-start.21 = (bf16[352,128]{1,0:T(8,128)(2,1)S(1)}, bf16[352,128]{1,0:T(8,128)(2,1)S(1)}, u32[]{:S(2)}, u32[]{:S(2)}) collective-permute-start(bf16[352,128]{1,0:T(8,128)(2,1)S(1)} %get-tuple-element.107), channel_id=1, source_target_pairs={{0,2},{2,0},{4,6},{6,4},{8,10},{10,8},{12,14},{14,12},{16,18},{18,... | collective-permute-start | bytes 270344 | tf_op jit(solution)/shard_map/ppermute | solution.py:273
  73.0 2.1 %collective-permute-start.22 = (bf16[352,128]{1,0:T(8,128)(2,1)S(1)}, bf16[352,128]{1,0:T(8,128)(2,1)S(1)}, u32[]{:S(2)}, u32[]{:S(2)}) collective-permute-start(bf16[352,128]{1,0:T(8,128)(2,1)S(1)} %get-tuple-element.108), channel_id=1, source_target_pairs={{0,4},{2,6},{4,0},{6,2},{8,12},{10,14},{12,8},{14,10},{16,20},{18,... | collective-permute-start | bytes 270344 | tf_op jit(solution)/shard_map/ppermute | solution.py:273
  75.1 4.6 %collective-permute-done.17.refs_3_ = bf16[336,1024]{1,0:T(8,128)(2,1)S(1)} collective-permute-done((bf16[336,1024]{1,0:T(8,128)(2,1)S(1)}, bf16[336,1024]{1,0:T(8,128)(2,1)S(1)}, u32[]{:S(2)}, u32[]{:S(2)}) %collective-permute-start.17) | collective-permute-done | bytes 688160 | tf_op jit(solution)/shard_map/ppermute | solution.py:278
  79.8 2.0 %shard_map.97 = (f32[256,1024]{1,0:T(8,128)S(1)}, f32[256,1024]{1,0:T(8,128)S(1)}) custom-call(bf16[512,1024]{1,0:T(8,128)(2,1)S(1)} %copy-done, bf16[512,1024]{1,0:T(8,128)(2,1)S(1)} %copy-done.1, bf16[192,1024]{1,0:T(8,128)(2,1)S(1)} %collective-permute-done.16.refs_5_.refs_2_, bf16[336,1024]{1,0:T(8,128)(2,1)S(1)} %collective-permute-done.17.refs_3_, ...), custom_call_target="tpu_custom_call" | custom-call | flops 536870912 | bytes 3145728 | tf_op jit(solution)/shard_map/pallas_call | solution.py:95
  81.8 1.9 %shard_map.98 = (bf16[512,1024]{1,0:T(8,128)(2,1)}, bf16[512,1024]{1,0:T(8,128)(2,1)}) custom-call(bf16[512,1024]{1,0:T(8,128)(2,1)S(1)} %copy-done, bf16[512,1024]{1,0:T(8,128)(2,1)S(1)} %copy-done.1, f32[256,1024]{1,0:T(8,128)S(1)} %get-tuple-element.105.refs_2_, f32[256,1024]{1,0:T(8,128)S(1)} %get-tuple-element.106.refs_3_, ...), custom_call_target="tpu_custom_call" | custom-call | flops 268435456 | bytes 9437184 | tf_op jit(solution)/shard_map/pallas_call | solution.py:95
  (55 shorter events, 7.1 us)
Async XLA Ops:
  0.6 10.6 %copy-start = (bf16[512,1024]{1,0:T(8,128)(2,1)S(1)}, bf16[512,1024]{1,0:T(8,128)(2,1)}, u32[]{:S(2)}) copy-start(bf16[512,1024]{1,0:T(8,128)(2,1)} %refs_0_.19) | copy-start | bytes 3145732
  0.6 10.6 %copy-start.1 = (bf16[512,1024]{1,0:T(8,128)(2,1)S(1)}, bf16[512,1024]{1,0:T(8,128)(2,1)}, u32[]{:S(2)}) copy-start(bf16[512,1024]{1,0:T(8,128)(2,1)} %refs_1_.17) | copy-start | bytes 3145732
  1.8 20.0 %collective-permute-start.3 = (bf16[256,768]{1,0:T(8,128)(2,1)S(1)}, bf16[256,768]{1,0:T(8,128)(2,1)S(1)}, u32[]{:S(2)}, u32[]{:S(2)}) collective-permute-start(bf16[256,768]{1,0:T(8,128)(2,1)S(1)} %slice.6), channel_id=1, source_target_pairs={{0,2},{2,4},{4,6},{6,8},{8,10},{10,12},{12,14},{14,16},{16,18},{18... | collective-permute-start | bytes 1179656 | tf_op jit(solution)/shard_map/ppermute | solution.py:278
  7.7 10.4 %collective-permute-start = (bf16[352,128]{1,0:T(8,128)(2,1)}, bf16[352,128]{1,0:T(8,128)(2,1)S(1)}, u32[]{:S(2)}, u32[]{:S(2)}) collective-permute-start(bf16[352,128]{1,0:T(8,128)(2,1)} %get-tuple-element.60), channel_id=1, source_target_pairs={{0,2},{2,0},{4,6},{6,4},{8,10},{10,8},{12,14},{14,12},{16,18},{18,... | collective-permute-start | bytes 270344 | tf_op jit(solution)/shard_map/ppermute | solution.py:273
  9.2 10.7 %collective-permute-start.1 = (bf16[352,128]{1,0:T(8,128)(2,1)}, bf16[352,128]{1,0:T(8,128)(2,1)S(1)}, u32[]{:S(2)}, u32[]{:S(2)}) collective-permute-start(bf16[352,128]{1,0:T(8,128)(2,1)} %get-tuple-element.61), channel_id=1, source_target_pairs={{0,4},{2,6},{4,0},{6,2},{8,12},{10,14},{12,8},{14,10},{16,20},{18,... | collective-permute-start | bytes 270344 | tf_op jit(solution)/shard_map/ppermute | solution.py:273
  10.8 11.1 %collective-permute-start.2 = (bf16[352,128]{1,0:T(8,128)(2,1)}, bf16[352,128]{1,0:T(8,128)(2,1)S(1)}, u32[]{:S(2)}, u32[]{:S(2)}) collective-permute-start(bf16[352,128]{1,0:T(8,128)(2,1)} %get-tuple-element.62), channel_id=1, source_target_pairs={{0,6},{2,4},{4,2},{6,0},{8,14},{10,12},{12,10},{14,8},{16,22},{18,... | collective-permute-start | bytes 270344 | tf_op jit(solution)/shard_map/ppermute | solution.py:273
  13.3 8.5 %copy-start.5 = (bf16[256,768]{1,0:T(8,128)(2,1)S(1)}, bf16[256,768]{1,0:T(8,128)(2,1)}, u32[]{:S(2)}) copy-start(bf16[256,768]{1,0:T(8,128)(2,1)} %get-tuple-element.63.refs_4_) | copy-start | bytes 1179652
  13.4 8.5 %copy-start.7 = (bf16[352,128]{1,0:T(8,128)(2,1)S(1)}, bf16[352,128]{1,0:T(8,128)(2,1)}, u32[]{:S(2)}) copy-start(bf16[352,128]{1,0:T(8,128)(2,1)} %get-tuple-element.59.refs_3_.refs_0_) | copy-start | bytes 270340
  13.4 8.5 %copy-start.8 = (bf16[512,256]{1,0:T(8,128)(2,1)S(1)}, bf16[512,256]{1,0:T(8,128)(2,1)}, u32[]{:S(2)}) copy-start(bf16[512,256]{1,0:T(8,128)(2,1)} %get-tuple-element.64.refs_5_) | copy-start | bytes 786436
  15.5 6.5 %copy-start.9 = (bf16[1024]{0:T(1024)(128)(2,1)S(1)}, bf16[1024]{0:T(1024)(128)(2,1)}, u32[]{:S(2)}) copy-start(bf16[1024]{0:T(1024)(128)(2,1)} %param.8) | copy-start | bytes 6148
  15.5 17.9 %copy-start.3 = (bf16[512,1024]{1,0:T(8,128)(2,1)S(1)}, bf16[512,1024]{1,0:T(8,128)(2,1)}, u32[]{:S(2)}) copy-start(bf16[512,1024]{1,0:T(8,128)(2,1)} %refs_0_.17) | copy-start | bytes 3145732
  21.9 17.5 %collective-permute-start.10 = (bf16[256,768]{1,0:T(8,128)(2,1)S(1)}, bf16[256,768]{1,0:T(8,128)(2,1)S(1)}, u32[]{:S(2)}, u32[]{:S(2)}) collective-permute-start(bf16[256,768]{1,0:T(8,128)(2,1)S(1)} %get-tuple-element.72), channel_id=1, source_target_pairs={{0,2},{2,4},{4,6},{6,8},{8,10},{10,12},{12,14},{14,16},{16,18},{18... | collective-permute-start | bytes 1179656 | tf_op jit(solution)/shard_map/ppermute | solution.py:278
  22.0 13.5 %collective-permute-start.6 = (bf16[352,128]{1,0:T(8,128)(2,1)S(1)}, bf16[352,128]{1,0:T(8,128)(2,1)S(1)}, u32[]{:S(2)}, u32[]{:S(2)}) collective-permute-start(bf16[352,128]{1,0:T(8,128)(2,1)S(1)} %get-tuple-element.66.refs_3_), channel_id=1, source_target_pairs={{0,24},{2,26},{4,28},{1,25},{3,27},{5,29}} | collective-permute-start | bytes 270344 | tf_op jit(solution)/shard_map/ppermute | solution.py:283
  26.2 9.3 %collective-permute-start.5 = (bf16[352,128]{1,0:T(8,128)(2,1)S(1)}, bf16[352,128]{1,0:T(8,128)(2,1)S(1)}, u32[]{:S(2)}, u32[]{:S(2)}) collective-permute-start(bf16[352,128]{1,0:T(8,128)(2,1)S(1)} %get-tuple-element.66.refs_3_), channel_id=1, source_target_pairs={{0,16},{2,18},{4,20},{8,24},{10,26},{12,28},{1,17},{3,19},{5,21},{... | collective-permute-start | bytes 270344 | tf_op jit(solution)/shard_map/ppermute | solution.py:283
  27.5 8.1 %collective-permute-start.4 = (bf16[352,128]{1,0:T(8,128)(2,1)S(1)}, bf16[352,128]{1,0:T(8,128)(2,1)S(1)}, u32[]{:S(2)}, u32[]{:S(2)}) collective-permute-start(bf16[352,128]{1,0:T(8,128)(2,1)S(1)} %get-tuple-element.66.refs_3_), channel_id=1, source_target_pairs={{0,8},{2,10},{4,12},{8,16},{10,18},{12,20},{16,24},{18,26},{20,28}... | collective-permute-start | bytes 270344 | tf_op jit(solution)/shard_map/ppermute | solution.py:283
  30.0 12.4 %collective-permute-start.11 = (bf16[512,256]{1,0:T(8,128)(2,1)S(1)}, bf16[512,256]{1,0:T(8,128)(2,1)S(1)}, u32[]{:S(2)}, u32[]{:S(2)}) collective-permute-start(bf16[512,256]{1,0:T(8,128)(2,1)S(1)} %get-tuple-element.74), channel_id=1, source_target_pairs={{0,2},{2,4},{4,6},{6,8},{8,10},{10,12},{12,14},{14,16},{16,18},{18... | collective-permute-start | bytes 786440 | tf_op jit(solution)/shard_map/ppermute | solution.py:283
  35.9 7.6 %collective-permute-start.7 = (bf16[352,128]{1,0:T(8,128)(2,1)S(1)}, bf16[352,128]{1,0:T(8,128)(2,1)S(1)}, u32[]{:S(2)}, u32[]{:S(2)}) collective-permute-start(bf16[352,128]{1,0:T(8,128)(2,1)S(1)} %get-tuple-element.69), channel_id=1, source_target_pairs={{0,2},{2,0},{4,6},{6,4},{8,10},{10,8},{12,14},{14,12},{16,18},{18,... | collective-permute-start | bytes 270344 | tf_op jit(solution)/shard_map/ppermute | solution.py:273
  36.4 7.1 %collective-permute-start.8 = (bf16[352,128]{1,0:T(8,128)(2,1)S(1)}, bf16[352,128]{1,0:T(8,128)(2,1)S(1)}, u32[]{:S(2)}, u32[]{:S(2)}) collective-permute-start(bf16[352,128]{1,0:T(8,128)(2,1)S(1)} %get-tuple-element.70), channel_id=1, source_target_pairs={{0,4},{2,6},{4,0},{6,2},{8,12},{10,14},{12,8},{14,10},{16,20},{18,... | collective-permute-start | bytes 270344 | tf_op jit(solution)/shard_map/ppermute | solution.py:273
  37.4 6.2 %collective-permute-start.9 = (bf16[352,128]{1,0:T(8,128)(2,1)S(1)}, bf16[352,128]{1,0:T(8,128)(2,1)S(1)}, u32[]{:S(2)}, u32[]{:S(2)}) collective-permute-start(bf16[352,128]{1,0:T(8,128)(2,1)S(1)} %get-tuple-element.71), channel_id=1, source_target_pairs={{0,6},{2,4},{4,2},{6,0},{8,14},{10,12},{12,10},{14,8},{16,22},{18,... | collective-permute-start | bytes 270344 | tf_op jit(solution)/shard_map/ppermute | solution.py:273
  42.3 1.2 %copy-start.4 = (bf16[512,1024]{1,0:T(8,128)(2,1)S(1)}, bf16[512,1024]{1,0:T(8,128)(2,1)}, u32[]{:S(2)}) copy-start(bf16[512,1024]{1,0:T(8,128)(2,1)} %refs_3_.1) | copy-start | bytes 3145732
  44.7 13.7 %collective-permute-start.16 = (bf16[192,1024]{1,0:T(8,128)(2,1)S(1)}, bf16[192,1024]{1,0:T(8,128)(2,1)S(1)}, u32[]{:S(2)}, u32[]{:S(2)}) collective-permute-start(bf16[192,1024]{1,0:T(8,128)(2,1)S(1)} %get-tuple-element.98), channel_id=1, source_target_pairs={{0,30},{2,0},{4,2},{6,4},{8,6},{10,8},{12,10},{14,12},{16,14},{18,... | collective-permute-start | bytes 1179656 | tf_op jit(solution)/shard_map/ppermute | solution.py:278
  46.3 1.2 %collective-permute-start.12 = (f32[8,512]{1,0:T(8,128)S(1)}, f32[8,512]{1,0:T(8,128)S(1)}, u32[]{:S(2)}, u32[]{:S(2)}) collective-permute-start(f32[8,512]{1,0:T(8,128)S(1)} %get-tuple-element.77), channel_id=1, source_target_pairs={{0,1},{1,0},{2,3},{3,2},{4,5},{5,4},{6,7},{7,6},{8,9},{9,8},{10,11... | collective-permute-start | bytes 49160 | tf_op jit(solution)/shard_map/ppermute | solution.py:711
  49.7 6.8 %collective-permute-start.13 = (bf16[352,128]{1,0:T(8,128)(2,1)S(1)}, bf16[352,128]{1,0:T(8,128)(2,1)S(1)}, u32[]{:S(2)}, u32[]{:S(2)}) collective-permute-start(bf16[352,128]{1,0:T(8,128)(2,1)S(1)} %get-tuple-element.94), channel_id=1, source_target_pairs={{0,2},{2,0},{4,6},{6,4},{8,10},{10,8},{12,14},{14,12},{16,18},{18,... | collective-permute-start | bytes 270344 | tf_op jit(solution)/shard_map/ppermute | solution.py:273
  50.5 6.1 %collective-permute-start.14 = (bf16[352,128]{1,0:T(8,128)(2,1)S(1)}, bf16[352,128]{1,0:T(8,128)(2,1)S(1)}, u32[]{:S(2)}, u32[]{:S(2)}) collective-permute-start(bf16[352,128]{1,0:T(8,128)(2,1)S(1)} %get-tuple-element.95), channel_id=1, source_target_pairs={{0,4},{2,6},{4,0},{6,2},{8,12},{10,14},{12,8},{14,10},{16,20},{18,... | collective-permute-start | bytes 270344 | tf_op jit(solution)/shard_map/ppermute | solution.py:273
  50.8 7.6 %collective-permute-start.15 = (bf16[352,128]{1,0:T(8,128)(2,1)S(1)}, bf16[352,128]{1,0:T(8,128)(2,1)S(1)}, u32[]{:S(2)}, u32[]{:S(2)}) collective-permute-start(bf16[352,128]{1,0:T(8,128)(2,1)S(1)} %get-tuple-element.96), channel_id=1, source_target_pairs={{0,6},{2,4},{4,2},{6,0},{8,14},{10,12},{12,10},{14,8},{16,22},{18,... | collective-permute-start | bytes 270344 | tf_op jit(solution)/shard_map/ppermute | solution.py:273
  58.5 21.3 %collective-permute-start.17 = (bf16[336,1024]{1,0:T(8,128)(2,1)S(1)}, bf16[336,1024]{1,0:T(8,128)(2,1)S(1)}, u32[]{:S(2)}, u32[]{:S(2)}) collective-permute-start(bf16[336,1024]{1,0:T(8,128)(2,1)S(1)} %get-tuple-element.102), channel_id=1, source_target_pairs={{0,30},{2,0},{4,2},{6,4},{8,6},{10,8},{12,10},{14,12},{16,14},{18,... | collective-permute-start | bytes 2064392 | tf_op jit(solution)/shard_map/ppermute | solution.py:278
  64.9 6.4 %collective-permute-start.20 = (bf16[352,128]{1,0:T(8,128)(2,1)S(1)}, bf16[352,128]{1,0:T(8,128)(2,1)S(1)}, u32[]{:S(2)}, u32[]{:S(2)}) collective-permute-start(bf16[352,128]{1,0:T(8,128)(2,1)S(1)} %get-tuple-element.100.refs_18_), channel_id=1, source_target_pairs={{26,2},{28,4},{30,6},{27,3},{29,5},{31,7}} | collective-permute-start | bytes 270344 | tf_op jit(solution)/shard_map/ppermute | solution.py:283
  65.5 5.7 %collective-permute-start.19 = (bf16[352,128]{1,0:T(8,128)(2,1)S(1)}, bf16[352,128]{1,0:T(8,128)(2,1)S(1)}, u32[]{:S(2)}, u32[]{:S(2)}) collective-permute-start(bf16[352,128]{1,0:T(8,128)(2,1)S(1)} %get-tuple-element.100.refs_18_), channel_id=1, source_target_pairs={{18,2},{20,4},{22,6},{26,10},{28,12},{30,14},{19,3},{21,5},{23,7},... | collective-permute-start | bytes 270344 | tf_op jit(solution)/shard_map/ppermute | solution.py:283
  66.2 5.1 %collective-permute-start.18 = (bf16[352,128]{1,0:T(8,128)(2,1)S(1)}, bf16[352,128]{1,0:T(8,128)(2,1)S(1)}, u32[]{:S(2)}, u32[]{:S(2)}) collective-permute-start(bf16[352,128]{1,0:T(8,128)(2,1)S(1)} %get-tuple-element.100.refs_18_), channel_id=1, source_target_pairs={{10,2},{12,4},{14,6},{18,10},{20,12},{22,14},{26,18},{28,20},{30,2... | collective-permute-start | bytes 270344 | tf_op jit(solution)/shard_map/ppermute | solution.py:283
  71.6 10.2 %collective-permute-start.21 = (bf16[352,128]{1,0:T(8,128)(2,1)S(1)}, bf16[352,128]{1,0:T(8,128)(2,1)S(1)}, u32[]{:S(2)}, u32[]{:S(2)}) collective-permute-start(bf16[352,128]{1,0:T(8,128)(2,1)S(1)} %get-tuple-element.107), channel_id=1, source_target_pairs={{0,2},{2,0},{4,6},{6,4},{8,10},{10,8},{12,14},{14,12},{16,18},{18,... | collective-permute-start | bytes 270344 | tf_op jit(solution)/shard_map/ppermute | solution.py:273
  73.0 8.8 %collective-permute-start.22 = (bf16[352,128]{1,0:T(8,128)(2,1)S(1)}, bf16[352,128]{1,0:T(8,128)(2,1)S(1)}, u32[]{:S(2)}, u32[]{:S(2)}) collective-permute-start(bf16[352,128]{1,0:T(8,128)(2,1)S(1)} %get-tuple-element.108), channel_id=1, source_target_pairs={{0,4},{2,6},{4,0},{6,2},{8,12},{10,14},{12,8},{14,10},{16,20},{18,... | collective-permute-start | bytes 270344 | tf_op jit(solution)/shard_map/ppermute | solution.py:273
  75.0 6.8 %collective-permute-start.23 = (bf16[352,128]{1,0:T(8,128)(2,1)S(1)}, bf16[352,128]{1,0:T(8,128)(2,1)S(1)}, u32[]{:S(2)}, u32[]{:S(2)}) collective-permute-start(bf16[352,128]{1,0:T(8,128)(2,1)S(1)} %get-tuple-element.109), channel_id=1, source_target_pairs={{0,6},{2,4},{4,2},{6,0},{8,14},{10,12},{12,10},{14,8},{16,22},{18,... | collective-permute-start | bytes 270344 | tf_op jit(solution)/shard_map/ppermute | solution.py:273
  (2 other events, 2.1 us)

commit v6 on v5

--- a/solution.py
+++ b/solution.py
@@ -71,7 +71,8 @@
 
 
 def even_chunks(heads):
-    return [(0, heads // 2), (heads // 2, heads - heads // 2)] if heads > 1 else [(0, 1)]
+    first = max(1, heads * 5 // 8)
+    return [(0, first), (first, heads - first)] if heads > 1 else [(0, 1)]
 
 
 def picked(chunks, refs, head):
@@ -295,7 +296,7 @@
     full = whole(shape)
     size = shape[0] * shape[1]
     out = jax.ShapeDtypeStruct(shape, BF16)
-    own = [pieces[0]] + [swap(pieces[other], other) for other in range(1, GROUP)]
+    own = [pieces[0]] + [swap(pieces[other], other) for other in range(GROUP - 1, 0, -1)][::-1]
     along, after = first()
     (total,), held = call(
         total_body, (1,), [full] * GROUP, [full], [out], [], GROUP * size, 2 * 5 * size, own, None, along, after
@@ -318,7 +319,7 @@
         along,
         after,
     )
-    return [merged[0]] + [swap(merged[other], other) for other in range(1, GROUP)], merged, held
+    return [merged[0]] + [swap(merged[other], other) for other in range(GROUP - 1, 0, -1)][::-1], merged, held
 
 
 def attend(scores, masks, coef, linear):

time: 85.5 us -> 85.4 us (level)
  starting transfers between devices: 38.8 us -> 40 us
  waiting for transfers between devices: 14 us -> 12.8 us
    ppermute x12, waiting for transfers between devices: 8.12 us -> 7.03 us  [swap(): return lax.ppermute(value, 'ctx', [(at, at ^ mask) for at in range(count)])]
    ppermute x12, starting transfers between devices: 14.2 us -> 15.3 us  [swap(): return lax.ppermute(value, 'ctx', [(at, at ^ mask) for at in range(count)])]
where the time goes in v6:
time: 85.4 us; the launch traced here: 83.8 us
  starting transfers between devices  40 us (47%)
  Pallas kernels  26.4 us (31%)
  waiting for transfers between devices  12.8 us (15%)
  local copies, waits for them, and re-layouts  3.38 us (4%)
  between operations  1.16 us (1%)
    pallas_call x15, Pallas kernels, call(): pl.pallas_call(run, grid=grid, input_output_aliases={**(aliases or {}), *...  26.4 us
    ppermute x12, starting transfers between devices, swap(): return lax.ppermute(value, 'ctx', [(at, at ^ mask) for at in range(count)])  15.3 us
    ppermute x7, starting transfers between devices, shift(): lax.ppermute(value, 'ctx', [(at, at + steps) for at in range(count) if at...  13.3 us
    ppermute x4, starting transfers between devices, turn(): lax.ppermute(value, 'ctx', [(at, (at + steps) % count) for at in range(co...  11.4 us
    ppermute x12, waiting for transfers between devices, swap(): return lax.ppermute(value, 'ctx', [(at, at ^ mask) for at in range(count)])  7.03 us
    ppermute x4, waiting for transfers between devices, turn(): lax.ppermute(value, 'ctx', [(at, (at + steps) % count) for at in range(co...  4.61 us
    unnamed x20, local copies, waits for them, and re-layouts  2.18 us
  transfers between devices with their start and end apart: 24, of which 6 were waited for; matrix products, arithmetic and copies ran while one was open for 0% of the time, Pallas kernels for 28%

profile of v6, /device:TPU:0, one launch (start us, length us, event | category | flops | bytes accessed | tf_op | source)
XLA Modules:
  0.0 83.8 jit_solution(11732651688383184780)
XLA Ops:
  0.7 1.2 %slice.6 = bf16[256,768]{1,0:T(8,128)(2,1)S(1)} slice(bf16[512,1024]{1,0:T(8,128)(2,1)} %refs_0_.19), slice={[256:512], [0:768]} | slice | bytes 786432 | tf_op jit(solution)/shard_map/slice | solution.py:725
  1.8 3.0 %collective-permute-start.3 = (bf16[256,768]{1,0:T(8,128)(2,1)S(1)}, bf16[256,768]{1,0:T(8,128)(2,1)S(1)}, u32[]{:S(2)}, u32[]{:S(2)}) collective-permute-start(bf16[256,768]{1,0:T(8,128)(2,1)S(1)} %slice.6), channel_id=1, source_target_pairs={{0,2},{2,4},{4,6},{6,8},{8,10},{10,12},{12,14},{14,16},{16,18},{18... | collective-permute-start | bytes 1179656 | tf_op jit(solution)/shard_map/ppermute | solution.py:279
  4.8 2.8 %shard_map.84 = (bf16[352,128]{1,0:T(8,128)(2,1)}, bf16[352,128]{1,0:T(8,128)(2,1)}, bf16[352,128]{1,0:T(8,128)(2,1)}, bf16[352,128]{1,0:T(8,128)(2,1)}, bf16[25...) custom-call(bf16[512,1024]{1,0:T(8,128)(2,1)} %refs_0_.19, bf16[512,1024]{1,0:T(8,128)(2,1)} %refs_1_.17), custom_call_target="tpu_custom_call" | custom-call | flops 134217728 | bytes 2097152 | tf_op jit(solution)/shard_map/pallas_call | solution.py:96
  7.7 1.6 %collective-permute-start = (bf16[352,128]{1,0:T(8,128)(2,1)}, bf16[352,128]{1,0:T(8,128)(2,1)S(1)}, u32[]{:S(2)}, u32[]{:S(2)}) collective-permute-start(bf16[352,128]{1,0:T(8,128)(2,1)} %get-tuple-element.60), channel_id=1, source_target_pairs={{0,2},{2,0},{4,6},{6,4},{8,10},{10,8},{12,14},{14,12},{16,18},{18,... | collective-permute-start | bytes 270344 | tf_op jit(solution)/shard_map/ppermute | solution.py:274
  9.2 1.5 %collective-permute-start.1 = (bf16[352,128]{1,0:T(8,128)(2,1)}, bf16[352,128]{1,0:T(8,128)(2,1)S(1)}, u32[]{:S(2)}, u32[]{:S(2)}) collective-permute-start(bf16[352,128]{1,0:T(8,128)(2,1)} %get-tuple-element.61), channel_id=1, source_target_pairs={{0,4},{2,6},{4,0},{6,2},{8,12},{10,14},{12,8},{14,10},{16,20},{18,... | collective-permute-start | bytes 270344 | tf_op jit(solution)/shard_map/ppermute | solution.py:274
  11.2 1.2 %copy-done.2 = bf16[512,1024]{1,0:T(8,128)(2,1)S(1)} copy-done((bf16[512,1024]{1,0:T(8,128)(2,1)S(1)}, bf16[512,1024]{1,0:T(8,128)(2,1)}, u32[]{:S(2)}) %copy-start.2) | copy-done | bytes 1048600
  13.4 2.6 %shard_map.85 = (bf16[5,2,256,256]{3,2,1,0:T(8,128)(2,1)S(1)}, bf16[5,2,256,256]{3,2,1,0:T(8,128)(2,1)S(1)}, f32[256,640]{1,0:T(8,128)S(1)}) custom-call(bf16[512,1024]{1,0:T(8,128)(2,1)S(1)} %copy-done.2, bf16[512,1024]{1,0:T(8,128)(2,1)S(1)} %copy-done, bf16[512,1024]{1,0:T(8,128)(2,1)S(1)} %copy-done.1, bf16[352,128]{1,0:T(8,128)(2,1)S(1)} %copy-done.6), custom_call_target="tpu_custom_call" | custom-call | flops 1342177280 | bytes 3932160 | tf_op jit(solution)/shard_map/pallas_call | solution.py:96
  16.0 2.1 %collective-permute-done.refs_1_.refs_4_ = bf16[352,128]{1,0:T(8,128)(2,1)S(1)} collective-permute-done((bf16[352,128]{1,0:T(8,128)(2,1)}, bf16[352,128]{1,0:T(8,128)(2,1)S(1)}, u32[]{:S(2)}, u32[]{:S(2)}) %collective-permute-start) | collective-permute-done | bytes 90144 | tf_op jit(solution)/shard_map/ppermute | solution.py:274
  18.1 1.9 %collective-permute-done.1.refs_2_.refs_5_ = bf16[352,128]{1,0:T(8,128)(2,1)S(1)} collective-permute-done((bf16[352,128]{1,0:T(8,128)(2,1)}, bf16[352,128]{1,0:T(8,128)(2,1)S(1)}, u32[]{:S(2)}, u32[]{:S(2)}) %collective-permute-start.1) | collective-permute-done | bytes 90144 | tf_op jit(solution)/shard_map/ppermute | solution.py:274
  20.0 1.8 %collective-permute-done.2.refs_3_.refs_6_ = bf16[352,128]{1,0:T(8,128)(2,1)S(1)} collective-permute-done((bf16[352,128]{1,0:T(8,128)(2,1)}, bf16[352,128]{1,0:T(8,128)(2,1)S(1)}, u32[]{:S(2)}, u32[]{:S(2)}) %collective-permute-start.2) | collective-permute-done | bytes 90144 | tf_op jit(solution)/shard_map/ppermute | solution.py:274
  22.0 4.2 %collective-permute-start.6 = (bf16[352,128]{1,0:T(8,128)(2,1)S(1)}, bf16[352,128]{1,0:T(8,128)(2,1)S(1)}, u32[]{:S(2)}, u32[]{:S(2)}) collective-permute-start(bf16[352,128]{1,0:T(8,128)(2,1)S(1)} %get-tuple-element.66.refs_3_), channel_id=1, source_target_pairs={{0,24},{2,26},{4,28},{1,25},{3,27},{5,29}} | collective-permute-start | bytes 270344 | tf_op jit(solution)/shard_map/ppermute | solution.py:284
  26.2 1.3 %collective-permute-start.5 = (bf16[352,128]{1,0:T(8,128)(2,1)S(1)}, bf16[352,128]{1,0:T(8,128)(2,1)S(1)}, u32[]{:S(2)}, u32[]{:S(2)}) collective-permute-start(bf16[352,128]{1,0:T(8,128)(2,1)S(1)} %get-tuple-element.66.refs_3_), channel_id=1, source_target_pairs={{0,16},{2,18},{4,20},{8,24},{10,26},{12,28},{1,17},{3,19},{5,21},{... | collective-permute-start | bytes 270344 | tf_op jit(solution)/shard_map/ppermute | solution.py:284
  27.5 2.5 %collective-permute-start.4 = (bf16[352,128]{1,0:T(8,128)(2,1)S(1)}, bf16[352,128]{1,0:T(8,128)(2,1)S(1)}, u32[]{:S(2)}, u32[]{:S(2)}) collective-permute-start(bf16[352,128]{1,0:T(8,128)(2,1)S(1)} %get-tuple-element.66.refs_3_), channel_id=1, source_target_pairs={{0,8},{2,10},{4,12},{8,16},{10,18},{12,20},{16,24},{18,26},{20,28}... | collective-permute-start | bytes 270344 | tf_op jit(solution)/shard_map/ppermute | solution.py:284
  30.0 3.4 %collective-permute-start.11 = (bf16[512,256]{1,0:T(8,128)(2,1)S(1)}, bf16[512,256]{1,0:T(8,128)(2,1)S(1)}, u32[]{:S(2)}, u32[]{:S(2)}) collective-permute-start(bf16[512,256]{1,0:T(8,128)(2,1)S(1)} %get-tuple-element.74), channel_id=1, source_target_pairs={{0,2},{2,4},{4,6},{6,8},{8,10},{10,12},{12,14},{14,16},{16,18},{18... | collective-permute-start | bytes 786440 | tf_op jit(solution)/shard_map/ppermute | solution.py:284
  33.4 1.7 %shard_map.87 = (bf16[3,2,256,256]{3,2,1,0:T(8,128)(2,1)S(1)}, bf16[3,2,256,256]{3,2,1,0:T(8,128)(2,1)S(1)}, f32[256,384]{1,0:T(8,128)S(1)}) custom-call(bf16[512,1024]{1,0:T(8,128)(2,1)S(1)} %copy-done.3, bf16[512,1024]{1,0:T(8,128)(2,1)S(1)} %copy-done, bf16[512,1024]{1,0:T(8,128)(2,1)S(1)} %copy-done.1, bf16[352,128]{1,0:T(8,128)(2,1)S(1)} %get-tuple-element.66.refs_3_), custom_call_target="tpu_custom_call" | custom-call | flops 805306368 | bytes 2359296 | tf_op jit(solution)/shard_map/pallas_call | solution.py:96
  37.0 2.0 %collective-permute-start.9 = (bf16[352,128]{1,0:T(8,128)(2,1)S(1)}, bf16[352,128]{1,0:T(8,128)(2,1)S(1)}, u32[]{:S(2)}, u32[]{:S(2)}) collective-permute-start(bf16[352,128]{1,0:T(8,128)(2,1)S(1)} %get-tuple-element.71), channel_id=1, source_target_pairs={{0,6},{2,4},{4,2},{6,0},{8,14},{10,12},{12,10},{14,8},{16,22},{18,... | collective-permute-start | bytes 270344 | tf_op jit(solution)/shard_map/ppermute | solution.py:274
  39.0 2.9 %shard_map.89 = (bf16[6,2,256,256]{3,2,1,0:T(8,128)(2,1)S(1)}, bf16[6,256,256]{2,1,0:T(8,128)(2,1)S(1)}, f32[256,768]{1,0:T(8,128)S(1)}, f32[256,768]{1,0:T(8,128)S(1)}, f32[8,256]{1,0:T(8,128)S(1)}) custom-call(bf16[512,1024]{1,0:T(8,128)(2,1)S(1)} %copy-done.3, bf16[512,1024]{1,0:T(8,128)(2,1)S(1)} %copy-done, bf16[512,1024]{1,0:T(8,128)(2,1)S(1)} %copy-done.1, ...), custom_call_target="tpu_custom_call" | custom-call | flops 2013265920 | bytes 4718592 | tf_op jit(solution)/shard_map/pallas_call | solution.py:96
  41.9 1.2 %shard_map.90 = (bf16[2,2,256,256]{3,2,1,0:T(8,128)(2,1)S(1)}, bf16[2,256,256]{2,1,0:T(8,128)(2,1)S(1)}, f32[256,256]{1,0:T(8,128)S(1)}, f32[256,256]{1,0:T(8,128)S(1)}, f32[8,256]{1,0:T(8,128)S(1)}) custom-call(bf16[512,1024]{1,0:T(8,128)(2,1)S(1)} %copy-done.3, bf16[512,1024]{1,0:T(8,128)(2,1)S(1)} %copy-done, bf16[512,1024]{1,0:T(8,128)(2,1)S(1)} %copy-done.1, ...), custom_call_target="tpu_custom_call" | custom-call | flops 671088640 | bytes 1572864 | tf_op jit(solution)/shard_map/pallas_call | solution.py:96
  43.1 1.1 %shard_map.91 = (f32[512,1024]{1,0:T(8,128)S(1)}, f32[8,512]{1,0:T(8,128)S(1)}, bf16[192,1024]{1,0:T(8,128)(2,1)S(1)}) custom-call(bf16[512,1024]{1,0:T(8,128)(2,1)S(1)} %copy-done.3, bf16[1,1024]{1,0:T(2,128)(2,1)S(1)} %reshape.11.refs_1_.refs_2_, bf16[512,1024]{1,0:T(8,128)(2,1)S(1)} %copy-done.4, ...), custom_call_target="tpu_custom_call", output_to_operand_aliasing={{2}: (11, {})} | custom-call | flops 134217728 | bytes 6291456 | tf_op jit(solution)/shard_map/pallas_call | solution.py:96
  44.2 2.1 %collective-permute-start.16 = (bf16[192,1024]{1,0:T(8,128)(2,1)S(1)}, bf16[192,1024]{1,0:T(8,128)(2,1)S(1)}, u32[]{:S(2)}, u32[]{:S(2)}) collective-permute-start(bf16[192,1024]{1,0:T(8,128)(2,1)S(1)} %get-tuple-element.98), channel_id=1, source_target_pairs={{0,30},{2,0},{4,2},{6,4},{8,6},{10,8},{12,10},{14,12},{16,14},{18,... | collective-permute-start | bytes 1179656 | tf_op jit(solution)/shard_map/ppermute | solution.py:279
  46.3 1.2 %collective-permute-done.12 = f32[8,512]{1,0:T(8,128)S(1)} collective-permute-done((f32[8,512]{1,0:T(8,128)S(1)}, f32[8,512]{1,0:T(8,128)S(1)}, u32[]{:S(2)}, u32[]{:S(2)}) %collective-permute-start.12) | collective-permute-done | bytes 16416 | tf_op jit(solution)/shard_map/ppermute | solution.py:712
  47.5 2.3 %shard_map.92 = (bf16[512,1024]{1,0:T(8,128)(2,1)}, bf16[512,1024]{1,0:T(8,128)(2,1)S(1)}, bf16[336,1024]{1,0:T(8,128)(2,1)S(1)}, bf16[352,128]{1,0:T(8,128)(2,1...) custom-call(f32[8,512]{1,0:T(8,128)S(1)} %add.3.refs_0_, ...), custom_call_target="tpu_custom_call" | custom-call | flops 134217728 | bytes 7340032 | tf_op jit(solution)/shard_map/pallas_call | solution.py:96
  50.9 2.4 %collective-permute-start.15 = (bf16[352,128]{1,0:T(8,128)(2,1)S(1)}, bf16[352,128]{1,0:T(8,128)(2,1)S(1)}, u32[]{:S(2)}, u32[]{:S(2)}) collective-permute-start(bf16[352,128]{1,0:T(8,128)(2,1)S(1)} %get-tuple-element.96), channel_id=1, source_target_pairs={{0,6},{2,4},{4,2},{6,0},{8,14},{10,12},{12,10},{14,8},{16,22},{18,... | collective-permute-start | bytes 270344 | tf_op jit(solution)/shard_map/ppermute | solution.py:274
  53.3 4.0 %shard_map.93 = (bf16[512,640]{1,0:T(8,128)(2,1)S(1)}, f32[512,640]{1,0:T(8,128)S(1)}, f32[512,640]{1,0:T(8,128)S(1)}) custom-call(bf16[512,1024]{1,0:T(8,128)(2,1)S(1)} %copy-done.3, bf16[512,1024]{1,0:T(8,128)(2,1)S(1)} %copy-done, bf16[512,1024]{1,0:T(8,128)(2,1)S(1)} %copy-done.1, bf16[512,1024]{1,0:T(8,128)(2,1)S(1)} %get-tuple-element.83.refs_3_, ...), custom_call_target="tpu_custom_call" | custom-call | flops 2684354560 | bytes 13107200 | tf_op jit(solution)/shard_map/pallas_call | solution.py:96
  57.4 1.2 %collective-permute-done.15.refs_3_.refs_6_ = bf16[352,128]{1,0:T(8,128)(2,1)S(1)} collective-permute-done((bf16[352,128]{1,0:T(8,128)(2,1)S(1)}, bf16[352,128]{1,0:T(8,128)(2,1)S(1)}, u32[]{:S(2)}, u32[]{:S(2)}) %collective-permute-start.15) | collective-permute-done | bytes 90144 | tf_op jit(solution)/shard_map/ppermute | solution.py:274
  58.6 6.3 %collective-permute-start.17 = (bf16[336,1024]{1,0:T(8,128)(2,1)S(1)}, bf16[336,1024]{1,0:T(8,128)(2,1)S(1)}, u32[]{:S(2)}, u32[]{:S(2)}) collective-permute-start(bf16[336,1024]{1,0:T(8,128)(2,1)S(1)} %get-tuple-element.102), channel_id=1, source_target_pairs={{0,30},{2,0},{4,2},{6,4},{8,6},{10,8},{12,10},{14,12},{16,14},{18,... | collective-permute-start | bytes 2064392 | tf_op jit(solution)/shard_map/ppermute | solution.py:279
  66.9 3.3 %shard_map.95 = (bf16[512,1024]{1,0:T(8,128)(2,1)}, f32[512,384]{1,0:T(8,128)S(1)}, f32[512,384]{1,0:T(8,128)S(1)}) custom-call(bf16[512,1024]{1,0:T(8,128)(2,1)S(1)} %copy-done.3, bf16[512,1024]{1,0:T(8,128)(2,1)S(1)} %copy-done, bf16[512,1024]{1,0:T(8,128)(2,1)S(1)} %copy-done.1, bf16[512,1024]{1,0:T(8,128)(2,1)S(1)} %get-tuple-element.83.refs_3_, ...), custom_call_target="tpu_custom_call" | custom-call | flops 1610612736 | bytes 7864320 | tf_op jit(solution)/shard_map/pallas_call | solution.py:96
  70.5 2.6 %collective-permute-start.21 = (bf16[352,128]{1,0:T(8,128)(2,1)S(1)}, bf16[352,128]{1,0:T(8,128)(2,1)S(1)}, u32[]{:S(2)}, u32[]{:S(2)}) collective-permute-start(bf16[352,128]{1,0:T(8,128)(2,1)S(1)} %get-tuple-element.107), channel_id=1, source_target_pairs={{0,2},{2,0},{4,6},{6,4},{8,10},{10,8},{12,14},{14,12},{16,18},{18,... | collective-permute-start | bytes 270344 | tf_op jit(solution)/shard_map/ppermute | solution.py:274
  73.1 2.1 %collective-permute-start.22 = (bf16[352,128]{1,0:T(8,128)(2,1)S(1)}, bf16[352,128]{1,0:T(8,128)(2,1)S(1)}, u32[]{:S(2)}, u32[]{:S(2)}) collective-permute-start(bf16[352,128]{1,0:T(8,128)(2,1)S(1)} %get-tuple-element.108), channel_id=1, source_target_pairs={{0,4},{2,6},{4,0},{6,2},{8,12},{10,14},{12,8},{14,10},{16,20},{18,... | collective-permute-start | bytes 270344 | tf_op jit(solution)/shard_map/ppermute | solution.py:274
  75.2 4.6 %collective-permute-done.17.refs_3_ = bf16[336,1024]{1,0:T(8,128)(2,1)S(1)} collective-permute-done((bf16[336,1024]{1,0:T(8,128)(2,1)S(1)}, bf16[336,1024]{1,0:T(8,128)(2,1)S(1)}, u32[]{:S(2)}, u32[]{:S(2)}) %collective-permute-start.17) | collective-permute-done | bytes 688160 | tf_op jit(solution)/shard_map/ppermute | solution.py:279
  79.8 2.0 %shard_map.97 = (f32[256,1024]{1,0:T(8,128)S(1)}, f32[256,1024]{1,0:T(8,128)S(1)}) custom-call(bf16[512,1024]{1,0:T(8,128)(2,1)S(1)} %copy-done, bf16[512,1024]{1,0:T(8,128)(2,1)S(1)} %copy-done.1, bf16[192,1024]{1,0:T(8,128)(2,1)S(1)} %collective-permute-done.16.refs_5_.refs_2_, bf16[336,1024]{1,0:T(8,128)(2,1)S(1)} %collective-permute-done.17.refs_3_, ...), custom_call_target="tpu_custom_call" | custom-call | flops 536870912 | bytes 3145728 | tf_op jit(solution)/shard_map/pallas_call | solution.py:96
  81.8 1.9 %shard_map.98 = (bf16[512,1024]{1,0:T(8,128)(2,1)}, bf16[512,1024]{1,0:T(8,128)(2,1)}) custom-call(bf16[512,1024]{1,0:T(8,128)(2,1)S(1)} %copy-done, bf16[512,1024]{1,0:T(8,128)(2,1)S(1)} %copy-done.1, f32[256,1024]{1,0:T(8,128)S(1)} %get-tuple-element.105.refs_2_, f32[256,1024]{1,0:T(8,128)S(1)} %get-tuple-element.106.refs_3_, ...), custom_call_target="tpu_custom_call" | custom-call | flops 268435456 | bytes 9437184 | tf_op jit(solution)/shard_map/pallas_call | solution.py:96
  (55 shorter events, 6.9 us)
Async XLA Ops:
  0.6 10.6 %copy-start = (bf16[512,1024]{1,0:T(8,128)(2,1)S(1)}, bf16[512,1024]{1,0:T(8,128)(2,1)}, u32[]{:S(2)}) copy-start(bf16[512,1024]{1,0:T(8,128)(2,1)} %refs_0_.19) | copy-start | bytes 3145732
  0.6 10.6 %copy-start.1 = (bf16[512,1024]{1,0:T(8,128)(2,1)S(1)}, bf16[512,1024]{1,0:T(8,128)(2,1)}, u32[]{:S(2)}) copy-start(bf16[512,1024]{1,0:T(8,128)(2,1)} %refs_1_.17) | copy-start | bytes 3145732
  1.8 20.0 %collective-permute-start.3 = (bf16[256,768]{1,0:T(8,128)(2,1)S(1)}, bf16[256,768]{1,0:T(8,128)(2,1)S(1)}, u32[]{:S(2)}, u32[]{:S(2)}) collective-permute-start(bf16[256,768]{1,0:T(8,128)(2,1)S(1)} %slice.6), channel_id=1, source_target_pairs={{0,2},{2,4},{4,6},{6,8},{8,10},{10,12},{12,14},{14,16},{16,18},{18... | collective-permute-start | bytes 1179656 | tf_op jit(solution)/shard_map/ppermute | solution.py:279
  7.7 10.4 %collective-permute-start = (bf16[352,128]{1,0:T(8,128)(2,1)}, bf16[352,128]{1,0:T(8,128)(2,1)S(1)}, u32[]{:S(2)}, u32[]{:S(2)}) collective-permute-start(bf16[352,128]{1,0:T(8,128)(2,1)} %get-tuple-element.60), channel_id=1, source_target_pairs={{0,2},{2,0},{4,6},{6,4},{8,10},{10,8},{12,14},{14,12},{16,18},{18,... | collective-permute-start | bytes 270344 | tf_op jit(solution)/shard_map/ppermute | solution.py:274
  9.2 10.7 %collective-permute-start.1 = (bf16[352,128]{1,0:T(8,128)(2,1)}, bf16[352,128]{1,0:T(8,128)(2,1)S(1)}, u32[]{:S(2)}, u32[]{:S(2)}) collective-permute-start(bf16[352,128]{1,0:T(8,128)(2,1)} %get-tuple-element.61), channel_id=1, source_target_pairs={{0,4},{2,6},{4,0},{6,2},{8,12},{10,14},{12,8},{14,10},{16,20},{18,... | collective-permute-start | bytes 270344 | tf_op jit(solution)/shard_map/ppermute | solution.py:274
  10.8 11.1 %collective-permute-start.2 = (bf16[352,128]{1,0:T(8,128)(2,1)}, bf16[352,128]{1,0:T(8,128)(2,1)S(1)}, u32[]{:S(2)}, u32[]{:S(2)}) collective-permute-start(bf16[352,128]{1,0:T(8,128)(2,1)} %get-tuple-element.62), channel_id=1, source_target_pairs={{0,6},{2,4},{4,2},{6,0},{8,14},{10,12},{12,10},{14,8},{16,22},{18,... | collective-permute-start | bytes 270344 | tf_op jit(solution)/shard_map/ppermute | solution.py:274
  13.3 8.5 %copy-start.5 = (bf16[256,768]{1,0:T(8,128)(2,1)S(1)}, bf16[256,768]{1,0:T(8,128)(2,1)}, u32[]{:S(2)}) copy-start(bf16[256,768]{1,0:T(8,128)(2,1)} %get-tuple-element.63.refs_4_) | copy-start | bytes 1179652
  13.4 8.5 %copy-start.7 = (bf16[352,128]{1,0:T(8,128)(2,1)S(1)}, bf16[352,128]{1,0:T(8,128)(2,1)}, u32[]{:S(2)}) copy-start(bf16[352,128]{1,0:T(8,128)(2,1)} %get-tuple-element.59.refs_3_.refs_0_) | copy-start | bytes 270340
  13.4 8.5 %copy-start.8 = (bf16[512,256]{1,0:T(8,128)(2,1)S(1)}, bf16[512,256]{1,0:T(8,128)(2,1)}, u32[]{:S(2)}) copy-start(bf16[512,256]{1,0:T(8,128)(2,1)} %get-tuple-element.64.refs_5_) | copy-start | bytes 786436
  21.8 8.1 %copy-start.9 = (bf16[1024]{0:T(1024)(128)(2,1)S(1)}, bf16[1024]{0:T(1024)(128)(2,1)}, u32[]{:S(2)}) copy-start(bf16[1024]{0:T(1024)(128)(2,1)} %param.8) | copy-start | bytes 6148
  21.8 11.6 %copy-start.3 = (bf16[512,1024]{1,0:T(8,128)(2,1)S(1)}, bf16[512,1024]{1,0:T(8,128)(2,1)}, u32[]{:S(2)}) copy-start(bf16[512,1024]{1,0:T(8,128)(2,1)} %refs_0_.17) | copy-start | bytes 3145732
  21.9 17.1 %collective-permute-start.10 = (bf16[256,768]{1,0:T(8,128)(2,1)S(1)}, bf16[256,768]{1,0:T(8,128)(2,1)S(1)}, u32[]{:S(2)}, u32[]{:S(2)}) collective-permute-start(bf16[256,768]{1,0:T(8,128)(2,1)S(1)} %get-tuple-element.72), channel_id=1, source_target_pairs={{0,2},{2,4},{4,6},{6,8},{8,10},{10,12},{12,14},{14,16},{16,18},{18... | collective-permute-start | bytes 1179656 | tf_op jit(solution)/shard_map/ppermute | solution.py:279
  22.0 13.1 %collective-permute-start.6 = (bf16[352,128]{1,0:T(8,128)(2,1)S(1)}, bf16[352,128]{1,0:T(8,128)(2,1)S(1)}, u32[]{:S(2)}, u32[]{:S(2)}) collective-permute-start(bf16[352,128]{1,0:T(8,128)(2,1)S(1)} %get-tuple-element.66.refs_3_), channel_id=1, source_target_pairs={{0,24},{2,26},{4,28},{1,25},{3,27},{5,29}} | collective-permute-start | bytes 270344 | tf_op jit(solution)/shard_map/ppermute | solution.py:284
  26.2 9.0 %collective-permute-start.5 = (bf16[352,128]{1,0:T(8,128)(2,1)S(1)}, bf16[352,128]{1,0:T(8,128)(2,1)S(1)}, u32[]{:S(2)}, u32[]{:S(2)}) collective-permute-start(bf16[352,128]{1,0:T(8,128)(2,1)S(1)} %get-tuple-element.66.refs_3_), channel_id=1, source_target_pairs={{0,16},{2,18},{4,20},{8,24},{10,26},{12,28},{1,17},{3,19},{5,21},{... | collective-permute-start | bytes 270344 | tf_op jit(solution)/shard_map/ppermute | solution.py:284
  27.5 7.7 %collective-permute-start.4 = (bf16[352,128]{1,0:T(8,128)(2,1)S(1)}, bf16[352,128]{1,0:T(8,128)(2,1)S(1)}, u32[]{:S(2)}, u32[]{:S(2)}) collective-permute-start(bf16[352,128]{1,0:T(8,128)(2,1)S(1)} %get-tuple-element.66.refs_3_), channel_id=1, source_target_pairs={{0,8},{2,10},{4,12},{8,16},{10,18},{12,20},{16,24},{18,26},{20,28}... | collective-permute-start | bytes 270344 | tf_op jit(solution)/shard_map/ppermute | solution.py:284
  30.0 11.9 %collective-permute-start.11 = (bf16[512,256]{1,0:T(8,128)(2,1)S(1)}, bf16[512,256]{1,0:T(8,128)(2,1)S(1)}, u32[]{:S(2)}, u32[]{:S(2)}) collective-permute-start(bf16[512,256]{1,0:T(8,128)(2,1)S(1)} %get-tuple-element.74), channel_id=1, source_target_pairs={{0,2},{2,4},{4,6},{6,8},{8,10},{10,12},{12,14},{14,16},{16,18},{18... | collective-permute-start | bytes 786440 | tf_op jit(solution)/shard_map/ppermute | solution.py:284
  35.4 7.6 %collective-permute-start.7 = (bf16[352,128]{1,0:T(8,128)(2,1)S(1)}, bf16[352,128]{1,0:T(8,128)(2,1)S(1)}, u32[]{:S(2)}, u32[]{:S(2)}) collective-permute-start(bf16[352,128]{1,0:T(8,128)(2,1)S(1)} %get-tuple-element.69), channel_id=1, source_target_pairs={{0,2},{2,0},{4,6},{6,4},{8,10},{10,8},{12,14},{14,12},{16,18},{18,... | collective-permute-start | bytes 270344 | tf_op jit(solution)/shard_map/ppermute | solution.py:274
  36.0 7.1 %collective-permute-start.8 = (bf16[352,128]{1,0:T(8,128)(2,1)S(1)}, bf16[352,128]{1,0:T(8,128)(2,1)S(1)}, u32[]{:S(2)}, u32[]{:S(2)}) collective-permute-start(bf16[352,128]{1,0:T(8,128)(2,1)S(1)} %get-tuple-element.70), channel_id=1, source_target_pairs={{0,4},{2,6},{4,0},{6,2},{8,12},{10,14},{12,8},{14,10},{16,20},{18,... | collective-permute-start | bytes 270344 | tf_op jit(solution)/shard_map/ppermute | solution.py:274
  37.0 6.1 %collective-permute-start.9 = (bf16[352,128]{1,0:T(8,128)(2,1)S(1)}, bf16[352,128]{1,0:T(8,128)(2,1)S(1)}, u32[]{:S(2)}, u32[]{:S(2)}) collective-permute-start(bf16[352,128]{1,0:T(8,128)(2,1)S(1)} %get-tuple-element.71), channel_id=1, source_target_pairs={{0,6},{2,4},{4,2},{6,0},{8,14},{10,12},{12,10},{14,8},{16,22},{18,... | collective-permute-start | bytes 270344 | tf_op jit(solution)/shard_map/ppermute | solution.py:274
  41.9 1.2 %copy-start.4 = (bf16[512,1024]{1,0:T(8,128)(2,1)S(1)}, bf16[512,1024]{1,0:T(8,128)(2,1)}, u32[]{:S(2)}) copy-start(bf16[512,1024]{1,0:T(8,128)(2,1)} %refs_3_.1) | copy-start | bytes 3145732
  44.2 14.3 %collective-permute-start.16 = (bf16[192,1024]{1,0:T(8,128)(2,1)S(1)}, bf16[192,1024]{1,0:T(8,128)(2,1)S(1)}, u32[]{:S(2)}, u32[]{:S(2)}) collective-permute-start(bf16[192,1024]{1,0:T(8,128)(2,1)S(1)} %get-tuple-element.98), channel_id=1, source_target_pairs={{0,30},{2,0},{4,2},{6,4},{8,6},{10,8},{12,10},{14,12},{16,14},{18,... | collective-permute-start | bytes 1179656 | tf_op jit(solution)/shard_map/ppermute | solution.py:279
  46.3 1.2 %collective-permute-start.12 = (f32[8,512]{1,0:T(8,128)S(1)}, f32[8,512]{1,0:T(8,128)S(1)}, u32[]{:S(2)}, u32[]{:S(2)}) collective-permute-start(f32[8,512]{1,0:T(8,128)S(1)} %get-tuple-element.77), channel_id=1, source_target_pairs={{0,1},{1,0},{2,3},{3,2},{4,5},{5,4},{6,7},{7,6},{8,9},{9,8},{10,11... | collective-permute-start | bytes 49160 | tf_op jit(solution)/shard_map/ppermute | solution.py:712
  49.8 7.6 %collective-permute-start.13 = (bf16[352,128]{1,0:T(8,128)(2,1)S(1)}, bf16[352,128]{1,0:T(8,128)(2,1)S(1)}, u32[]{:S(2)}, u32[]{:S(2)}) collective-permute-start(bf16[352,128]{1,0:T(8,128)(2,1)S(1)} %get-tuple-element.94), channel_id=1, source_target_pairs={{0,2},{2,0},{4,6},{6,4},{8,10},{10,8},{12,14},{14,12},{16,18},{18,... | collective-permute-start | bytes 270344 | tf_op jit(solution)/shard_map/ppermute | solution.py:274
  50.0 7.3 %collective-permute-start.14 = (bf16[352,128]{1,0:T(8,128)(2,1)S(1)}, bf16[352,128]{1,0:T(8,128)(2,1)S(1)}, u32[]{:S(2)}, u32[]{:S(2)}) collective-permute-start(bf16[352,128]{1,0:T(8,128)(2,1)S(1)} %get-tuple-element.95), channel_id=1, source_target_pairs={{0,4},{2,6},{4,0},{6,2},{8,12},{10,14},{12,8},{14,10},{16,20},{18,... | collective-permute-start | bytes 270344 | tf_op jit(solution)/shard_map/ppermute | solution.py:274
  50.9 7.6 %collective-permute-start.15 = (bf16[352,128]{1,0:T(8,128)(2,1)S(1)}, bf16[352,128]{1,0:T(8,128)(2,1)S(1)}, u32[]{:S(2)}, u32[]{:S(2)}) collective-permute-start(bf16[352,128]{1,0:T(8,128)(2,1)S(1)} %get-tuple-element.96), channel_id=1, source_target_pairs={{0,6},{2,4},{4,2},{6,0},{8,14},{10,12},{12,10},{14,8},{16,22},{18,... | collective-permute-start | bytes 270344 | tf_op jit(solution)/shard_map/ppermute | solution.py:274
  58.6 21.2 %collective-permute-start.17 = (bf16[336,1024]{1,0:T(8,128)(2,1)S(1)}, bf16[336,1024]{1,0:T(8,128)(2,1)S(1)}, u32[]{:S(2)}, u32[]{:S(2)}) collective-permute-start(bf16[336,1024]{1,0:T(8,128)(2,1)S(1)} %get-tuple-element.102), channel_id=1, source_target_pairs={{0,30},{2,0},{4,2},{6,4},{8,6},{10,8},{12,10},{14,12},{16,14},{18,... | collective-permute-start | bytes 2064392 | tf_op jit(solution)/shard_map/ppermute | solution.py:279
  64.9 5.3 %collective-permute-start.20 = (bf16[352,128]{1,0:T(8,128)(2,1)S(1)}, bf16[352,128]{1,0:T(8,128)(2,1)S(1)}, u32[]{:S(2)}, u32[]{:S(2)}) collective-permute-start(bf16[352,128]{1,0:T(8,128)(2,1)S(1)} %get-tuple-element.100.refs_18_), channel_id=1, source_target_pairs={{26,2},{28,4},{30,6},{27,3},{29,5},{31,7}} | collective-permute-start | bytes 270344 | tf_op jit(solution)/shard_map/ppermute | solution.py:284
  65.5 4.7 %collective-permute-start.19 = (bf16[352,128]{1,0:T(8,128)(2,1)S(1)}, bf16[352,128]{1,0:T(8,128)(2,1)S(1)}, u32[]{:S(2)}, u32[]{:S(2)}) collective-permute-start(bf16[352,128]{1,0:T(8,128)(2,1)S(1)} %get-tuple-element.100.refs_18_), channel_id=1, source_target_pairs={{18,2},{20,4},{22,6},{26,10},{28,12},{30,14},{19,3},{21,5},{23,7},... | collective-permute-start | bytes 270344 | tf_op jit(solution)/shard_map/ppermute | solution.py:284
  66.2 4.0 %collective-permute-start.18 = (bf16[352,128]{1,0:T(8,128)(2,1)S(1)}, bf16[352,128]{1,0:T(8,128)(2,1)S(1)}, u32[]{:S(2)}, u32[]{:S(2)}) collective-permute-start(bf16[352,128]{1,0:T(8,128)(2,1)S(1)} %get-tuple-element.100.refs_18_), channel_id=1, source_target_pairs={{10,2},{12,4},{14,6},{18,10},{20,12},{22,14},{26,18},{28,20},{30,2... | collective-permute-start | bytes 270344 | tf_op jit(solution)/shard_map/ppermute | solution.py:284
  70.5 11.2 %collective-permute-start.21 = (bf16[352,128]{1,0:T(8,128)(2,1)S(1)}, bf16[352,128]{1,0:T(8,128)(2,1)S(1)}, u32[]{:S(2)}, u32[]{:S(2)}) collective-permute-start(bf16[352,128]{1,0:T(8,128)(2,1)S(1)} %get-tuple-element.107), channel_id=1, source_target_pairs={{0,2},{2,0},{4,6},{6,4},{8,10},{10,8},{12,14},{14,12},{16,18},{18,... | collective-permute-start | bytes 270344 | tf_op jit(solution)/shard_map/ppermute | solution.py:274
  73.1 8.7 %collective-permute-start.22 = (bf16[352,128]{1,0:T(8,128)(2,1)S(1)}, bf16[352,128]{1,0:T(8,128)(2,1)S(1)}, u32[]{:S(2)}, u32[]{:S(2)}) collective-permute-start(bf16[352,128]{1,0:T(8,128)(2,1)S(1)} %get-tuple-element.108), channel_id=1, source_target_pairs={{0,4},{2,6},{4,0},{6,2},{8,12},{10,14},{12,8},{14,10},{16,20},{18,... | collective-permute-start | bytes 270344 | tf_op jit(solution)/shard_map/ppermute | solution.py:274
  75.2 6.6 %collective-permute-start.23 = (bf16[352,128]{1,0:T(8,128)(2,1)S(1)}, bf16[352,128]{1,0:T(8,128)(2,1)S(1)}, u32[]{:S(2)}, u32[]{:S(2)}) collective-permute-start(bf16[352,128]{1,0:T(8,128)(2,1)S(1)} %get-tuple-element.109), channel_id=1, source_target_pairs={{0,6},{2,4},{4,2},{6,0},{8,14},{10,12},{12,10},{14,8},{16,22},{18,... | collective-permute-start | bytes 270344 | tf_op jit(solution)/shard_map/ppermute | solution.py:274
  (2 other events, 2.1 us)
